TPU v7x, 256 devices: a whole 4x4x8 slice. The times are simulated.
256 devices in a mesh: coarse: 16 (over z_hi, y), fine: 16 (over z_lo, x, core).
Axes of the slice: x: 4, y: 4, z: 8 (z_hi: 4, z_lo: 2; z = z_hi * 2 + z_lo), core: 2. Of those that a mesh axis runs over, the one named last changes fastest.
Arguments:
- right_side: float32 [128, 128, 128], P('coarse', 'fine'), may hold values from -6 to 6
- coefficient_index: int32 [128, 128, 128], P('coarse', 'fine'), may hold values from 0 to 15
- material_coefficients: float32 [16], replicated, may hold values from 0.02 to 0.5
- block_cells: int32 [16, 16, 64, 128], P('coarse', 'fine'), may hold values from 0 to 8191, as said below
- block_inverses: float32 [16, 16, 64, 128, 128], P('coarse', 'fine'), as said below
- aggregate_map: int32 [128, 128, 128], P('coarse', 'fine'), may hold values from 0 to 15, as said below
- coarse_diagonal: float32 [16, 16, 16], P('coarse', 'fine'), may hold values from 0.1 to 8
Outputs:
- solution: float32 [128, 128, 128], P('coarse', 'fine')
- residual: float32 [128, 128, 128], P('coarse', 'fine')
- direction: float32 [128, 128, 128], P('coarse', 'fine')
Inputs may be any that keep to these rules, and one draw needn't show every extreme that they name: `block_cells`: each device block's 64 x 128 entries list each of its local cell numbers exactly once. `block_inverses`: every 128 x 128 matrix is symmetric positive definite. A cell with third index j has aggregate_map equal to j // 8 - 1, j // 8 or j // 8 + 1.
All inputs are finite; a program needn't handle non-finite values.
Results may differ from a plain program's by a relative error of at most 0.00016.
Values sent between devices are 32-bit elements; how exact they have to be, the bound alone decides.
No kernel may reach another device: no remote copies, remote signals or barrier semaphores. Data moves between devices by JAX's collectives and lax.ppermute only.
A program may use at most 64 MiB of HBM per device.

v0:
```python
import jax
import jax.numpy as jnp
from jax import lax
from jax.sharding import Mesh
from jax.sharding import PartitionSpec as P

AGG = 8
ITERS = 2
SWEEPS = 4
COARSE_FINE = ("coarse_0", "coarse_1", "fine_0", "fine_1", "fine_2")
COARSE = ("coarse_0", "coarse_1")
FINE = ("fine_0", "fine_1", "fine_2")


omega = 0.8
restrict_scale = 0.25


def with_halo(cells, sides, width):
    for axis, dim in sides:
        count = lax.axis_size(axis)
        ends = count - 1
        head = lax.slice_in_dim(cells, 0, width, axis=dim)
        tail = lax.slice_in_dim(cells, cells.shape[dim] - width, cells.shape[dim], axis=dim)
        cells = jnp.concatenate(
            [
                lax.ppermute(tail, axis, [(i, (i + 1) % count) for i in range(ends)]),
                cells,
                lax.ppermute(head, axis, [((i + 1) % count, i) for i in range(ends)]),
            ],
            axis=dim,
        )
    return cells


def copy_for_each(x, axis):
    size = lax.axis_size(axis)
    return lax.all_to_all(jnp.broadcast_to(x[None], (size, *x.shape)), axis, 0, 0, tiled=True)


def laid_out(tiles, dim):
    tiles = jnp.moveaxis(tiles, 0, dim)
    shape = tiles.shape
    return tiles.reshape(*shape[:dim], shape[dim] * shape[dim + 1], *shape[dim + 2 :])


def gather_directly(x, axis, dim):
    tiles = copy_for_each(x, axis)
    return laid_out(tiles, dim)


def one_axis_at_a_time(x, axes):
    for axis in axes:
        x = lax.psum(x, axis)
    return x


def neighbours():
    result = []
    for shift_x in (-1, 0, 1):
        for shift_z in (-1, 0, 1):
            for shift_y in (-1, 0, 1):
                reach = abs(shift_x) + abs(shift_z) + abs(shift_y)
                if reach > 0:
                    result.append((shift_x, shift_z, shift_y, 0.5 ** (reach - 1)))
    return result


def window(padded, shift_x, shift_z, shift_y, shape):
    return padded[
        1 + shift_x : 1 + shift_x + shape[0],
        1 + shift_z : 1 + shift_z + shape[1],
        1 + shift_y : 1 + shift_y + shape[2],
    ]


def pad_last(array):
    return jnp.pad(array, ((0, 0), (0, 0), (1, 1)))


def seven_point(padded, diagonal, guess):
    beside = padded[2:, 1:-1, 1:-1] + padded[:-2, 1:-1, 1:-1]
    beside = beside + padded[1:-1, 2:, 1:-1] + padded[1:-1, :-2, 1:-1]
    beside = beside + padded[1:-1, 1:-1, 2:] + padded[1:-1, 1:-1, :-2]
    return (6.0 + diagonal) * guess - beside


def jacobi(source, diagonal, operate_coarse):
    scaled = 6.0 + diagonal
    guess = omega * source / scaled
    for sweep in range(SWEEPS - 1):
        guess = guess + omega * (source - operate_coarse(guess)) / scaled
    return guess


def displace(values, move):
    if move > 0:
        return jnp.pad(values[:-move], (move, 0))
    if move < 0:
        return jnp.pad(values[-move:], (0, -move))
    return values


def shards(
    right_side,
    coefficient_index,
    material_coefficients,
    block_cells,
    block_inverses,
    aggregate_map,
    coarse_diagonal,
):
    extent_x, extent_z, extent_y = right_side.shape
    shape = right_side.shape
    cells = extent_x * extent_z * extent_y
    boxes = extent_y // AGG
    table = jnp.arange(material_coefficients.shape[0], dtype=jnp.int32)
    kappa = jnp.sum(
        jnp.where(coefficient_index[..., None] == table, material_coefficients, 0.0), axis=-1
    )
    kappa_wide = pad_last(with_halo(kappa, ((COARSE, 0), (FINE, 1)), 1))
    couplings = []
    centre = jnp.zeros(shape, jnp.float32)
    for shift_x, shift_z, shift_y, weight in neighbours():
        coupling = weight * 0.5 * (kappa + window(kappa_wide, shift_x, shift_z, shift_y, shape))
        couplings.append(coupling)
        centre = centre + coupling

    def operate(field):
        wide = pad_last(with_halo(field, ((COARSE, 0), (FINE, 1)), 1))
        total = centre * field
        for (shift_x, shift_z, shift_y, weight), coupling in zip(neighbours(), couplings):
            total = total - coupling * window(wide, shift_x, shift_z, shift_y, shape)
        return total

    order = block_cells.reshape(cells)
    places = jnp.zeros((cells,), jnp.int32).at[order].set(jnp.arange(cells, dtype=jnp.int32))
    matrices = block_inverses.reshape(
        block_inverses.shape[2], block_inverses.shape[3], block_inverses.shape[4]
    )

    def block_apply(residual):
        picked = residual.reshape(cells)[order].reshape(matrices.shape[0], matrices.shape[1])
        product = jnp.einsum("bij,bj->bi", matrices, picked, precision=lax.Precision.HIGHEST)
        return product.reshape(cells)[places].reshape(shape)

    offset = aggregate_map - (jnp.arange(extent_y, dtype=jnp.int32) // AGG)[None, None, :]

    def restrict(residual):
        total = jnp.zeros((boxes,), jnp.float32)
        for move in (-1, 0, 1):
            masked = jnp.where(offset == move, residual, 0.0).reshape(
                extent_x, extent_z, boxes, AGG
            )
            total = total + displace(jnp.sum(masked, axis=(0, 1, 3)), move)
        return (restrict_scale * total).reshape(1, 1, boxes)

    def prolong(coarse):
        values = coarse.reshape(boxes)
        result = jnp.zeros(shape, jnp.float32)
        for move in (-1, 0, 1):
            repeated = jnp.repeat(displace(values, -move), AGG)
            result = jnp.where(offset == move, repeated[None, None, :], result)
        return result

    column_diagonal = gather_directly(coarse_diagonal, FINE, 1)

    def coarse_solve(source):
        group = gather_directly(source, FINE, 1)

        def operate_column(guess):
            edges = with_halo(guess, ((COARSE, 0),), 1)
            wide = jnp.pad(edges, ((0, 0), (1, 1), (1, 1)))
            return seven_point(wide, column_diagonal, guess)

        whole = jacobi(group, column_diagonal, operate_column)
        return lax.dynamic_slice_in_dim(whole, lax.axis_index(FINE), 1, 1)

    def precondition(residual):
        return block_apply(residual) + prolong(coarse_solve(restrict(residual)))

    def paired(residual, smoothed, image):
        if image is None:
            second = jnp.float32(0.0)
        else:
            second = jnp.sum(smoothed * image)
        return (
            one_axis_at_a_time(jnp.sum(residual * smoothed), COARSE_FINE),
            one_axis_at_a_time(second, COARSE_FINE),
        )

    solution = jnp.zeros(shape, jnp.float32)
    residual = right_side
    smoothed = precondition(residual)
    image = operate(smoothed)
    current, product = paired(residual, smoothed, image)
    alpha = current / product
    search = smoothed
    along = image
    for step in range(ITERS):
        solution = solution + alpha * search
        residual = residual - alpha * along
        smoothed = precondition(residual)
        if step + 1 < ITERS:
            image = operate(smoothed)
            following, product = paired(residual, smoothed, image)
            ratio = following / current
            alpha = following / (product - ratio * following / alpha)
            along = image + ratio * along
        else:
            following, unused = paired(residual, smoothed, None)
            ratio = following / current
        search = smoothed + ratio * search
        current = following
    return (solution, residual, search)


def solution(mesh):
    finer = Mesh(
        mesh.devices.reshape(4, 4, 2, 4, 2), ("coarse_0", "coarse_1", "fine_0", "fine_1", "fine_2")
    )
    in_specs = (
        P(COARSE, FINE, None),
        P(COARSE, FINE, None),
        P(),
        P(COARSE, FINE, None, None),
        P(COARSE, FINE, None, None, None),
        P(COARSE, FINE, None),
        P(COARSE, FINE, None),
    )
    out_specs = (P(COARSE, FINE, None), P(COARSE, FINE, None), P(COARSE, FINE, None))
    return jax.shard_map(
        shards, mesh=finer, in_specs=in_specs, out_specs=out_specs, check_vma=False
    )
```

profile of v0, /device:TPU:1, one launch (start us, length us, event | category | flops | bytes accessed | tf_op | source)
XLA Modules:
  0.0 656.5 jit_solution(12125266717823259401)
XLA Ops:
  1.9 7.2 %all-to-all-start.1 = ((f32[16,1,1,16]{3,2,1,0:T(1,128)}), f32[16,1,1,16]{3,2,1,0:T(1,128)S(1)}, u32[]{:S(2)}, u32[]{:S(2)}) async-start(f32[16,1,1,16]{3,2,1,0:T(1,128)} %broadcast_in_dim.152), calls=%async_computation.1 | async-start | bytes 16384 | tf_op jit(solution)/shard_map/all_to_all | solution.py:38
  10.1 3.2 collective-permute-start.6
  17.0 45.5 %gather_fusion = f32[8192]{0:T(1024)S(1)} fusion(f32[8192]{0:T(1024)S(1)} %bitcast.96, s32[8192]{0:T(1024)S(1)} %broadcast_clamp_fusion), kind=kCustom, calls=%fused_computation | custom fusion | bytes 98304 | tf_op jit(solution)/shard_map/gather | solution.py:143
  63.2 6.0 all-to-all-start
  69.2 8.3 %fusion.4 = f32[64,1,128]{2,1,0:T(1,128)S(1)} fusion(f32[64,128,1]{1,2,0:T(1,128)S(1)} %bitcast.128, f32[1,1,64,128,128]{4,3,2,1,0:T(8,128)} %param.11), kind=kOutput, calls=%fused_computation.11 | convolution fusion | flops 12582912 | bytes 4259840 | tf_op jit(solution)/shard_map/bij,bj->bi/dot_general | solution.py:144
  77.5 30.5 %scatter_custom_fusion = s32[8192]{0:T(1024)S(1)} fusion(s32[8192]{0:T(1024)S(1)} %bitcast.125, s32[8192]{0:T(1024)S(1)} %iota.12, s32[]{:T(128)} %constant.17.clone.1), kind=kCustom, calls=%fused_computation.253 | custom fusion | bytes 32772 | tf_op jit(solution)/shard_map/scatter | solution.py:137
  108.0 4.3 collective-permute-start.1
  113.6 3.1 collective-permute-done
  116.9 3.7 collective-permute-start.3
  121.9 45.5 %gather_fusion.1 = f32[8192]{0:T(1024)S(1)} fusion(f32[8192]{0:T(1024)S(1)} %bitcast.99, s32[8192]{0:T(1024)S(1)} %fusion.10), kind=kCustom, calls=%fused_computation.1 | custom fusion | bytes 98304 | tf_op jit(solution)/shard_map/gather | solution.py:145
  167.6 7.3 %collective-permute-start.5 = (f32[1,16,16]{2,1,0:T(8,128)S(1)}, f32[1,16,16]{2,1,0:T(8,128)S(1)}, u32[]{:S(2)}, u32[]{:S(2)}) collective-permute-start(f32[1,16,16]{2,1,0:T(8,128)S(1)} %fusion.121), channel_id=1, source_target_pairs={{0,16},{16,32},{32,48},{48,64},{64,80},{80,96},{96,112},{112,128},... | collective-permute-start | bytes 3080 | tf_op jit(solution)/shard_map/ppermute | solution.py:27
  176.2 6.1 collective-permute-done.4
  183.2 3.4 collective-permute-start.10
  187.9 6.9 %collective-permute-start.8 = (f32[10,1,128]{2,1,0:T(1,128)S(1)}, f32[10,1,128]{2,1,0:T(1,128)S(1)}, u32[]{:S(2)}, u32[]{:S(2)}) collective-permute-start(f32[10,1,128]{2,1,0:T(1,128)S(1)} %get-tuple-element.51), channel_id=1, source_target_pairs={{0,1},{1,2},{2,3},{3,4},{4,5},{5,6},{6,7},{7,8},{8,9},{9,10},{10,1... | collective-permute-start | bytes 15368 | tf_op jit(solution)/shard_map/ppermute | solution.py:27
  196.8 3.6 collective-permute-start.12
  202.6 2.8 collective-permute-done.13
  206.5 22.7 %all-reduce.29 = (f32[]{:T(128)}, f32[]{:T(128)}) all-reduce(f32[]{:T(128)} %get-tuple-element.12, f32[]{:T(128)} %get-tuple-element.11), channel_id=1, replica_groups=mesh['coarse_0'=4,'coarse_1'=4,'fine_0'=2,'fine_1'=4,'fine_2'=2] {'coars..., use_global_device_ids=true, to_apply=%region_8.9 | all-reduce | flops 2 | bytes 16 | tf_op jit(solution)/shard_map/psum | solution.py:54
  229.2 8.7 %all-reduce.27 = (f32[]{:T(128)}, f32[]{:T(128)}) all-reduce(f32[]{:T(128)} %get-tuple-element.26, f32[]{:T(128)} %get-tuple-element.27), channel_id=1, replica_groups=mesh['coarse_0'=4,'coarse_1'=4,'fine_0'=2,'fine_1'=4,'fine_2'=2] {'coars..., use_global_device_ids=true, to_apply=%region_9.10 | all-reduce | flops 2 | bytes 16 | tf_op jit(solution)/shard_map/psum | solution.py:54
  237.9 4.4 all-reduce.33
  242.3 13.1 %all-reduce.25 = (f32[]{:T(128)}, f32[]{:T(128)}) all-reduce(f32[]{:T(128)} %get-tuple-element.34, f32[]{:T(128)} %get-tuple-element.35), channel_id=1, replica_groups=mesh['coarse_0'=4,'coarse_1'=4,'fine_0'=2,'fine_1'=4,'fine_2'=2] {'fine_1'}, use_global_device_ids=true, to_apply=%region_11.12 | all-reduce | flops 2 | bytes 16 | tf_op jit(solution)/shard_map/psum | solution.py:54
  255.4 6.0 all-reduce.31
  263.5 10.1 %all_to_all.20 = f32[16,1,1,16]{3,2,1,0:T(1,128)S(1)} all-to-all(f32[16,1,1,16]{3,2,1,0:T(1,128)S(1)} %broadcast_in_dim.164), channel_id=1, replica_groups=mesh['coarse_0'=4,'coarse_1'=4,'fine_0'=2,'fine_1'=4,'fine_2'=2] {'fine_..., dimensions={0} | all-to-all | bytes 2048 | tf_op jit(solution)/shard_map/all_to_all | solution.py:38
  276.2 3.1 collective-permute-done.14
  279.5 2.8 collective-permute-start.17
  283.6 45.5 %gather_fusion.2 = f32[8192]{0:T(1024)S(1)} fusion(f32[8192]{0:T(1024)S(1)} %bitcast.97, s32[8192]{0:T(1024)S(1)} %broadcast_clamp_fusion), kind=kCustom, calls=%fused_computation.2 | custom fusion | bytes 98304 | tf_op jit(solution)/shard_map/gather | solution.py:143
  329.3 4.2 collective-permute-start.19
  335.0 8.3 %fusion.2 = f32[64,1,128]{2,1,0:T(1,128)S(1)} fusion(f32[64,128,1]{1,2,0:T(1,128)S(1)} %bitcast.127, f32[1,1,64,128,128]{4,3,2,1,0:T(8,128)} %param.11), kind=kOutput, calls=%fused_computation.9 | convolution fusion | flops 12582912 | bytes 4259840 | tf_op jit(solution)/shard_map/bij,bj->bi/dot_general | solution.py:144
  343.3 45.5 %gather_fusion.3 = f32[8192]{0:T(1024)S(1)} fusion(f32[8192]{0:T(1024)S(1)} %bitcast.101, s32[8192]{0:T(1024)S(1)} %fusion.10), kind=kCustom, calls=%fused_computation.3 | custom fusion | bytes 98304 | tf_op jit(solution)/shard_map/gather | solution.py:145
  389.7 7.0 %collective-permute-start.20 = (f32[1,8,128]{2,1,0:T(8,128)S(1)}, f32[1,8,128]{2,1,0:T(8,128)S(1)}, u32[]{:S(2)}, u32[]{:S(2)}) collective-permute-start(f32[1,8,128]{2,1,0:T(8,128)S(1)} %get-tuple-element.63), channel_id=1, source_target_pairs={{0,16},{16,32},{32,48},{48,64},{64,80},{80,96},{96,112},{112,128},... | collective-permute-start | bytes 12296 | tf_op jit(solution)/shard_map/ppermute | solution.py:27
  398.0 3.0 collective-permute-done.21
  401.1 6.2 collective-permute-start.22
  409.2 3.0 collective-permute-done.23
  413.4 20.8 %all-reduce.28 = (f32[]{:T(128)}, f32[]{:T(128)}) all-reduce(f32[]{:T(128)} %get-tuple-element.7, f32[]{:T(128)} %get-tuple-element.6), channel_id=1, replica_groups=mesh['coarse_0'=4,'coarse_1'=4,'fine_0'=2,'fine_1'=4,'fine_2'=2] {'coars..., use_global_device_ids=true, to_apply=%region_27.28 | all-reduce | flops 2 | bytes 16 | tf_op jit(solution)/shard_map/psum | solution.py:54
  434.2 13.1 %all-reduce.26 = (f32[]{:T(128)}, f32[]{:T(128)}) all-reduce(f32[]{:T(128)} %get-tuple-element.24, f32[]{:T(128)} %get-tuple-element.25), channel_id=1, replica_groups=mesh['coarse_0'=4,'coarse_1'=4,'fine_0'=2,'fine_1'=4,'fine_2'=2] {'coars..., use_global_device_ids=true, to_apply=%region_28.29 | all-reduce | flops 2 | bytes 16 | tf_op jit(solution)/shard_map/psum | solution.py:54
  447.3 4.5 all-reduce.32
  451.7 11.2 %all-reduce.24 = (f32[]{:T(128)}, f32[]{:T(128)}) all-reduce(f32[]{:T(128)} %get-tuple-element.32, f32[]{:T(128)} %get-tuple-element.33), channel_id=1, replica_groups=mesh['coarse_0'=4,'coarse_1'=4,'fine_0'=2,'fine_1'=4,'fine_2'=2] {'fine_1'}, use_global_device_ids=true, to_apply=%region_30.31 | all-reduce | flops 2 | bytes 16 | tf_op jit(solution)/shard_map/psum | solution.py:54
  462.9 6.3 all-reduce.30
  474.8 9.9 %all_to_all.21 = f32[16,1,1,16]{3,2,1,0:T(1,128)S(1)} all-to-all(f32[16,1,1,16]{3,2,1,0:T(1,128)S(1)} %broadcast_in_dim.174), channel_id=1, replica_groups=mesh['coarse_0'=4,'coarse_1'=4,'fine_0'=2,'fine_1'=4,'fine_2'=2] {'fine_..., dimensions={0} | all-to-all | bytes 2048 | tf_op jit(solution)/shard_map/all_to_all | solution.py:38
  487.3 3.1 collective-permute-done.24
  494.6 45.5 %gather_fusion.4 = f32[8192]{0:T(1024)S(1)} fusion(f32[8192]{0:T(1024)S(1)} %bitcast.98, s32[8192]{0:T(1024)S(1)} %broadcast_clamp_fusion), kind=kCustom, calls=%fused_computation.4 | custom fusion | bytes 98304 | tf_op jit(solution)/shard_map/gather | solution.py:143
  540.3 4.0 collective-permute-start.29
  545.6 8.3 %fusion = f32[64,1,128]{2,1,0:T(1,128)S(1)} fusion(f32[64,128,1]{1,2,0:T(1,128)S(1)} %bitcast.126, f32[1,1,64,128,128]{4,3,2,1,0:T(8,128)} %param.11), kind=kOutput, calls=%fused_computation.7 | convolution fusion | flops 12582912 | bytes 4259840 | tf_op jit(solution)/shard_map/bij,bj->bi/dot_general | solution.py:144
  553.9 45.5 %gather_fusion.5 = f32[8192]{0:T(1024)S(1)} fusion(f32[8192]{0:T(1024)S(1)} %bitcast.100, s32[8192]{0:T(1024)S(1)} %fusion.10), kind=kCustom, calls=%fused_computation.5 | custom fusion | bytes 98304 | tf_op jit(solution)/shard_map/gather | solution.py:145
  601.0 22.0 %psum.195 = f32[]{:T(128)} all-reduce(f32[]{:T(128)} %multiply_reduce_fusion), channel_id=1, replica_groups=mesh['coarse_0'=4,'coarse_1'=4,'fine_0'=2,'fine_1'=4,'fine_2'=2] {'coars..., use_global_device_ids=true, to_apply=%region_45.46 | all-reduce | flops 1 | bytes 8 | tf_op jit(solution)/shard_map/psum | solution.py:54
  623.0 6.9 %psum.196 = f32[]{:T(128)} all-reduce(f32[]{:T(128)} %psum.195), channel_id=1, replica_groups=mesh['coarse_0'=4,'coarse_1'=4,'fine_0'=2,'fine_1'=4,'fine_2'=2] {'coars..., use_global_device_ids=true, to_apply=%region_46.47 | all-reduce | flops 1 | bytes 8 | tf_op jit(solution)/shard_map/psum | solution.py:54
  629.9 4.4 psum.197
  634.3 7.6 %psum.198 = f32[]{:T(128)} all-reduce(f32[]{:T(128)} %psum.197), channel_id=1, replica_groups=mesh['coarse_0'=4,'coarse_1'=4,'fine_0'=2,'fine_1'=4,'fine_2'=2] {'fine_1'}, use_global_device_ids=true, to_apply=%region_48.49 | all-reduce | flops 1 | bytes 8 | tf_op jit(solution)/shard_map/psum | solution.py:54
  641.8 12.6 %psum.199 = f32[]{:T(128)} all-reduce(f32[]{:T(128)} %psum.198), channel_id=1, replica_groups=mesh['coarse_0'=4,'coarse_1'=4,'fine_0'=2,'fine_1'=4,'fine_2'=2] {'fine_2'}, use_global_device_ids=true, to_apply=%region_49.50 | all-reduce | flops 1 | bytes 8 | tf_op jit(solution)/shard_map/psum | solution.py:54
  (154 shorter events, 41.1 us)
Async XLA Ops:
  0.6 16.4 %copy-start = (f32[8,8,128]{2,1,0:T(8,128)S(1)}, f32[8,8,128]{2,1,0:T(8,128)}, u32[]{:S(2)}) copy-start(f32[8,8,128]{2,1,0:T(8,128)} %param.7) | copy-start | bytes 98308
  1.9 60.7 %all-to-all-start.1 = ((f32[16,1,1,16]{3,2,1,0:T(1,128)}), f32[16,1,1,16]{3,2,1,0:T(1,128)S(1)}, u32[]{:S(2)}, u32[]{:S(2)}) async-start(f32[16,1,1,16]{3,2,1,0:T(1,128)} %broadcast_in_dim.152), calls=%async_computation.1 | async-start | bytes 16384 | tf_op jit(solution)/shard_map/all_to_all | solution.py:38
  10.1 177.7 %collective-permute-start.6 = (f32[1,8,128]{2,1,0:T(8,128)S(1)}, f32[1,8,128]{2,1,0:T(8,128)S(1)}, u32[]{:S(2)}, u32[]{:S(2)}) collective-permute-start(f32[1,8,128]{2,1,0:T(8,128)S(1)} %get-tuple-element.65), channel_id=1, source_target_pairs={{0,16},{16,32},{32,48},{48,64},{64,80},{80,96},{96,112},{112,128},... | collective-permute-start | bytes 12296 | tf_op jit(solution)/shard_map/ppermute | solution.py:27
  13.3 174.5 %collective-permute-start.7 = (f32[1,8,128]{2,1,0:T(8,128)S(1)}, f32[1,8,128]{2,1,0:T(8,128)S(1)}, u32[]{:S(2)}, u32[]{:S(2)}) collective-permute-start(f32[1,8,128]{2,1,0:T(8,128)S(1)} %get-tuple-element.66), channel_id=1, source_target_pairs={{16,0},{32,16},{48,32},{64,48},{80,64},{96,80},{112,96},{128,112},... | collective-permute-start | bytes 12296 | tf_op jit(solution)/shard_map/ppermute | solution.py:29
  63.2 44.8 %all-to-all-start = ((f32[16,1,1,16]{3,2,1,0:T(1,128)}), f32[16,1,1,16]{3,2,1,0:T(1,128)S(1)}, u32[]{:S(2)}, u32[]{:S(2)}) async-start(f32[16,1,1,16]{3,2,1,0:T(1,128)} %broadcast_in_dim.150), calls=%async_computation | async-start | bytes 16384 | tf_op jit(solution)/shard_map/all_to_all | solution.py:38
  108.0 5.6 collective-permute-start.1
  112.3 4.4 collective-permute-start
  116.9 50.5 %collective-permute-start.3 = (f32[1,16,16]{2,1,0:T(8,128)S(1)}, f32[1,16,16]{2,1,0:T(8,128)S(1)}, u32[]{:S(2)}, u32[]{:S(2)}) collective-permute-start(f32[1,16,16]{2,1,0:T(8,128)S(1)} %fusion.126), channel_id=1, source_target_pairs={{0,16},{16,32},{32,48},{48,64},{64,80},{80,96},{96,112},{112,128},... | collective-permute-start | bytes 3080 | tf_op jit(solution)/shard_map/ppermute | solution.py:27
  120.6 46.9 %collective-permute-start.2 = (f32[1,16,16]{2,1,0:T(8,128)S(1)}, f32[1,16,16]{2,1,0:T(8,128)S(1)}, u32[]{:S(2)}, u32[]{:S(2)}) collective-permute-start(f32[1,16,16]{2,1,0:T(8,128)S(1)} %fusion.126), channel_id=1, source_target_pairs={{16,0},{32,16},{48,32},{64,48},{80,64},{96,80},{112,96},{128,112},... | collective-permute-start | bytes 3080 | tf_op jit(solution)/shard_map/ppermute | solution.py:29
  167.6 8.6 %collective-permute-start.5 = (f32[1,16,16]{2,1,0:T(8,128)S(1)}, f32[1,16,16]{2,1,0:T(8,128)S(1)}, u32[]{:S(2)}, u32[]{:S(2)}) collective-permute-start(f32[1,16,16]{2,1,0:T(8,128)S(1)} %fusion.121), channel_id=1, source_target_pairs={{0,16},{16,32},{32,48},{48,64},{64,80},{80,96},{96,112},{112,128},... | collective-permute-start | bytes 3080 | tf_op jit(solution)/shard_map/ppermute | solution.py:27
  174.9 7.4 %collective-permute-start.4 = (f32[1,16,16]{2,1,0:T(8,128)S(1)}, f32[1,16,16]{2,1,0:T(8,128)S(1)}, u32[]{:S(2)}, u32[]{:S(2)}) collective-permute-start(f32[1,16,16]{2,1,0:T(8,128)S(1)} %fusion.121), channel_id=1, source_target_pairs={{16,0},{32,16},{48,32},{64,48},{80,64},{96,80},{112,96},{128,112},... | collective-permute-start | bytes 3080 | tf_op jit(solution)/shard_map/ppermute | solution.py:29
  183.2 13.6 %collective-permute-start.10 = (f32[1,8,128]{2,1,0:T(8,128)S(1)}, f32[1,8,128]{2,1,0:T(8,128)S(1)}, u32[]{:S(2)}, u32[]{:S(2)}) collective-permute-start(f32[1,8,128]{2,1,0:T(8,128)S(1)} %get-tuple-element.67), channel_id=1, source_target_pairs={{0,16},{16,32},{32,48},{48,64},{64,80},{80,96},{96,112},{112,128},... | collective-permute-start | bytes 12296 | tf_op jit(solution)/shard_map/ppermute | solution.py:27
  186.5 10.2 %collective-permute-start.11 = (f32[1,8,128]{2,1,0:T(8,128)S(1)}, f32[1,8,128]{2,1,0:T(8,128)S(1)}, u32[]{:S(2)}, u32[]{:S(2)}) collective-permute-start(f32[1,8,128]{2,1,0:T(8,128)S(1)} %get-tuple-element.68), channel_id=1, source_target_pairs={{16,0},{32,16},{48,32},{64,48},{80,64},{96,80},{112,96},{128,112},... | collective-permute-start | bytes 12296 | tf_op jit(solution)/shard_map/ppermute | solution.py:29
  187.9 14.5 %collective-permute-start.8 = (f32[10,1,128]{2,1,0:T(1,128)S(1)}, f32[10,1,128]{2,1,0:T(1,128)S(1)}, u32[]{:S(2)}, u32[]{:S(2)}) collective-permute-start(f32[10,1,128]{2,1,0:T(1,128)S(1)} %get-tuple-element.51), channel_id=1, source_target_pairs={{0,1},{1,2},{2,3},{3,4},{4,5},{5,6},{6,7},{7,8},{8,9},{9,10},{10,1... | collective-permute-start | bytes 15368 | tf_op jit(solution)/shard_map/ppermute | solution.py:27
  194.8 7.6 %collective-permute-start.9 = (f32[10,1,128]{2,1,0:T(1,128)S(1)}, f32[10,1,128]{2,1,0:T(1,128)S(1)}, u32[]{:S(2)}, u32[]{:S(2)}) collective-permute-start(f32[10,1,128]{2,1,0:T(1,128)S(1)} %get-tuple-element.52), channel_id=1, source_target_pairs={{1,0},{2,1},{3,2},{4,3},{5,4},{6,5},{7,6},{8,7},{9,8},{10,9},{11,1... | collective-permute-start | bytes 15368 | tf_op jit(solution)/shard_map/ppermute | solution.py:29
  196.8 5.8 collective-permute-start.12
  200.4 4.9 collective-permute-start.13
  273.6 2.6 collective-permute-start.15
  274.9 4.4 collective-permute-start.14
  279.5 49.6 %collective-permute-start.17 = (f32[1,16,16]{2,1,0:T(8,128)S(1)}, f32[1,16,16]{2,1,0:T(8,128)S(1)}, u32[]{:S(2)}, u32[]{:S(2)}) collective-permute-start(f32[1,16,16]{2,1,0:T(8,128)S(1)} %fusion.116), channel_id=1, source_target_pairs={{0,16},{16,32},{32,48},{48,64},{64,80},{80,96},{96,112},{112,128},... | collective-permute-start | bytes 3080 | tf_op jit(solution)/shard_map/ppermute | solution.py:27
  282.3 46.9 %collective-permute-start.16 = (f32[1,16,16]{2,1,0:T(8,128)S(1)}, f32[1,16,16]{2,1,0:T(8,128)S(1)}, u32[]{:S(2)}, u32[]{:S(2)}) collective-permute-start(f32[1,16,16]{2,1,0:T(8,128)S(1)} %fusion.116), channel_id=1, source_target_pairs={{16,0},{32,16},{48,32},{64,48},{80,64},{96,80},{112,96},{128,112},... | collective-permute-start | bytes 3080 | tf_op jit(solution)/shard_map/ppermute | solution.py:29
  329.3 59.5 %collective-permute-start.19 = (f32[1,16,16]{2,1,0:T(8,128)S(1)}, f32[1,16,16]{2,1,0:T(8,128)S(1)}, u32[]{:S(2)}, u32[]{:S(2)}) collective-permute-start(f32[1,16,16]{2,1,0:T(8,128)S(1)} %fusion.111), channel_id=1, source_target_pairs={{0,16},{16,32},{32,48},{48,64},{64,80},{80,96},{96,112},{112,128},... | collective-permute-start | bytes 3080 | tf_op jit(solution)/shard_map/ppermute | solution.py:27
  333.5 55.4 %collective-permute-start.18 = (f32[1,16,16]{2,1,0:T(8,128)S(1)}, f32[1,16,16]{2,1,0:T(8,128)S(1)}, u32[]{:S(2)}, u32[]{:S(2)}) collective-permute-start(f32[1,16,16]{2,1,0:T(8,128)S(1)} %fusion.111), channel_id=1, source_target_pairs={{16,0},{32,16},{48,32},{64,48},{80,64},{96,80},{112,96},{128,112},... | collective-permute-start | bytes 3080 | tf_op jit(solution)/shard_map/ppermute | solution.py:29
  389.7 8.3 %collective-permute-start.20 = (f32[1,8,128]{2,1,0:T(8,128)S(1)}, f32[1,8,128]{2,1,0:T(8,128)S(1)}, u32[]{:S(2)}, u32[]{:S(2)}) collective-permute-start(f32[1,8,128]{2,1,0:T(8,128)S(1)} %get-tuple-element.63), channel_id=1, source_target_pairs={{0,16},{16,32},{32,48},{48,64},{64,80},{80,96},{96,112},{112,128},... | collective-permute-start | bytes 12296 | tf_op jit(solution)/shard_map/ppermute | solution.py:27
  396.7 4.4 collective-permute-start.21
  401.1 8.1 %collective-permute-start.22 = (f32[10,1,128]{2,1,0:T(1,128)S(1)}, f32[10,1,128]{2,1,0:T(1,128)S(1)}, u32[]{:S(2)}, u32[]{:S(2)}) collective-permute-start(f32[10,1,128]{2,1,0:T(1,128)S(1)} %get-tuple-element.47), channel_id=1, source_target_pairs={{0,1},{1,2},{2,3},{3,4},{4,5},{5,6},{6,7},{7,8},{8,9},{9,10},{10,1... | collective-permute-start | bytes 15368 | tf_op jit(solution)/shard_map/ppermute | solution.py:27
  407.3 4.9 collective-permute-start.23
  474.0 126.3 %copy-start.1 = (f32[8,8,128]{2,1,0:T(8,128)}, f32[8,8,128]{2,1,0:T(8,128)S(1)}, u32[]{:S(2)}) copy-start(f32[8,8,128]{2,1,0:T(8,128)S(1)} %get-tuple-element.36) | copy-start | bytes 98308
  484.7 2.6 collective-permute-start.25
  486.0 4.4 collective-permute-start.24
  490.5 49.6 %collective-permute-start.27 = (f32[1,16,16]{2,1,0:T(8,128)S(1)}, f32[1,16,16]{2,1,0:T(8,128)S(1)}, u32[]{:S(2)}, u32[]{:S(2)}) collective-permute-start(f32[1,16,16]{2,1,0:T(8,128)S(1)} %fusion.106), channel_id=1, source_target_pairs={{0,16},{16,32},{32,48},{48,64},{64,80},{80,96},{96,112},{112,128},... | collective-permute-start | bytes 3080 | tf_op jit(solution)/shard_map/ppermute | solution.py:27
  493.3 46.9 %collective-permute-start.26 = (f32[1,16,16]{2,1,0:T(8,128)S(1)}, f32[1,16,16]{2,1,0:T(8,128)S(1)}, u32[]{:S(2)}, u32[]{:S(2)}) collective-permute-start(f32[1,16,16]{2,1,0:T(8,128)S(1)} %fusion.106), channel_id=1, source_target_pairs={{16,0},{32,16},{48,32},{64,48},{80,64},{96,80},{112,96},{128,112},... | collective-permute-start | bytes 3080 | tf_op jit(solution)/shard_map/ppermute | solution.py:29
  540.3 59.1 %collective-permute-start.29 = (f32[1,16,16]{2,1,0:T(8,128)S(1)}, f32[1,16,16]{2,1,0:T(8,128)S(1)}, u32[]{:S(2)}, u32[]{:S(2)}) collective-permute-start(f32[1,16,16]{2,1,0:T(8,128)S(1)} %fusion.101), channel_id=1, source_target_pairs={{0,16},{16,32},{32,48},{48,64},{64,80},{80,96},{96,112},{112,128},... | collective-permute-start | bytes 3080 | tf_op jit(solution)/shard_map/ppermute | solution.py:27
  544.3 55.2 %collective-permute-start.28 = (f32[1,16,16]{2,1,0:T(8,128)S(1)}, f32[1,16,16]{2,1,0:T(8,128)S(1)}, u32[]{:S(2)}, u32[]{:S(2)}) collective-permute-start(f32[1,16,16]{2,1,0:T(8,128)S(1)} %fusion.101), channel_id=1, source_target_pairs={{16,0},{32,16},{48,32},{64,48},{80,64},{96,80},{112,96},{128,112},... | collective-permute-start | bytes 3080 | tf_op jit(solution)/shard_map/ppermute | solution.py:29
where the time goes:
time: 658 us; the launch traced here: 656 us
  local copies, waits for them, and re-layouts  308 us (47%)
  blocking collectives  184 us (28%)
  starting transfers between devices  96.4 us (15%)
  matrix products  24.9 us (4%)
  waiting for transfers between devices  24.2 us (4%)
  other arithmetic  9.45 us (1%)
  between operations  8.92 us (1%)
    psum x15, blocking collectives, one_axis_at_a_time(): x = lax.psum(x, axis)  164 us
    gather x3, local copies, waits for them, and re-layouts, block_apply(): return product.reshape(cells)[places].reshape(shape)  137 us
    gather x3, local copies, waits for them, and re-layouts, block_apply(): residual.reshape(cells)[order].reshape(matrices.shape[0], matrices.shape[1])  137 us
    ppermute x15, starting transfers between devices, with_halo(): lax.ppermute(tail, axis, [(i, (i + 1) % count) for i in range(ends)])  61.8 us
    scatter x1, local copies, waits for them, and re-layouts, shards(): jnp.zeros((cells,), jnp.int32).at[order]  30.5 us
    dot_general x3, matrix products, block_apply(): jnp.einsum('bij,bj->bi', matrices, picked, precision=lax.Precision.HIGHEST)  24.9 us
    ppermute x15, waiting for transfers between devices, with_halo(): lax.ppermute(head, axis, [((i + 1) % count, i) for i in range(ends)])  24.2 us
    ppermute x15, starting transfers between devices, with_halo(): lax.ppermute(head, axis, [((i + 1) % count, i) for i in range(ends)])  21.4 us
  transfers between devices with their start and end apart: 32, of which 7 were waited for; matrix products, arithmetic and copies ran while one was open for 51% of the time, Pallas kernels for 0%

commit v1 on v0

v1 whole, which is shorter than its diff:
```python
import functools

import jax
import jax.numpy as jnp
from jax import lax
from jax.experimental import pallas as pl
from jax.experimental.pallas import tpu as pltpu
from jax.sharding import PartitionSpec as P

AGG = 8
COARSE, FINE = "coarse", "fine"
SWEEPS = 4
OMEGA = 0.8
SIDE = 16
ROWS = 64
LANES = 128
WIDE = SIDE * SIDE
F32 = jnp.float32

SLAB = 16
RIGHT, LEFT = 8, 15


def vmem():
    return pl.BlockSpec(memory_space=pltpu.VMEM)


def smem():
    return pl.BlockSpec(memory_space=pltpu.SMEM)


def anywhere():
    return pl.BlockSpec(memory_space=pl.ANY)


def params():
    return pltpu.CompilerParams(vmem_limit_bytes=24 * 1024 * 1024)


def shape(*dims, dtype=F32):
    return jax.ShapeDtypeStruct(dims, dtype)


def iota(dims, axis):
    return lax.broadcasted_iota(jnp.int32, dims, axis)


def take_lanes(values, lanes):
    numbers = lax.GatherDimensionNumbers(
        offset_dims=(),
        collapsed_slice_dims=(1,),
        start_index_map=(1,),
        operand_batching_dims=(0,),
        start_indices_batching_dims=(0,),
    )
    return lax.gather(
        values,
        lanes[..., None],
        numbers,
        slice_sizes=(1, 1),
        mode=lax.GatherScatterMode.PROMISE_IN_BOUNDS,
    )


def permute(source_ref, index_ref, target_ref):
    rows = [index_ref[8 * g : 8 * g + 8, :] // LANES for g in range(8)]
    lanes = [index_ref[8 * g : 8 * g + 8, :] % LANES for g in range(8)]

    def body(step, picked):
        for part in range(8):
            row = step * 8 + part
            source = jnp.broadcast_to(source_ref[pl.ds(row, 1), :], (8, LANES))
            picked = tuple(
                jnp.where(rows[g] == row, take_lanes(source, lanes[g]), picked[g])
                for g in range(8)
            )
        return picked

    zero = jnp.zeros((8, LANES), F32)
    picked = lax.fori_loop(0, ROWS // 8, body, (zero,) * 8)
    for g in range(8):
        target_ref[8 * g : 8 * g + 8, :] = picked[g]


def multiply_blocks(matrices_ref, picked_ref, product_ref):
    def body(group, carry):
        start = pl.multiple_of(group * 8, 8)
        columns = jnp.transpose(picked_ref[pl.ds(start, 8), :])
        rows = []
        for part in range(8):
            matrix = matrices_ref[group * 8 + part].reshape(16, 8, LANES)
            column = columns[:, part : part + 1].reshape(16, 8, 1)
            total = jnp.sum(matrix * column, axis=0)
            rows.append(jnp.sum(total, axis=0, keepdims=True))
        product_ref[pl.ds(start, 8), :] = jnp.concatenate(rows, axis=0)
        return carry

    lax.fori_loop(0, ROWS // 8, body, 0)


def invert(order_ref):
    cell_rows = iota((ROWS, LANES), 0)
    cell_lanes = iota((LANES, LANES), 0)
    slots = iota((ROWS, LANES), 1).astype(F32)

    def body(block, total):
        entry = order_ref[pl.ds(block, 1), :]
        hit = cell_rows == entry // LANES
        numbers = jnp.concatenate(
            [jnp.where(hit, block.astype(F32), 0.0), jnp.where(hit, slots, 0.0)], axis=0
        ).astype(jnp.bfloat16)
        lanes = jnp.where(cell_lanes == entry % LANES, 1.0, 0.0).astype(jnp.bfloat16)
        return total + lax.dot_general(
            numbers, lanes, (((1,), (1,)), ((), ())), preferred_element_type=F32
        )

    total = lax.fori_loop(0, ROWS, body, jnp.zeros((LANES, LANES), F32))
    return (total[:ROWS] * float(LANES) + total[ROWS:]).astype(jnp.int32)


def restrict(field, offset, member):
    total = jnp.sum(jnp.where(offset == 0, field, 0.0), axis=0, keepdims=True)
    up = jnp.sum(jnp.where(offset == 1, field, 0.0), axis=0, keepdims=True)
    down = jnp.sum(jnp.where(offset == -1, field, 0.0), axis=0, keepdims=True)
    total, up, down = (jnp.broadcast_to(x, (8, LANES)) for x in (total, up, down))
    total = total + pltpu.roll(up, AGG, 1) + pltpu.roll(down, LANES - AGG, 1)
    for distance in (1, 2, 4):
        total = total + pltpu.roll(total, LANES - distance, 1)
    lane = iota((8, LANES), 1)
    total = 0.25 * take_lanes(total, (lane % SIDE) * AGG)
    return jnp.where(lane // SIDE == member % 8, total, 0.0)


def half_rows(values, member):
    return jnp.where(iota((8, LANES), 0) == member // 8, values, 0.0)


def moved(values, distance, axis, keep):
    size = values.shape[axis]
    return jnp.where(keep, pltpu.roll(values, distance % size, axis), 0.0)


def coarse_solve(source, diagonal):
    owner, lane = iota((SIDE, WIDE), 0), iota((SIDE, WIDE), 1)
    cell = lane % SIDE
    weight = OMEGA / (6.0 + diagonal)
    guess = weight * source
    for sweep in range(SWEEPS - 1):
        beside = moved(guess, 1, 0, owner > 0) + moved(guess, -1, 0, owner < SIDE - 1)
        beside = beside + moved(guess, SIDE, 1, lane >= SIDE)
        beside = beside + moved(guess, -SIDE, 1, lane < WIDE - SIDE)
        beside = beside + moved(guess, 1, 1, cell > 0) + moved(guess, -1, 1, cell < SIDE - 1)
        guess = (1.0 - OMEGA) * guess + weight * (source + beside)
    return guess


def nearby(coarse, member, rows_ref):
    rows_ref[...] = pltpu.roll(coarse, lax.rem((SIDE + 1 - member) * SIDE, WIDE), 1)[:, :LANES]


def smooth(slabs):
    total = slabs[1:9] + 0.5 * (slabs[0:8] + slabs[2:10])
    planes = []
    lane = iota((8, LANES), 1)
    row = iota((8, LANES), 0)
    for plane in range(8):
        own, ends = total[plane, :8], total[plane, 8:]
        before = jnp.where(row == 0, ends[LEFT - 8 :, :], pltpu.roll(own, 1, 0))
        after = jnp.where(row == 7, ends[:1, :], pltpu.roll(own, 7, 0))
        own = own + 0.5 * (before + after)
        below = jnp.where(lane > 0, pltpu.roll(own, 1, 1), 0.0)
        above = jnp.where(lane < LANES - 1, pltpu.roll(own, LANES - 1, 1), 0.0)
        planes.append(own + 0.5 * (below + above))
    return jnp.stack(planes)


def position():
    return lax.axis_index(COARSE), lax.axis_index(FINE)


def put_faces(field_ref, pieces_ref, row, member):
    pieces_ref[jnp.maximum(member - 1, 0), row : row + 8, :] = field_ref[
        pl.ds(0, 8, stride=8), :
    ]
    pieces_ref[jnp.minimum(member + 1, SIDE - 1), row : row + 8, :] = field_ref[
        pl.ds(7, 8, stride=8), :
    ]


def get_faces(pieces_ref, row, member, outside):
    left = pieces_ref[jnp.maximum(member - 1, 0), row : row + 8, :]
    right = pieces_ref[jnp.minimum(member + 1, SIDE - 1), row : row + 8, :]
    left = jnp.where(member > 0, left, outside)
    right = jnp.where(member < SIDE - 1, right, outside)
    return left, right


def fill_slabs(slabs_ref, field_ref, faces_ref, ends_ref, face_row, end_row, halo_row, outside):
    owner, member = position()
    left, right = get_faces(faces_ref, face_row, member, outside)
    gap = jnp.full((8, LANES), outside, F32)
    for plane in range(8):
        slabs_ref[plane + 1, :8, :] = field_ref[8 * plane : 8 * plane + 8, :]
        slabs_ref[plane + 1, 8:, :] = gap
        slabs_ref[plane + 1, RIGHT : RIGHT + 1, :] = right[plane : plane + 1, :]
        slabs_ref[plane + 1, LEFT : LEFT + 1, :] = left[plane : plane + 1, :]
    for plane, there, inside in (
        (0, jnp.maximum(owner - 1, 0), owner > 0),
        (9, jnp.minimum(owner + 1, SIDE - 1), owner < SIDE - 1),
    ):
        slabs_ref[plane, 8:, :] = gap
        slabs_ref[plane, :8, :] = jnp.where(
            inside, ends_ref[there, end_row : end_row + 8, :], outside
        )
        halo = jnp.where(inside, ends_ref[there, halo_row : halo_row + 2, :], outside)
        slabs_ref[plane, LEFT : LEFT + 1, :] = halo[0:1, :]
        slabs_ref[plane, RIGHT : RIGHT + 1, :] = halo[1:2, :]


def add_prolonged(slabs_ref, numbers_ref, rows_ref):
    owner, member = position()
    for plane in range(10):
        if plane == 0:
            there = jnp.maximum(owner - 1, 0)
        elif plane == 9:
            there = jnp.minimum(owner + 1, SIDE - 1)
        else:
            there = owner
        row = jnp.broadcast_to(rows_ref[pl.ds(there, 1), :], (8, LANES))
        for part in (0, 8):
            number = numbers_ref[plane, part : part + 8, :]
            value = take_lanes(row, jnp.maximum(number, 0))
            slabs_ref[plane, part : part + 8, :] += jnp.where(number >= 0, value, 0.0)


def operate(field, kappa):
    own, own_kappa = field[1:9, :8], kappa[1:9, :8]
    return own_kappa * (8.0 * own - smooth(field)) + own * smooth(kappa) - smooth(
        kappa * field
    )


def offsets(aggregate):
    return aggregate - iota((ROWS, LANES), 1) // AGG


F_FIELD, F_KAPPA, F_MAP, F_SOURCE, F_DIAGONAL, F_FIRST = 0, 8, 16, 24, 26, 32
C_FIELD, C_KAPPA, C_MAP, C_HALOS, C_SOURCE, C_DIAGONAL, C_FIRST = 0, 8, 16, 24, 30, 32, 40
C_HALO_2, C_SOURCE_2, C_SECOND = 8, 10, 16


def begin(
    table_ref, side_ref, index_ref, order_ref, matrices_hbm, map_ref, diagonal_ref,
    pieces_ref, kappa_ref, places_ref, smoothed_ref, numbers_ref,
    matrices_ref, picked_ref, product_ref, arrived,
):
    owner, member = position()
    copy = pltpu.make_async_copy(matrices_hbm, matrices_ref, arrived)
    copy.start()
    index = index_ref[...]
    kappa = jnp.zeros((ROWS, LANES), F32)
    for entry in range(table_ref.shape[0]):
        kappa = jnp.where(index == entry, table_ref[entry], kappa)
    kappa_ref[...] = kappa
    places_ref[...] = invert(order_ref)
    permute(side_ref, order_ref, picked_ref)
    copy.wait()
    multiply_blocks(matrices_ref, picked_ref, product_ref)
    permute(product_ref, places_ref, smoothed_ref)
    aggregate = map_ref[...]
    numbers_ref[...] = aggregate.astype(F32)
    source = half_rows(restrict(side_ref[...], offsets(aggregate), member), member)
    lane = iota((8, LANES), 1)
    spread = jnp.concatenate([diagonal_ref[...]] * 8, axis=1)
    spread = jnp.where(lane // SIDE == member % 8, jnp.broadcast_to(spread, (8, LANES)), 0.0)
    source = source + pltpu.roll(half_rows(spread, member), 2, 0)
    for piece in range(SIDE):
        pieces_ref[piece, F_SOURCE : F_SOURCE + 8, :] = source
    put_faces(smoothed_ref, pieces_ref, F_FIELD, member)
    put_faces(kappa_ref, pieces_ref, F_KAPPA, member)
    put_faces(numbers_ref, pieces_ref, F_MAP, member)


def put_planes(field_ref, pieces_ref, row, owner):
    pieces_ref[jnp.maximum(owner - 1, 0), row : row + 8, :] = field_ref[0:8, :]
    pieces_ref[jnp.minimum(owner + 1, SIDE - 1), row : row + 8, :] = field_ref[56:64, :]


def relay_first(faces_ref, smoothed_ref, kappa_ref, numbers_ref, pieces_ref):
    owner, member = position()
    sources = jnp.sum(faces_ref[:, F_SOURCE : F_SOURCE + 8, :], axis=0)
    before, after = jnp.maximum(owner - 1, 0), jnp.minimum(owner + 1, SIDE - 1)
    for piece in range(SIDE):
        pieces_ref[piece, C_SOURCE : C_SOURCE + 4, :] = sources[0:4, :]
    put_planes(smoothed_ref, pieces_ref, C_FIELD, owner)
    put_planes(kappa_ref, pieces_ref, C_KAPPA, owner)
    put_planes(numbers_ref, pieces_ref, C_MAP, owner)
    for number, (row, outside) in enumerate(((F_FIELD, 0.0), (F_KAPPA, 0.0), (F_MAP, -1.0))):
        left, right = get_faces(faces_ref, row, member, outside)
        start = C_HALOS + 2 * number
        pieces_ref[before, start : start + 1, :] = left[0:1, :]
        pieces_ref[before, start + 1 : start + 2, :] = right[0:1, :]
        pieces_ref[after, start : start + 1, :] = left[7:8, :]
        pieces_ref[after, start + 1 : start + 2, :] = right[7:8, :]


def halves(pieces_ref, row):
    return jnp.concatenate([pieces_ref[:, row, :], pieces_ref[:, row + 1, :]], axis=1)


def first_image(
    faces_ref, ends_ref, own_ref, own_kappa_ref, numbers_ref, map_ref, order_ref, places_ref,
    matrices_hbm,
    pieces_ref, field_ref, image_ref, smoothed_ref, kappa_ref, lanes_ref, diagonal_ref,
    matrices_ref, picked_ref, product_ref, slabs_ref, rows_ref, arrived,
):
    owner, member = position()
    copy = pltpu.make_async_copy(matrices_hbm, matrices_ref, arrived)
    copy.start()
    diagonal = halves(ends_ref, C_DIAGONAL)
    diagonal_ref[...] = diagonal
    nearby(coarse_solve(halves(ends_ref, C_SOURCE), diagonal), member, rows_ref)
    fill_slabs(
        slabs_ref, numbers_ref, faces_ref, ends_ref, F_MAP, C_MAP, C_HALOS + 4, -1.0
    )
    row = iota((10, SLAB, LANES), 1)
    shift = jnp.where(row < 8, SIDE, jnp.where(row == RIGHT, 2 * SIDE, 0))
    number = slabs_ref[...]
    lanes_ref[...] = jnp.where(number >= 0.0, number.astype(jnp.int32) + shift, -1)
    fill_slabs(
        kappa_ref, own_kappa_ref, faces_ref, ends_ref, F_KAPPA, C_KAPPA, C_HALOS + 2, 0.0
    )
    fill_slabs(slabs_ref, own_ref, faces_ref, ends_ref, F_FIELD, C_FIELD, C_HALOS, 0.0)
    add_prolonged(slabs_ref, lanes_ref, rows_ref)
    field = slabs_ref[...]
    field_ref[...] = field[1:9, :8].reshape(ROWS, LANES)
    image_ref[...] = operate(field, kappa_ref[...]).reshape(ROWS, LANES)
    permute(image_ref, order_ref, picked_ref)
    copy.wait()
    multiply_blocks(matrices_ref, picked_ref, product_ref)
    permute(product_ref, places_ref, smoothed_ref)
    source = half_rows(restrict(image_ref[...], offsets(map_ref[...]), member), member)
    for piece in range(SIDE):
        pieces_ref[piece, 8:16, :] = source
    put_faces(smoothed_ref, pieces_ref, 0, member)


def relay_second(faces_ref, smoothed_ref, pieces_ref):
    owner, member = position()
    sources = jnp.sum(faces_ref[:, 8:16, :], axis=0)
    before, after = jnp.maximum(owner - 1, 0), jnp.minimum(owner + 1, SIDE - 1)
    for piece in range(SIDE):
        pieces_ref[piece, C_SOURCE_2 : C_SOURCE_2 + 2, :] = sources[0:2, :]
    put_planes(smoothed_ref, pieces_ref, 0, owner)
    left, right = get_faces(faces_ref, 0, member, 0.0)
    pieces_ref[before, C_HALO_2 : C_HALO_2 + 1, :] = left[0:1, :]
    pieces_ref[before, C_HALO_2 + 1 : C_HALO_2 + 2, :] = right[0:1, :]
    pieces_ref[after, C_HALO_2 : C_HALO_2 + 1, :] = left[7:8, :]
    pieces_ref[after, C_HALO_2 + 1 : C_HALO_2 + 2, :] = right[7:8, :]


def second_image(
    faces_ref, ends_ref, own_ref, kappa_ref, lanes_ref, map_ref, order_ref, places_ref,
    diagonal_ref, side_ref, first_ref, image_ref, matrices_hbm,
    pieces_ref, field_ref, second_ref, smoothed_ref,
    matrices_ref, picked_ref, product_ref, slabs_ref, rows_ref, arrived,
):
    owner, member = position()
    copy = pltpu.make_async_copy(matrices_hbm, matrices_ref, arrived)
    copy.start()
    nearby(coarse_solve(halves(ends_ref, C_SOURCE_2), diagonal_ref[...]), member, rows_ref)
    fill_slabs(slabs_ref, own_ref, faces_ref, ends_ref, 0, 0, C_HALO_2, 0.0)
    add_prolonged(slabs_ref, lanes_ref, rows_ref)
    slabs = slabs_ref[...]
    field = slabs[1:9, :8].reshape(ROWS, LANES)
    field_ref[...] = field
    second = operate(slabs, kappa_ref[...]).reshape(ROWS, LANES)
    second_ref[...] = second
    permute(second_ref, order_ref, picked_ref)
    copy.wait()
    multiply_blocks(matrices_ref, picked_ref, product_ref)
    permute(product_ref, places_ref, smoothed_ref)
    first = first_ref[...]
    image = image_ref[...]
    pairs = (
        side_ref[...] * first,
        first * image,
        image * field,
        second * first,
        second * field,
        second * smoothed_ref[...],
    )
    lane = iota((8, LANES), 1)
    message = restrict(second, offsets(map_ref[...]), member)
    beside = lax.rem(member + 1, 8) * SIDE
    for number, pair in enumerate(pairs):
        total = jnp.sum(jnp.sum(pair, axis=0, keepdims=True), axis=1, keepdims=True)
        message = jnp.where(lane == beside + number, total, message)
    for start in range(0, WIDE, 8):
        pieces_ref[start : start + 8, :] = message


def finish(
    pieces_ref, diagonal_ref, map_ref, side_ref, first_ref, image_ref, field_ref, second_ref,
    smoothed_ref,
    solution_ref, residual_ref, search_ref,
):
    owner, member = position()
    pieces = pieces_ref[...].reshape(SIDE, SIDE, LANES)
    place = iota((SIDE, LANES), 0) % 8
    group = iota((SIDE, LANES), 1) // SIDE
    pieces_sum = jnp.sum(pieces, axis=0)
    sums = jnp.where(group == (place + 1) % 8, pieces_sum, 0.0)
    kept = jnp.where((group == place)[None], pieces, 0.0)
    source = jnp.concatenate(
        [jnp.sum(kept[:, :8], axis=1), jnp.sum(kept[:, 8:], axis=1)], axis=1
    )
    coarse = coarse_solve(source, diagonal_ref[...])
    lane = iota((1, LANES), 1)
    sums = jnp.sum(sums, axis=0, keepdims=True)

    def total(number):
        picked = jnp.where(lane % SIDE == number, sums, 0.0)
        return jnp.sum(picked, axis=1, keepdims=True)

    def whole(array):
        return jnp.sum(jnp.sum(array, axis=0, keepdims=True), axis=1, keepdims=True)

    r_z, z_az, w_y, v_z, v_y, v_bv = (total(number) for number in range(6))
    v_u = v_bv + 4.0 * whole(source * coarse)
    alpha = r_z / z_az
    following = r_z - 2.0 * alpha * z_az + alpha * alpha * w_y
    grown = 1.0 + following / r_z
    product = grown * grown * z_az - grown * alpha * (v_z + w_y) + alpha * alpha * v_y
    again = following / product
    one = alpha + again * grown
    two = again * alpha
    last = (
        r_z - 2.0 * one * z_az + 2.0 * two * v_z + one * one * w_y
        - 2.0 * one * two * v_y + two * two * v_u
    )
    ratio = last / following
    lanes = iota((SIDE, WIDE), 1)
    rows = iota((SIDE, WIDE), 0)
    near = pltpu.roll(coarse, lax.rem((SIDE - member) * SIDE, WIDE), 1)[:, :LANES]
    row = jnp.sum(
        jnp.where(iota((SIDE, LANES), 0) == owner, near, 0.0), axis=0, keepdims=True
    )
    row = jnp.broadcast_to(row, (8, LANES))
    for g in range(8):
        at = slice(8 * g, 8 * g + 8)
        first, image, field, second = (
            ref[at, :] for ref in (first_ref, image_ref, field_ref, second_ref)
        )
        smoothed = smoothed_ref[at, :] + take_lanes(row, map_ref[at, :])
        solution_ref[at, :] = one * first - two * field
        residual_ref[at, :] = side_ref[at, :] - one * image + two * second
        search_ref[at, :] = (
            first - one * field + two * smoothed + ratio * (grown * first - alpha * field)
        )


def shards(
    right_side, coefficient_index, material_coefficients, block_cells, block_inverses,
    aggregate_map, coarse_diagonal,
):
    dims = right_side.shape
    side = right_side.reshape(ROWS, LANES)
    index = coefficient_index.reshape(ROWS, LANES)
    order = block_cells.reshape(ROWS, LANES)
    matrices = block_inverses.reshape(ROWS, LANES, LANES)
    aggregate = aggregate_map.reshape(ROWS, LANES)
    diagonal = coarse_diagonal.reshape(1, SIDE)
    local = shape(ROWS, LANES)
    block_scratch = [
        pltpu.VMEM((ROWS, LANES, LANES), F32),
        pltpu.VMEM((ROWS, LANES), F32),
        pltpu.VMEM((ROWS, LANES), F32),
    ]
    slab_scratch = [pltpu.VMEM((10, SLAB, LANES), F32), pltpu.VMEM((SIDE, LANES), F32)]
    arrived = [pltpu.SemaphoreType.DMA]

    def call(kernel, outs, ins, scratch=(), specs=None):
        return pl.pallas_call(
            kernel,
            out_shape=outs,
            in_specs=specs or [vmem()] * ins,
            out_specs=[vmem()] * len(outs),
            scratch_shapes=list(scratch),
            compiler_params=params(),
        )

    def exchange(pieces, axis):
        return lax.all_to_all(pieces, axis, 0, 0, tiled=True)

    pieces, kappa, places, smoothed, numbers = call(
        begin,
        [shape(SIDE, F_FIRST, LANES), local, shape(ROWS, LANES, dtype=jnp.int32), local, local],
        7,
        block_scratch + arrived,
        [smem()] + [vmem()] * 3 + [anywhere()] + [vmem()] * 2,
    )(material_coefficients, side, index, order, matrices, aggregate, diagonal)
    faces = exchange(pieces, FINE)
    (pieces,) = call(relay_first, [shape(SIDE, C_FIRST, LANES)], 4)(
        faces, smoothed, kappa, numbers
    )
    ends = exchange(pieces, COARSE)
    pieces, first, image, smoothed, kappa, lanes, diagonals = call(
        first_image,
        [
            shape(SIDE, SLAB, LANES), local, local, local, shape(10, SLAB, LANES),
            shape(10, SLAB, LANES, dtype=jnp.int32), shape(SIDE, WIDE),
        ],
        9,
        block_scratch + slab_scratch + arrived,
        [vmem()] * 8 + [anywhere()],
    )(faces, ends, smoothed, kappa, numbers, aggregate, order, places, matrices)
    faces = exchange(pieces, FINE)
    (pieces,) = call(relay_second, [shape(SIDE, C_SECOND, LANES)], 2)(faces, smoothed)
    ends = exchange(pieces, COARSE)
    pieces, field, second, smoothed = call(
        second_image,
        [shape(WIDE, LANES), local, local, local],
        13,
        block_scratch + slab_scratch + arrived,
        [vmem()] * 12 + [anywhere()],
    )(
        faces, ends, smoothed, kappa, lanes, aggregate, order, places, diagonals, side, first,
        image, matrices,
    )
    pieces = exchange(pieces, (COARSE, FINE))
    results = call(finish, [local, local, local], 9)(
        pieces, diagonals, aggregate, side, first, image, field, second, smoothed
    )
    return tuple(result.reshape(dims) for result in results)


def solution(mesh):
    cells = P(COARSE, FINE, None)
    in_specs = (
        cells,
        cells,
        P(),
        P(COARSE, FINE, None, None),
        P(COARSE, FINE, None, None, None),
        cells,
        cells,
    )
    return jax.shard_map(
        shards, mesh=mesh, in_specs=in_specs, out_specs=(cells,) * 3, check_vma=False
    )
```

time: 658 us -> 124 us (0.19)
  local copies, waits for them, and re-layouts: 308 us -> 6.54 us
  blocking collectives: 184 us -> 80.5 us
  starting transfers between devices: 96.4 us -> 0 us
  Pallas kernels: 0 us -> 35.2 us
  matrix products: 24.9 us -> 0 us
  waiting for transfers between devices: 24.2 us -> 0 us
  other arithmetic: 9.45 us -> 0 us
  between operations: 8.92 us -> 0.69 us
    gather x6 -> x0, local copies, waits for them, and re-layouts: 273 us -> none  [the longest x3 137 us: block_apply(): return product.reshape(cells)[places].reshape(shape)]
    psum x15 -> x0, blocking collectives: 164 us -> none  [one_axis_at_a_time(): x = lax.psum(x, axis)]
    ppermute x30 -> x0, starting transfers between devices: 83.2 us -> none  [the longest x15 61.8 us: with_halo(): lax.ppermute(tail, axis, [(i, (i + 1) % count) for i in range(ends)])]
    all_to_all x2 -> x5, blocking collectives: 20 us -> 80.5 us  [exchange(): return lax.all_to_all(pieces, axis, 0, 0, tiled=True)]
    pallas_call x0 -> x6, Pallas kernels: none -> 35.2 us  [the longest x1 18.4 us: shards(): call(begin, [shape(SIDE, F_FIRST, LANES), local, shape(ROWS, LANES, dtype...]
    scatter x1 -> x0, local copies, waits for them, and re-layouts: 30.5 us -> none  [shards(): jnp.zeros((cells,), jnp.int32).at[order]]
    dot_general x3 -> x0, matrix products: 24.9 us -> none  [block_apply(): jnp.einsum('bij,bj->bi', matrices, picked, precision=lax.Precision.HIGHEST)]
    ppermute x30 -> x0, waiting for transfers between devices: 24.2 us -> none  [the longest x15 24.2 us: with_halo(): lax.ppermute(head, axis, [((i + 1) % count, i) for i in range(ends)])]
  transfers between devices with their start and end apart: 32 -> 0, of which waited for: 7 -> 0; matrix products, arithmetic and copies ran while one was open for 51% -> 0% of each run, Pallas kernels for 0% -> 0%
where the time goes in v1:
time: 124 us; the launch traced here: 123 us
  blocking collectives  80.5 us (65%)
  Pallas kernels  35.2 us (28%)
  local copies, waits for them, and re-layouts  6.54 us (5%)
    all_to_all x5, blocking collectives, exchange(): return lax.all_to_all(pieces, axis, 0, 0, tiled=True)  80.5 us
    pallas_call x1, Pallas kernels, shards(): call(begin, [shape(SIDE, F_FIRST, LANES), local, shape(ROWS, LANES, dtype...  18.4 us
    pallas_call x1, Pallas kernels, shards(): call(first_image, [shape(SIDE, SLAB, LANES), local, local, local, shape(1...  7.85 us
    pallas_call x1, Pallas kernels, shards(): call(second_image, [shape(WIDE, LANES), local, local, local], 13, block_s...  7.83 us
    unnamed x22, local copies, waits for them, and re-layouts  6.54 us

profile of v1, /device:TPU:1, one launch (start us, length us, event | category | flops | bytes accessed | tf_op | source)
XLA Modules:
  0.0 123.0 jit_solution(15337587823504456530)
XLA Ops:
  0.6 0.0 copy-start
  0.6 2.2 %copy-done = f32[1,1,64,128,128]{4,3,2,1,0:T(8,128)S(1)} copy-done((f32[1,1,64,128,128]{4,3,2,1,0:T(8,128)S(1)}, f32[1,1,64,128,128]{4,3,2,1,0:T(8,128)}, u32[]{:S(2)}) %copy-start) | copy-done | bytes 4194328
  2.8 0.0 copy-start.2
  2.8 0.8 copy-done.2
  3.6 0.0 copy-start.4
  3.6 0.8 copy-done.4
  4.3 0.0 copy-start.6
  4.3 0.8 copy-done.6
  5.1 0.0 copy-start.8
  5.1 0.8 copy-done.8
  5.9 0.0 copy-start.9
  5.9 0.7 copy-done.9
  6.5 0.0 copy-start.10
  6.5 0.7 copy-done.10
  7.2 0.0 copy-start.1
  7.2 0.0 copy-start.3
  7.2 0.0 copy-start.5
  7.2 18.4 %shard_map.94 = (f32[16,32,128]{2,1,0:T(8,128)S(1)}, f32[64,128]{1,0:T(8,128)S(1)}, s32[64,128]{1,0:T(8,128)S(1)}, f32[64,128]{1,0:T(8,128)S(1)}, f32[64,128]{1,0:T(8,128)S(1)}) custom-call(f32[16]{0:T(128)S(1)} %copy-done.9, f32[64,128]{1,0:T(8,128)S(1)} %bitcast.24, s32[64,128]{1,0:T(8,128)S(1)} %bitcast.28, s32[64,128]{1,0:T(8,128)S(1)} %bitcast.21, ...), custom_call_target="tpu_custom_call" | custom-call | tf_op jit(solution)/shard_map/pallas_call | solution.py:496
  25.5 0.0 copy-start.7
  25.6 14.1 %all_to_all.31.faces_ref = f32[16,32,128]{2,1,0:T(8,128)S(1)} all-to-all(f32[16,32,128]{2,1,0:T(8,128)S(1)} %get-tuple-element.22), channel_id=1, replica_groups=mesh['coarse'=16,'fine'=16] {'fine'}, dimensions={0} | all-to-all | bytes 524288 | tf_op jit(solution)/shard_map/all_to_all | solution.py:494
  39.7 20.3 %all_to_all.32.ends_ref = f32[16,40,128]{2,1,0:T(8,128)S(1)} all-to-all(f32[16,40,128]{2,1,0:T(8,128)S(1)} %shard_map.95), channel_id=1, replica_groups=mesh['coarse'=16,'fine'=16] {'coarse'}, dimensions={0} | all-to-all | bytes 655360 | tf_op jit(solution)/shard_map/all_to_all | solution.py:494
  60.0 0.0 copy-done.1
  60.0 0.0 copy-done.3
  60.0 0.0 copy-done.5
  60.1 7.8 %shard_map.96 = (f32[16,16,128]{2,1,0:T(8,128)S(1)}, f32[64,128]{1,0:T(8,128)S(1)}, f32[64,128]{1,0:T(8,128)S(1)}, f32[64,128]{1,0:T(8,128)S(1)}, f32[10,16,128]...) custom-call(f32[16,32,128]{2,1,0:T(8,128)S(1)} %all_to_all.31.faces_ref, ...), custom_call_target="tpu_custom_call" | custom-call | tf_op jit(solution)/shard_map/pallas_call | solution.py:508
  67.9 13.4 %all_to_all.33.faces_ref = f32[16,16,128]{2,1,0:T(8,128)S(1)} all-to-all(f32[16,16,128]{2,1,0:T(8,128)S(1)} %get-tuple-element.27), channel_id=1, replica_groups=mesh['coarse'=16,'fine'=16] {'fine'}, dimensions={0} | all-to-all | bytes 262144 | tf_op jit(solution)/shard_map/all_to_all | solution.py:494
  81.3 13.0 %all_to_all.34.ends_ref = f32[16,16,128]{2,1,0:T(8,128)S(1)} all-to-all(f32[16,16,128]{2,1,0:T(8,128)S(1)} %shard_map.97), channel_id=1, replica_groups=mesh['coarse'=16,'fine'=16] {'coarse'}, dimensions={0} | all-to-all | bytes 262144 | tf_op jit(solution)/shard_map/all_to_all | solution.py:494
  94.3 0.0 copy-done.7
  94.3 7.8 %shard_map.98 = (f32[256,128]{1,0:T(8,128)S(1)}, f32[64,128]{1,0:T(8,128)S(1)}, f32[64,128]{1,0:T(8,128)S(1)}, f32[64,128]{1,0:T(8,128)S(1)}) custom-call(f32[16,16,128]{2,1,0:T(8,128)S(1)} %all_to_all.33.faces_ref, f32[16,16,128]{2,1,0:T(8,128)S(1)} %all_to_all.34.ends_ref, f32[64,128]{1,0:T(8,128)S(1)} %get-tuple-element.28.smoothed_ref.own_ref, ...), custom_call_target="tpu_custom_call" | custom-call | tf_op jit(solution)/shard_map/pallas_call | solution.py:521
  102.1 19.7 %all_to_all.35 = f32[256,1,128]{2,1,0:T(1,128)S(1)} all-to-all(f32[256,1,128]{2,1,0:T(1,128)S(1)} %bitcast.27), channel_id=1, replica_groups=mesh['coarse'=16,'fine'=16] {'coarse','fine'}, dimensions={0} | all-to-all | bytes 262144 | tf_op jit(solution)/shard_map/all_to_all | solution.py:494
  121.9 1.1 shard_map.99
  (2 shorter events, 0.1 us)
Async XLA Ops:
  0.6 2.2 %copy-start = (f32[1,1,64,128,128]{4,3,2,1,0:T(8,128)S(1)}, f32[1,1,64,128,128]{4,3,2,1,0:T(8,128)}, u32[]{:S(2)}) copy-start(f32[1,1,64,128,128]{4,3,2,1,0:T(8,128)} %param.11) | copy-start | bytes 12582916
  2.8 0.8 copy-start.2
  3.6 0.8 copy-start.4
  4.3 0.8 copy-start.6
  5.1 0.8 copy-start.8
  5.9 0.7 copy-start.9
  6.5 0.7 copy-start.10
  7.2 52.9 %copy-start.1 = (f32[1,1,64,128,128]{4,3,2,1,0:T(8,128)S(1)}, f32[1,1,64,128,128]{4,3,2,1,0:T(8,128)}, u32[]{:S(2)}) copy-start(f32[1,1,64,128,128]{4,3,2,1,0:T(8,128)} %param.11) | copy-start | bytes 12582916
  7.2 52.9 %copy-start.3 = (s32[8,8,128]{2,1,0:T(8,128)S(1)}, s32[8,8,128]{2,1,0:T(8,128)}, u32[]{:S(2)}) copy-start(s32[8,8,128]{2,1,0:T(8,128)} %param.12) | copy-start | bytes 98308
  7.2 52.9 %copy-start.5 = (s32[1,1,64,128]{3,2,1,0:T(8,128)S(1)}, s32[1,1,64,128]{3,2,1,0:T(8,128)}, u32[]{:S(2)}) copy-start(s32[1,1,64,128]{3,2,1,0:T(8,128)} %param.10) | copy-start | bytes 98308
  25.5 68.7 %copy-start.7 = (f32[8,8,128]{2,1,0:T(8,128)S(1)}, f32[8,8,128]{2,1,0:T(8,128)}, u32[]{:S(2)}) copy-start(f32[8,8,128]{2,1,0:T(8,128)} %param.7) | copy-start | bytes 98308

commit v2 on v1

--- a/solution.py
+++ b/solution.py
@@ -29,8 +29,8 @@
     return pl.BlockSpec(memory_space=pltpu.SMEM)
 
 
-def anywhere():
-    return pl.BlockSpec(memory_space=pl.ANY)
+def hbm():
+    return pl.BlockSpec(memory_space=pltpu.HBM)
 
 
 def params():
@@ -67,8 +67,8 @@
     lanes = [index_ref[8 * g : 8 * g + 8, :] % LANES for g in range(8)]
 
     def body(step, picked):
-        for part in range(8):
-            row = step * 8 + part
+        for part in range(16):
+            row = step * 16 + part
             source = jnp.broadcast_to(source_ref[pl.ds(row, 1), :], (8, LANES))
             picked = tuple(
                 jnp.where(rows[g] == row, take_lanes(source, lanes[g]), picked[g])
@@ -77,25 +77,27 @@
         return picked
 
     zero = jnp.zeros((8, LANES), F32)
-    picked = lax.fori_loop(0, ROWS // 8, body, (zero,) * 8)
+    picked = lax.fori_loop(0, ROWS // 16, body, (zero,) * 8)
     for g in range(8):
         target_ref[8 * g : 8 * g + 8, :] = picked[g]
 
 
 def multiply_blocks(matrices_ref, picked_ref, product_ref):
+    step = 32
+
     def body(group, carry):
-        start = pl.multiple_of(group * 8, 8)
-        columns = jnp.transpose(picked_ref[pl.ds(start, 8), :])
+        start = pl.multiple_of(group * step, step)
+        columns = jnp.transpose(picked_ref[pl.ds(start, step), :])
         rows = []
-        for part in range(8):
-            matrix = matrices_ref[group * 8 + part].reshape(16, 8, LANES)
+        for part in range(step):
+            matrix = matrices_ref[group * step + part].reshape(16, 8, LANES)
             column = columns[:, part : part + 1].reshape(16, 8, 1)
             total = jnp.sum(matrix * column, axis=0)
             rows.append(jnp.sum(total, axis=0, keepdims=True))
-        product_ref[pl.ds(start, 8), :] = jnp.concatenate(rows, axis=0)
+        product_ref[pl.ds(start, step), :] = jnp.concatenate(rows, axis=0)
         return carry
 
-    lax.fori_loop(0, ROWS // 8, body, 0)
+    lax.fori_loop(0, ROWS // step, body, 0)
 
 
 def invert(order_ref):
@@ -103,18 +105,27 @@
     cell_lanes = iota((LANES, LANES), 0)
     slots = iota((ROWS, LANES), 1).astype(F32)
 
-    def body(block, total):
-        entry = order_ref[pl.ds(block, 1), :]
-        hit = cell_rows == entry // LANES
-        numbers = jnp.concatenate(
-            [jnp.where(hit, block.astype(F32), 0.0), jnp.where(hit, slots, 0.0)], axis=0
-        ).astype(jnp.bfloat16)
-        lanes = jnp.where(cell_lanes == entry % LANES, 1.0, 0.0).astype(jnp.bfloat16)
+    step = 8
+
+    def body(group, total):
+        numbers, lanes = [], []
+        for part in range(step):
+            block = group * step + part
+            entry = order_ref[pl.ds(block, 1), :]
+            hit = cell_rows == entry // LANES
+            number = jnp.where(hit, block.astype(F32), 0.0)
+            slot = jnp.where(hit, slots, 0.0)
+            numbers.append(jnp.concatenate([number, slot], axis=0).astype(jnp.bfloat16))
+            lane = jnp.where(cell_lanes == entry % LANES, 1.0, 0.0)
+            lanes.append(lane.astype(jnp.bfloat16))
         return total + lax.dot_general(
-            numbers, lanes, (((1,), (1,)), ((), ())), preferred_element_type=F32
+            jnp.concatenate(numbers, axis=1),
+            jnp.concatenate(lanes, axis=1),
+            (((1,), (1,)), ((), ())),
+            preferred_element_type=F32,
         )
 
-    total = lax.fori_loop(0, ROWS, body, jnp.zeros((LANES, LANES), F32))
+    total = lax.fori_loop(0, ROWS // step, body, jnp.zeros((LANES, LANES), F32))
     return (total[:ROWS] * float(LANES) + total[ROWS:]).astype(jnp.int32)
 
 
@@ -195,7 +206,14 @@
     return left, right
 
 
-def fill_slabs(slabs_ref, field_ref, faces_ref, ends_ref, face_row, end_row, halo_row, outside):
+def neighbours(ends_ref, owner):
+    return (
+        ends_ref.at[jnp.maximum(owner - 1, 0)],
+        ends_ref.at[jnp.minimum(owner + 1, SIDE - 1)],
+    )
+
+
+def fill_slabs(slabs_ref, field_ref, faces_ref, ends, face_row, end_row, halo_row, outside):
     owner, member = position()
     left, right = get_faces(faces_ref, face_row, member, outside)
     gap = jnp.full((8, LANES), outside, F32)
@@ -204,15 +222,10 @@
         slabs_ref[plane + 1, 8:, :] = gap
         slabs_ref[plane + 1, RIGHT : RIGHT + 1, :] = right[plane : plane + 1, :]
         slabs_ref[plane + 1, LEFT : LEFT + 1, :] = left[plane : plane + 1, :]
-    for plane, there, inside in (
-        (0, jnp.maximum(owner - 1, 0), owner > 0),
-        (9, jnp.minimum(owner + 1, SIDE - 1), owner < SIDE - 1),
-    ):
+    for plane, end_ref, inside in ((0, ends[0], owner > 0), (9, ends[1], owner < SIDE - 1)):
         slabs_ref[plane, 8:, :] = gap
-        slabs_ref[plane, :8, :] = jnp.where(
-            inside, ends_ref[there, end_row : end_row + 8, :], outside
-        )
-        halo = jnp.where(inside, ends_ref[there, halo_row : halo_row + 2, :], outside)
+        slabs_ref[plane, :8, :] = jnp.where(inside, end_ref[end_row : end_row + 8, :], outside)
+        halo = jnp.where(inside, end_ref[halo_row : halo_row + 2, :], outside)
         slabs_ref[plane, LEFT : LEFT + 1, :] = halo[0:1, :]
         slabs_ref[plane, RIGHT : RIGHT + 1, :] = halo[1:2, :]
 
@@ -245,26 +258,45 @@
 
 
 F_FIELD, F_KAPPA, F_MAP, F_SOURCE, F_DIAGONAL, F_FIRST = 0, 8, 16, 24, 26, 32
-C_FIELD, C_KAPPA, C_MAP, C_HALOS, C_SOURCE, C_DIAGONAL, C_FIRST = 0, 8, 16, 24, 30, 32, 40
+C_FIELD, C_KAPPA, C_MAP, C_HALOS, C_PLANES = 0, 8, 16, 24, 32
+C_SOURCE, C_DIAGONAL, C_FIRST = 0, 2, 8
 C_HALO_2, C_SOURCE_2, C_SECOND = 8, 10, 16
 
 
 def begin(
-    table_ref, side_ref, index_ref, order_ref, matrices_hbm, map_ref, diagonal_ref,
+    table_hbm, side_hbm, index_hbm, order_hbm, matrices_hbm, map_hbm, diagonal_hbm,
     pieces_ref, kappa_ref, places_ref, smoothed_ref, numbers_ref,
-    matrices_ref, picked_ref, product_ref, arrived,
+    table_ref, side_ref, index_ref, order_ref, map_ref, diagonal_ref, picked_ref, product_ref,
+    matrices_ref, arrived,
 ):
     owner, member = position()
-    copy = pltpu.make_async_copy(matrices_hbm, matrices_ref, arrived)
-    copy.start()
+    copies = [
+        pltpu.make_async_copy(source, target, arrived.at[number])
+        for number, (source, target) in enumerate(
+            (
+                (order_hbm, order_ref),
+                (side_hbm, side_ref),
+                (table_hbm, table_ref),
+                (index_hbm, index_ref),
+                (map_hbm, map_ref),
+                (diagonal_hbm, diagonal_ref),
+                (matrices_hbm, matrices_ref),
+            )
+        )
+    ]
+    for copy in copies:
+        copy.start()
+    copies[0].wait()
+    places_ref[...] = invert(order_ref)
+    for copy in copies[1:-1]:
+        copy.wait()
     index = index_ref[...]
     kappa = jnp.zeros((ROWS, LANES), F32)
     for entry in range(table_ref.shape[0]):
         kappa = jnp.where(index == entry, table_ref[entry], kappa)
     kappa_ref[...] = kappa
-    places_ref[...] = invert(order_ref)
     permute(side_ref, order_ref, picked_ref)
-    copy.wait()
+    copies[-1].wait()
     multiply_blocks(matrices_ref, picked_ref, product_ref)
     permute(product_ref, places_ref, smoothed_ref)
     aggregate = map_ref[...]
@@ -281,27 +313,33 @@
     put_faces(numbers_ref, pieces_ref, F_MAP, member)
 
 
-def put_planes(field_ref, pieces_ref, row, owner):
-    pieces_ref[jnp.maximum(owner - 1, 0), row : row + 8, :] = field_ref[0:8, :]
-    pieces_ref[jnp.minimum(owner + 1, SIDE - 1), row : row + 8, :] = field_ref[56:64, :]
-
-
-def relay_first(faces_ref, smoothed_ref, kappa_ref, numbers_ref, pieces_ref):
+def put_planes(field_ref, before_ref, after_ref, row):
+    before_ref[row : row + 8, :] = field_ref[0:8, :]
+    after_ref[row : row + 8, :] = field_ref[56:64, :]
+
+
+def put_halos(left, right, before_ref, after_ref, row):
+    before_ref[row : row + 1, :] = left[0:1, :]
+    before_ref[row + 1 : row + 2, :] = right[0:1, :]
+    after_ref[row : row + 1, :] = left[7:8, :]
+    after_ref[row + 1 : row + 2, :] = right[7:8, :]
+
+
+def relay_first(
+    faces_ref, smoothed_ref, kappa_ref, numbers_ref, pieces_ref, before_ref, after_ref
+):
     owner, member = position()
     sources = jnp.sum(faces_ref[:, F_SOURCE : F_SOURCE + 8, :], axis=0)
-    before, after = jnp.maximum(owner - 1, 0), jnp.minimum(owner + 1, SIDE - 1)
     for piece in range(SIDE):
-        pieces_ref[piece, C_SOURCE : C_SOURCE + 4, :] = sources[0:4, :]
-    put_planes(smoothed_ref, pieces_ref, C_FIELD, owner)
-    put_planes(kappa_ref, pieces_ref, C_KAPPA, owner)
-    put_planes(numbers_ref, pieces_ref, C_MAP, owner)
+        pieces_ref[piece] = sources
+    put_planes(smoothed_ref, before_ref, after_ref, C_FIELD)
+    put_planes(kappa_ref, before_ref, after_ref, C_KAPPA)
+    put_planes(numbers_ref, before_ref, after_ref, C_MAP)
+    before_ref[C_HALOS:, :] = jnp.zeros((8, LANES), F32)
+    after_ref[C_HALOS:, :] = jnp.zeros((8, LANES), F32)
     for number, (row, outside) in enumerate(((F_FIELD, 0.0), (F_KAPPA, 0.0), (F_MAP, -1.0))):
         left, right = get_faces(faces_ref, row, member, outside)
-        start = C_HALOS + 2 * number
-        pieces_ref[before, start : start + 1, :] = left[0:1, :]
-        pieces_ref[before, start + 1 : start + 2, :] = right[0:1, :]
-        pieces_ref[after, start : start + 1, :] = left[7:8, :]
-        pieces_ref[after, start + 1 : start + 2, :] = right[7:8, :]
+        put_halos(left, right, before_ref, after_ref, C_HALOS + 2 * number)
 
 
 def halves(pieces_ref, row):
@@ -309,10 +347,10 @@
 
 
 def first_image(
-    faces_ref, ends_ref, own_ref, own_kappa_ref, numbers_ref, map_ref, order_ref, places_ref,
+    faces_ref, ends_ref, before_ref, after_ref, own_ref, own_kappa_ref, numbers_ref, map_ref, order_ref, places_ref,
     matrices_hbm,
     pieces_ref, field_ref, image_ref, smoothed_ref, kappa_ref, lanes_ref, diagonal_ref,
-    matrices_ref, picked_ref, product_ref, slabs_ref, rows_ref, arrived,
+    picked_ref, product_ref, slabs_ref, rows_ref, matrices_ref, arrived,
 ):
     owner, member = position()
     copy = pltpu.make_async_copy(matrices_hbm, matrices_ref, arrived)
@@ -320,17 +358,14 @@
     diagonal = halves(ends_ref, C_DIAGONAL)
     diagonal_ref[...] = diagonal
     nearby(coarse_solve(halves(ends_ref, C_SOURCE), diagonal), member, rows_ref)
-    fill_slabs(
-        slabs_ref, numbers_ref, faces_ref, ends_ref, F_MAP, C_MAP, C_HALOS + 4, -1.0
-    )
+    ends = before_ref, after_ref
+    fill_slabs(slabs_ref, numbers_ref, faces_ref, ends, F_MAP, C_MAP, C_HALOS + 4, -1.0)
     row = iota((10, SLAB, LANES), 1)
     shift = jnp.where(row < 8, SIDE, jnp.where(row == RIGHT, 2 * SIDE, 0))
     number = slabs_ref[...]
     lanes_ref[...] = jnp.where(number >= 0.0, number.astype(jnp.int32) + shift, -1)
-    fill_slabs(
-        kappa_ref, own_kappa_ref, faces_ref, ends_ref, F_KAPPA, C_KAPPA, C_HALOS + 2, 0.0
-    )
-    fill_slabs(slabs_ref, own_ref, faces_ref, ends_ref, F_FIELD, C_FIELD, C_HALOS, 0.0)
+    fill_slabs(kappa_ref, own_kappa_ref, faces_ref, ends, F_KAPPA, C_KAPPA, C_HALOS + 2, 0.0)
+    fill_slabs(slabs_ref, own_ref, faces_ref, ends, F_FIELD, C_FIELD, C_HALOS, 0.0)
     add_prolonged(slabs_ref, lanes_ref, rows_ref)
     field = slabs_ref[...]
     field_ref[...] = field[1:9, :8].reshape(ROWS, LANES)
@@ -348,28 +383,25 @@
 def relay_second(faces_ref, smoothed_ref, pieces_ref):
     owner, member = position()
     sources = jnp.sum(faces_ref[:, 8:16, :], axis=0)
-    before, after = jnp.maximum(owner - 1, 0), jnp.minimum(owner + 1, SIDE - 1)
     for piece in range(SIDE):
         pieces_ref[piece, C_SOURCE_2 : C_SOURCE_2 + 2, :] = sources[0:2, :]
-    put_planes(smoothed_ref, pieces_ref, 0, owner)
+    before_ref, after_ref = neighbours(pieces_ref, owner)
+    put_planes(smoothed_ref, before_ref, after_ref, 0)
     left, right = get_faces(faces_ref, 0, member, 0.0)
-    pieces_ref[before, C_HALO_2 : C_HALO_2 + 1, :] = left[0:1, :]
-    pieces_ref[before, C_HALO_2 + 1 : C_HALO_2 + 2, :] = right[0:1, :]
-    pieces_ref[after, C_HALO_2 : C_HALO_2 + 1, :] = left[7:8, :]
-    pieces_ref[after, C_HALO_2 + 1 : C_HALO_2 + 2, :] = right[7:8, :]
+    put_halos(left, right, before_ref, after_ref, C_HALO_2)
 
 
 def second_image(
     faces_ref, ends_ref, own_ref, kappa_ref, lanes_ref, map_ref, order_ref, places_ref,
     diagonal_ref, side_ref, first_ref, image_ref, matrices_hbm,
     pieces_ref, field_ref, second_ref, smoothed_ref,
-    matrices_ref, picked_ref, product_ref, slabs_ref, rows_ref, arrived,
+    picked_ref, product_ref, slabs_ref, rows_ref, matrices_ref, arrived,
 ):
     owner, member = position()
     copy = pltpu.make_async_copy(matrices_hbm, matrices_ref, arrived)
     copy.start()
     nearby(coarse_solve(halves(ends_ref, C_SOURCE_2), diagonal_ref[...]), member, rows_ref)
-    fill_slabs(slabs_ref, own_ref, faces_ref, ends_ref, 0, 0, C_HALO_2, 0.0)
+    fill_slabs(slabs_ref, own_ref, faces_ref, neighbours(ends_ref, owner), 0, 0, C_HALO_2, 0.0)
     add_prolonged(slabs_ref, lanes_ref, rows_ref)
     slabs = slabs_ref[...]
     field = slabs[1:9, :8].reshape(ROWS, LANES)
@@ -472,13 +504,14 @@
     aggregate = aggregate_map.reshape(ROWS, LANES)
     diagonal = coarse_diagonal.reshape(1, SIDE)
     local = shape(ROWS, LANES)
-    block_scratch = [
-        pltpu.VMEM((ROWS, LANES, LANES), F32),
-        pltpu.VMEM((ROWS, LANES), F32),
-        pltpu.VMEM((ROWS, LANES), F32),
+    local_int = shape(ROWS, LANES, dtype=jnp.int32)
+    cells = pltpu.VMEM((ROWS, LANES), F32)
+    int_cells = pltpu.VMEM((ROWS, LANES), jnp.int32)
+    held = pltpu.VMEM(matrices.shape, F32)
+    scratch = [
+        cells, cells, pltpu.VMEM((10, SLAB, LANES), F32), pltpu.VMEM((SIDE, LANES), F32),
+        held, pltpu.SemaphoreType.DMA,
     ]
-    slab_scratch = [pltpu.VMEM((10, SLAB, LANES), F32), pltpu.VMEM((SIDE, LANES), F32)]
-    arrived = [pltpu.SemaphoreType.DMA]
 
     def call(kernel, outs, ins, scratch=(), specs=None):
         return pl.pallas_call(
@@ -493,17 +526,33 @@
     def exchange(pieces, axis):
         return lax.all_to_all(pieces, axis, 0, 0, tiled=True)
 
+    def ring(planes, step):
+        return lax.ppermute(planes, COARSE, [(i, (i + step) % SIDE) for i in range(SIDE)])
+
+    fixed = [
+        pltpu.with_memory_space_constraint(array, pltpu.HBM)
+        for array in (material_coefficients, side, index, order, matrices, aggregate, diagonal)
+    ]
     pieces, kappa, places, smoothed, numbers = call(
         begin,
-        [shape(SIDE, F_FIRST, LANES), local, shape(ROWS, LANES, dtype=jnp.int32), local, local],
+        [
+            shape(SIDE, F_FIRST, LANES), local, local_int, local, local,
+        ],
         7,
-        block_scratch + arrived,
-        [smem()] + [vmem()] * 3 + [anywhere()] + [vmem()] * 2,
-    )(material_coefficients, side, index, order, matrices, aggregate, diagonal)
+        [
+            pltpu.SMEM(material_coefficients.shape, F32), cells, int_cells, int_cells,
+            int_cells, pltpu.VMEM((1, SIDE), F32), cells, cells,
+            held, pltpu.SemaphoreType.DMA((7,)),
+        ],
+        [hbm()] * 7,
+    )(*fixed)
     faces = exchange(pieces, FINE)
-    (pieces,) = call(relay_first, [shape(SIDE, C_FIRST, LANES)], 4)(
-        faces, smoothed, kappa, numbers
-    )
+    pieces, before, after = call(
+        relay_first,
+        [shape(SIDE, C_FIRST, LANES), shape(C_PLANES, LANES), shape(C_PLANES, LANES)],
+        4,
+    )(faces, smoothed, kappa, numbers)
+    from_after, from_before = ring(before, -1), ring(after, 1)
     ends = exchange(pieces, COARSE)
     pieces, first, image, smoothed, kappa, lanes, diagonals = call(
         first_image,
@@ -511,10 +560,13 @@
             shape(SIDE, SLAB, LANES), local, local, local, shape(10, SLAB, LANES),
             shape(10, SLAB, LANES, dtype=jnp.int32), shape(SIDE, WIDE),
         ],
-        9,
-        block_scratch + slab_scratch + arrived,
-        [vmem()] * 8 + [anywhere()],
-    )(faces, ends, smoothed, kappa, numbers, aggregate, order, places, matrices)
+        11,
+        scratch,
+        [vmem()] * 10 + [hbm()],
+    )(
+        faces, ends, from_before, from_after, smoothed, kappa, numbers, aggregate, order,
+        places, fixed[4],
+    )
     faces = exchange(pieces, FINE)
     (pieces,) = call(relay_second, [shape(SIDE, C_SECOND, LANES)], 2)(faces, smoothed)
     ends = exchange(pieces, COARSE)
@@ -522,11 +574,11 @@
         second_image,
         [shape(WIDE, LANES), local, local, local],
         13,
-        block_scratch + slab_scratch + arrived,
-        [vmem()] * 12 + [anywhere()],
+        scratch,
+        [vmem()] * 12 + [hbm()],
     )(
         faces, ends, smoothed, kappa, lanes, aggregate, order, places, diagonals, side, first,
-        image, matrices,
+        image, fixed[4],
     )
     pieces = exchange(pieces, (COARSE, FINE))
     results = call(finish, [local, local, local], 9)(

time: 124 us -> 104 us (0.84)
  blocking collectives: 80.5 us -> 61.4 us
  starting transfers between devices: 0 us -> 15.8 us
  Pallas kernels: 35.2 us -> 22.7 us
  local copies, waits for them, and re-layouts: 6.54 us -> 0.01 us
  waiting for transfers between devices: 0 us -> 3.26 us
    all_to_all x5 -> x4, blocking collectives: 80.5 us -> 61.4 us  [exchange(): return lax.all_to_all(pieces, axis, 0, 0, tiled=True)]
    pallas_call x3, Pallas kernels: 26.2 us -> 15.2 us  [the longest x1 8.33 us: shards(): call(begin, [shape(SIDE, F_FIRST, LANES), local, local_int, local, local]...]
    all_to_all x0 -> x1, starting transfers between devices: none -> 10 us  [exchange(): return lax.all_to_all(pieces, axis, 0, 0, tiled=True)]
    unnamed x22 -> x6, local copies, waits for them, and re-layouts: 6.54 us -> 0.01 us
    ppermute x0 -> x2, starting transfers between devices: none -> 5.76 us  [ring(): lax.ppermute(planes, COARSE, [(i, (i + step) % SIDE) for i in range(SIDE)])]
    all_to_all x0 -> x1, waiting for transfers between devices: none -> 1.75 us  [exchange(): return lax.all_to_all(pieces, axis, 0, 0, tiled=True)]
    ppermute x0 -> x2, waiting for transfers between devices: none -> 1.51 us  [ring(): lax.ppermute(planes, COARSE, [(i, (i + step) % SIDE) for i in range(SIDE)])]
    pallas_call x1, Pallas kernels: 7.85 us -> 6.34 us  [shards(): call(first_image, [shape(SIDE, SLAB, LANES), local, local, local, shape(1...]
  transfers between devices with their start and end apart: 0 -> 3, of which waited for: 0 -> 2; matrix products, arithmetic and copies ran while one was open for 0% -> 0% of each run, Pallas kernels for 0% -> 0%
where the time goes in v2:
time: 104 us
  blocking collectives  61.4 us (59%)
  Pallas kernels  22.7 us (22%)
  starting transfers between devices  15.8 us (15%)
  waiting for transfers between devices  3.26 us (3%)
    all_to_all x4, blocking collectives, exchange(): return lax.all_to_all(pieces, axis, 0, 0, tiled=True)  61.4 us
    all_to_all x1, starting transfers between devices, exchange(): return lax.all_to_all(pieces, axis, 0, 0, tiled=True)  10 us
    pallas_call x1, Pallas kernels, shards(): call(begin, [shape(SIDE, F_FIRST, LANES), local, local_int, local, local]...  8.33 us
    pallas_call x1, Pallas kernels, shards(): call(first_image, [shape(SIDE, SLAB, LANES), local, local, local, shape(1...  6.34 us
    pallas_call x1, Pallas kernels, shards(): call(second_image, [shape(WIDE, LANES), local, local, local], 13, scratch...  6.23 us
    ppermute x2, starting transfers between devices, ring(): lax.ppermute(planes, COARSE, [(i, (i + step) % SIDE) for i in range(SIDE)])  5.76 us
  transfers between devices with their start and end apart: 3, of which 2 were waited for; matrix products, arithmetic and copies ran while one was open for 0% of the time, Pallas kernels for 0%

profile of v2, /device:TPU:1, one launch (start us, length us, event | category | flops | bytes accessed | tf_op | source)
XLA Modules:
  0.0 103.8 jit_solution(12667762063124347807)
XLA Ops:
  0.6 0.0 copy-start
  0.6 0.0 copy-start.1
  0.7 8.3 %shard_map.94 = (f32[16,32,128]{2,1,0:T(8,128)S(1)}, f32[64,128]{1,0:T(8,128)S(1)}, s32[64,128]{1,0:T(8,128)S(1)}, f32[64,128]{1,0:T(8,128)S(1)}, f32[64,128]{1,0:T(8,128)S(1)}) custom-call(f32[16]{0:T(128)} %table_hbm.1, f32[64,128]{1,0:T(8,128)} %bitcast.21, s32[64,128]{1,0:T(8,128)} %bitcast.28, s32[64,128]{1,0:T(8,128)} %bitcast.18, ...), custom_call_target="tpu_custom_call" | custom-call | tf_op jit(solution)/shard_map/pallas_call | solution.py:536
  9.0 0.0 copy-start.2
  9.0 14.1 %all_to_all.31.faces_ref = f32[16,32,128]{2,1,0:T(8,128)S(1)} all-to-all(f32[16,32,128]{2,1,0:T(8,128)S(1)} %get-tuple-element.25), channel_id=1, replica_groups=mesh['coarse'=16,'fine'=16] {'fine'}, dimensions={0} | all-to-all | bytes 524288 | tf_op jit(solution)/shard_map/all_to_all | solution.py:527
  23.1 0.6 shard_map.95
  23.8 10.0 %all-to-all-start.1 = ((f32[16,8,128]{2,1,0:T(8,128)}), f32[16,8,128]{2,1,0:T(8,128)S(1)}, u32[]{:S(2)}, u32[]{:S(2)}) async-start(f32[16,8,128]{2,1,0:T(8,128)} %get-tuple-element.29), calls=%async_computation.1 | async-start | bytes 131072 | tf_op jit(solution)/shard_map/all_to_all | solution.py:527
  33.8 1.4 %collective-permute-start = (f32[32,128]{1,0:T(8,128)S(1)}, f32[32,128]{1,0:T(8,128)S(1)}, u32[]{:S(2)}, u32[]{:S(2)}) collective-permute-start(f32[32,128]{1,0:T(8,128)S(1)} %get-tuple-element.30), channel_id=1, source_target_pairs={{0,16},{16,32},{32,48},{48,64},{64,80},{80,96},{96,112},{112,128},... | collective-permute-start | bytes 49160 | tf_op jit(solution)/shard_map/ppermute | solution.py:530
  35.2 4.4 %collective-permute-start.1 = (f32[32,128]{1,0:T(8,128)S(1)}, f32[32,128]{1,0:T(8,128)S(1)}, u32[]{:S(2)}, u32[]{:S(2)}) collective-permute-start(f32[32,128]{1,0:T(8,128)S(1)} %get-tuple-element.31), channel_id=1, source_target_pairs={{0,240},{16,0},{32,16},{48,32},{64,48},{80,64},{96,80},{112,96},{1... | collective-permute-start | bytes 49160 | tf_op jit(solution)/shard_map/ppermute | solution.py:530
  39.6 1.5 %collective-permute-done.before_ref = f32[32,128]{1,0:T(8,128)S(1)} collective-permute-done((f32[32,128]{1,0:T(8,128)S(1)}, f32[32,128]{1,0:T(8,128)S(1)}, u32[]{:S(2)}, u32[]{:S(2)}) %collective-permute-start) | collective-permute-done | bytes 16416 | tf_op jit(solution)/shard_map/ppermute | solution.py:530
  41.1 0.0 collective-permute-done.1.after_ref
  41.1 1.8 %all-to-all-done.1.ends_ref = f32[16,8,128]{2,1,0:T(8,128)S(1)} async-done(((f32[16,8,128]{2,1,0:T(8,128)}), f32[16,8,128]{2,1,0:T(8,128)S(1)}, u32[]{:S(2)}, u32[]{:S(2)}) %all-to-all-start.1) | async-done | bytes 65568 | tf_op jit(solution)/shard_map/all_to_all | solution.py:527
  42.8 0.0 copy-done
  42.8 0.0 copy-done.1
  42.8 6.3 %shard_map.96 = (f32[16,16,128]{2,1,0:T(8,128)S(1)}, f32[64,128]{1,0:T(8,128)S(1)}, f32[64,128]{1,0:T(8,128)S(1)}, f32[64,128]{1,0:T(8,128)S(1)}, f32[10,16,128]...) custom-call(f32[16,32,128]{2,1,0:T(8,128)S(1)} %all_to_all.31.faces_ref, ...), custom_call_target="tpu_custom_call" | custom-call | tf_op jit(solution)/shard_map/pallas_call | solution.py:557
  49.2 10.9 %all_to_all.32.faces_ref = f32[16,16,128]{2,1,0:T(8,128)S(1)} all-to-all(f32[16,16,128]{2,1,0:T(8,128)S(1)} %get-tuple-element.33), channel_id=1, replica_groups=mesh['coarse'=16,'fine'=16] {'fine'}, dimensions={0} | all-to-all | bytes 262144 | tf_op jit(solution)/shard_map/all_to_all | solution.py:527
  60.2 16.6 %all_to_all.33.ends_ref = f32[16,16,128]{2,1,0:T(8,128)S(1)} all-to-all(f32[16,16,128]{2,1,0:T(8,128)S(1)} %shard_map.97), channel_id=1, replica_groups=mesh['coarse'=16,'fine'=16] {'coarse'}, dimensions={0} | all-to-all | bytes 262144 | tf_op jit(solution)/shard_map/all_to_all | solution.py:527
  76.8 0.0 copy-done.2
  76.8 6.2 %shard_map.98 = (f32[256,128]{1,0:T(8,128)S(1)}, f32[64,128]{1,0:T(8,128)S(1)}, f32[64,128]{1,0:T(8,128)S(1)}, f32[64,128]{1,0:T(8,128)S(1)}) custom-call(f32[16,16,128]{2,1,0:T(8,128)S(1)} %all_to_all.32.faces_ref, f32[16,16,128]{2,1,0:T(8,128)S(1)} %all_to_all.33.ends_ref, f32[64,128]{1,0:T(8,128)S(1)} %get-tuple-element.34.smoothed_ref.own_ref, ...), custom_call_target="tpu_custom_call" | custom-call | tf_op jit(solution)/shard_map/pallas_call | solution.py:573
  83.0 19.7 %all_to_all.34 = f32[256,1,128]{2,1,0:T(1,128)S(1)} all-to-all(f32[256,1,128]{2,1,0:T(1,128)S(1)} %bitcast.24), channel_id=1, replica_groups=mesh['coarse'=16,'fine'=16] {'coarse','fine'}, dimensions={0} | all-to-all | bytes 262144 | tf_op jit(solution)/shard_map/all_to_all | solution.py:527
  102.7 1.1 %shard_map.99 = (f32[64,128]{1,0:T(8,128)}, f32[64,128]{1,0:T(8,128)}, f32[64,128]{1,0:T(8,128)}) custom-call(f32[256,128]{1,0:T(8,128)S(1)} %bitcast.17, f32[16,256]{1,0:T(8,128)S(1)} %get-tuple-element.37.diagonal_ref, s32[64,128]{1,0:T(8,128)S(1)} %bitcast.16, f32[64,128]{1,0:T(8,128)S(1)} %bitcast.23, f32[64,128]{1,0:T(8,128)S(1)} %get-tuple-element.38.first_ref, ...), custom_call_target="tpu_custom_call" | custom-call | tf_op jit(solution)/shard_map/pallas_call | solution.py:584
  (1 shorter events, 0.0 us)
Async XLA Ops:
  0.6 42.2 %copy-start = (s32[8,8,128]{2,1,0:T(8,128)S(1)}, s32[8,8,128]{2,1,0:T(8,128)}, u32[]{:S(2)}) copy-start(s32[8,8,128]{2,1,0:T(8,128)} %param.12) | copy-start | bytes 98308
  0.6 42.2 %copy-start.1 = (s32[1,1,64,128]{3,2,1,0:T(8,128)S(1)}, s32[1,1,64,128]{3,2,1,0:T(8,128)}, u32[]{:S(2)}) copy-start(s32[1,1,64,128]{3,2,1,0:T(8,128)} %param.10) | copy-start | bytes 98308
  9.0 67.8 %copy-start.2 = (f32[8,8,128]{2,1,0:T(8,128)S(1)}, f32[8,8,128]{2,1,0:T(8,128)}, u32[]{:S(2)}) copy-start(f32[8,8,128]{2,1,0:T(8,128)} %param.7) | copy-start | bytes 98308
  23.8 19.1 %all-to-all-start.1 = ((f32[16,8,128]{2,1,0:T(8,128)}), f32[16,8,128]{2,1,0:T(8,128)S(1)}, u32[]{:S(2)}, u32[]{:S(2)}) async-start(f32[16,8,128]{2,1,0:T(8,128)} %get-tuple-element.29), calls=%async_computation.1 | async-start | bytes 131072 | tf_op jit(solution)/shard_map/all_to_all | solution.py:527
  33.8 7.3 %collective-permute-start = (f32[32,128]{1,0:T(8,128)S(1)}, f32[32,128]{1,0:T(8,128)S(1)}, u32[]{:S(2)}, u32[]{:S(2)}) collective-permute-start(f32[32,128]{1,0:T(8,128)S(1)} %get-tuple-element.30), channel_id=1, source_target_pairs={{0,16},{16,32},{32,48},{48,64},{64,80},{80,96},{96,112},{112,128},... | collective-permute-start | bytes 49160 | tf_op jit(solution)/shard_map/ppermute | solution.py:530
  35.2 5.9 %collective-permute-start.1 = (f32[32,128]{1,0:T(8,128)S(1)}, f32[32,128]{1,0:T(8,128)S(1)}, u32[]{:S(2)}, u32[]{:S(2)}) collective-permute-start(f32[32,128]{1,0:T(8,128)S(1)} %get-tuple-element.31), channel_id=1, source_target_pairs={{0,240},{16,0},{32,16},{48,32},{64,48},{80,64},{96,80},{112,96},{1... | collective-permute-start | bytes 49160 | tf_op jit(solution)/shard_map/ppermute | solution.py:530

commit v3 on v2

v3 whole, which is shorter than its diff:
```python
import functools

import jax
import jax.numpy as jnp
from jax import lax
from jax.experimental import pallas as pl
from jax.experimental.pallas import tpu as pltpu
from jax.sharding import PartitionSpec as P

AGG = 8
COARSE, FINE = "coarse", "fine"
SWEEPS = 4
OMEGA = 0.8
SIDE = 16
ROWS = 64
LANES = 128
WIDE = SIDE * SIDE
F32, BF16 = jnp.float32, jnp.bfloat16
GROUP = 8

SLAB = 16
RIGHT, LEFT = 8, 15


def vmem():
    return pl.BlockSpec(memory_space=pltpu.VMEM)


def smem():
    return pl.BlockSpec(memory_space=pltpu.SMEM)


def hbm():
    return pl.BlockSpec(memory_space=pltpu.HBM)


def params():
    return pltpu.CompilerParams(vmem_limit_bytes=24 * 1024 * 1024)


def shape(*dims, dtype=F32):
    return jax.ShapeDtypeStruct(dims, dtype)


def iota(dims, axis):
    return lax.broadcasted_iota(jnp.int32, dims, axis)


def take_lanes(values, lanes):
    numbers = lax.GatherDimensionNumbers(
        offset_dims=(),
        collapsed_slice_dims=(1,),
        start_index_map=(1,),
        operand_batching_dims=(0,),
        start_indices_batching_dims=(0,),
    )
    return lax.gather(
        values,
        lanes[..., None],
        numbers,
        slice_sizes=(1, 1),
        mode=lax.GatherScatterMode.PROMISE_IN_BOUNDS,
    )


def split(values):
    high = values.astype(BF16)
    return high, (values - high.astype(F32)).astype(BF16)


def matmul(left, right, left_dim, right_dim):
    dims = (((left_dim,), (right_dim,)), ((), ()))
    return lax.dot_general(left, right, dims, preferred_element_type=F32)


def lane_hits(order_ref, group):
    lane = iota((LANES, LANES), 0)
    return jnp.concatenate(
        [
            jnp.where(lane == order_ref[b : b + 1, :] % LANES, 1.0, 0.0).astype(BF16)
            for b in range(group * GROUP, group * GROUP + GROUP)
        ],
        axis=1,
    )


def row_hit(order_ref, block):
    return iota((ROWS, LANES), 0) == order_ref[block : block + 1, :] // LANES


def column_sum(values):
    total = jnp.sum(values.reshape(-1, 8, LANES), axis=0)
    return jnp.sum(total, axis=0, keepdims=True)


def pick(source_ref, order_ref, picked_ref):
    source = jnp.concatenate(split(source_ref[...]), axis=0)
    for group in range(ROWS // GROUP):
        start = group * GROUP
        found = matmul(source, lane_hits(order_ref, group), 1, 0)
        found = found[:ROWS] + found[ROWS:]
        rows = []
        for part in range(GROUP):
            column = found[:, LANES * part : LANES * (part + 1)]
            rows.append(column_sum(jnp.where(row_hit(order_ref, start + part), column, 0.0)))
        picked_ref[start : start + GROUP, :] = jnp.concatenate(rows, axis=0)


def multiply_blocks(matrices_ref, picked_ref, product_ref):
    wide = (2 * GROUP, GROUP * LANES)
    spread = jnp.where(iota(wide, 0) % GROUP == iota(wide, 1) // LANES, 1.0, 0.0).astype(BF16)
    for start in range(0, ROWS, GROUP):
        high, low = split(picked_ref[start : start + GROUP, :])
        both = jnp.concatenate([high.astype(F32), low.astype(F32)], axis=0)
        columns = matmul(jnp.transpose(both).astype(BF16), spread, 1, 0)
        rows = [
            column_sum(
                matrices_ref[start + part] * columns[:, LANES * part : LANES * (part + 1)]
            )
            for part in range(GROUP)
        ]
        product_ref[start : start + GROUP, :] = jnp.concatenate(rows, axis=0)


def put_back(product_ref, order_ref, target_ref):
    total = jnp.zeros((2 * ROWS, LANES), F32)
    for group in range(ROWS // GROUP):
        start = group * GROUP
        halves_of = [part.astype(F32) for part in split(product_ref[start : start + GROUP, :])]
        hits = [row_hit(order_ref, start + part) for part in range(GROUP)]
        values = [
            jnp.concatenate(
                [
                    jnp.where(hits[part], half[part : part + 1, :], 0.0).astype(BF16)
                    for part in range(GROUP)
                ],
                axis=1,
            )
            for half in halves_of
        ]
        total = total + matmul(
            jnp.concatenate(values, axis=0), lane_hits(order_ref, group), 1, 1
        )
    target_ref[...] = total[:ROWS] + total[ROWS:]


def restrict(field, offset, member):
    total = jnp.sum(jnp.where(offset == 0, field, 0.0), axis=0, keepdims=True)
    up = jnp.sum(jnp.where(offset == 1, field, 0.0), axis=0, keepdims=True)
    down = jnp.sum(jnp.where(offset == -1, field, 0.0), axis=0, keepdims=True)
    total, up, down = (jnp.broadcast_to(x, (8, LANES)) for x in (total, up, down))
    total = total + pltpu.roll(up, AGG, 1) + pltpu.roll(down, LANES - AGG, 1)
    for distance in (1, 2, 4):
        total = total + pltpu.roll(total, LANES - distance, 1)
    lane = iota((8, LANES), 1)
    total = 0.25 * take_lanes(total, (lane % SIDE) * AGG)
    return jnp.where(lane // SIDE == member % 8, total, 0.0)


def moved(values, distance, axis, keep):
    size = values.shape[axis]
    return jnp.where(keep, pltpu.roll(values, distance % size, axis), 0.0)


def coarse_solve(source, diagonal):
    owner, lane = iota((SIDE, WIDE), 0), iota((SIDE, WIDE), 1)
    cell = lane % SIDE
    weight = OMEGA / (6.0 + diagonal)
    guess = weight * source
    for sweep in range(SWEEPS - 1):
        beside = moved(guess, 1, 0, owner > 0) + moved(guess, -1, 0, owner < SIDE - 1)
        beside = beside + moved(guess, SIDE, 1, lane >= SIDE)
        beside = beside + moved(guess, -SIDE, 1, lane < WIDE - SIDE)
        beside = beside + moved(guess, 1, 1, cell > 0) + moved(guess, -1, 1, cell < SIDE - 1)
        guess = (1.0 - OMEGA) * guess + weight * (source + beside)
    return guess


def nearby(coarse, member, rows_ref):
    rows_ref[...] = pltpu.roll(coarse, lax.rem((SIDE + 1 - member) * SIDE, WIDE), 1)[:, :LANES]


def smooth(slabs):
    total = slabs[1:9] + 0.5 * (slabs[0:8] + slabs[2:10])
    planes = []
    lane = iota((8, LANES), 1)
    row = iota((8, LANES), 0)
    for plane in range(8):
        own, ends = total[plane, :8], total[plane, 8:]
        before = jnp.where(row == 0, ends[LEFT - 8 :, :], pltpu.roll(own, 1, 0))
        after = jnp.where(row == 7, ends[:1, :], pltpu.roll(own, 7, 0))
        own = own + 0.5 * (before + after)
        below = jnp.where(lane > 0, pltpu.roll(own, 1, 1), 0.0)
        above = jnp.where(lane < LANES - 1, pltpu.roll(own, LANES - 1, 1), 0.0)
        planes.append(own + 0.5 * (below + above))
    return jnp.stack(planes)


def position():
    return lax.axis_index(COARSE), lax.axis_index(FINE)


def put_faces(field_ref, pieces_ref, rows, row, member):
    before, after = jnp.maximum(member - 1, 0), jnp.minimum(member + 1, SIDE - 1)
    pieces_ref[pl.ds(before * rows + row, 8), :] = field_ref[pl.ds(0, 8, stride=8), :]
    pieces_ref[pl.ds(after * rows + row, 8), :] = field_ref[pl.ds(7, 8, stride=8), :]


def get_faces(pieces_ref, rows, row, member, outside):
    before, after = jnp.maximum(member - 1, 0), jnp.minimum(member + 1, SIDE - 1)
    left = pieces_ref[pl.ds(before * rows + row, 8), :]
    right = pieces_ref[pl.ds(after * rows + row, 8), :]
    left = jnp.where(member > 0, left, outside)
    right = jnp.where(member < SIDE - 1, right, outside)
    return left, right


def fill_slabs(slabs_ref, field_ref, faces, pieces, outside):
    owner, member = position()
    faces_ref, face_rows, face_row = faces
    pieces_ref, rows, plane_row, halo_row = pieces
    left, right = get_faces(faces_ref, face_rows, face_row, member, outside)
    gap = jnp.full((8, LANES), outside, F32)
    for plane in range(8):
        slabs_ref[plane + 1, :8, :] = field_ref[8 * plane : 8 * plane + 8, :]
        slabs_ref[plane + 1, 8:, :] = gap
        slabs_ref[plane + 1, RIGHT : RIGHT + 1, :] = right[plane : plane + 1, :]
        slabs_ref[plane + 1, LEFT : LEFT + 1, :] = left[plane : plane + 1, :]
    for plane, there, inside in (
        (0, jnp.maximum(owner - 1, 0), owner > 0),
        (9, jnp.minimum(owner + 1, SIDE - 1), owner < SIDE - 1),
    ):
        start = there * rows
        slabs_ref[plane, 8:, :] = gap
        slabs_ref[plane, :8, :] = jnp.where(
            inside, pieces_ref[pl.ds(start + plane_row, 8), :], outside
        )
        for side, target in enumerate((LEFT, RIGHT)):
            slabs_ref[plane, target : target + 1, :] = jnp.where(
                inside, pieces_ref[pl.ds(start + halo_row + side, 1), :], outside
            )


def add_prolonged(slabs_ref, numbers_ref, rows_ref):
    owner, member = position()
    for plane in range(10):
        if plane == 0:
            there = jnp.maximum(owner - 1, 0)
        elif plane == 9:
            there = jnp.minimum(owner + 1, SIDE - 1)
        else:
            there = owner
        row = jnp.broadcast_to(rows_ref[pl.ds(there, 1), :], (8, LANES))
        for part in (0, 8):
            number = numbers_ref[plane, part : part + 8, :]
            value = take_lanes(row, jnp.maximum(number, 0))
            slabs_ref[plane, part : part + 8, :] += jnp.where(number >= 0, value, 0.0)


def operate(field, kappa):
    own, own_kappa = field[1:9, :8], kappa[1:9, :8]
    return own_kappa * (8.0 * own - smooth(field)) + own * smooth(kappa) - smooth(
        kappa * field
    )


def offsets(aggregate):
    return aggregate - iota((ROWS, LANES), 1) // AGG


F_FIELD, F_KAPPA, F_MAP, F_SOURCE, F_FIRST = 0, 8, 16, 24, 25
C_FIELD, C_KAPPA, C_MAP, C_HALOS, C_SOURCE, C_DIAGONAL, C_FIRST = 0, 8, 16, 24, 30, 32, 34
F_SOURCE_2, F_SECOND = 8, 9
C_HALO_2, C_SOURCE_2, C_SECOND = 8, 10, 12


def begin(
    table_hbm, side_hbm, index_hbm, order_hbm, matrices_hbm, map_hbm, diagonal_hbm,
    pieces_ref, kappa_ref, smoothed_ref, numbers_ref,
    table_ref, side_ref, index_ref, order_ref, map_ref, diagonal_ref, picked_ref, product_ref,
    matrices_ref, arrived,
):
    owner, member = position()
    copies = [
        pltpu.make_async_copy(source, target, arrived.at[number])
        for number, (source, target) in enumerate(
            (
                (order_hbm, order_ref),
                (side_hbm, side_ref),
                (table_hbm, table_ref),
                (index_hbm, index_ref),
                (map_hbm, map_ref),
                (diagonal_hbm, diagonal_ref),
                (matrices_hbm, matrices_ref),
            )
        )
    ]
    for copy in copies:
        copy.start()
    copies[0].wait()
    for copy in copies[1:-1]:
        copy.wait()
    index = index_ref[...]
    kappa = jnp.zeros((ROWS, LANES), F32)
    for entry in range(table_ref.shape[0]):
        kappa = jnp.where(index == entry, table_ref[entry], kappa)
    kappa_ref[...] = kappa
    pick(side_ref, order_ref, picked_ref)
    copies[-1].wait()
    multiply_blocks(matrices_ref, picked_ref, product_ref)
    put_back(product_ref, order_ref, smoothed_ref)
    aggregate = map_ref[...]
    numbers_ref[...] = aggregate.astype(F32)
    source = restrict(side_ref[...], offsets(aggregate), member)
    spread = jnp.broadcast_to(jnp.concatenate([diagonal_ref[...]] * 8, axis=1), (8, LANES))
    beside = iota((8, LANES), 1) // SIDE == (member + 1) % 8
    put_all(jnp.where(beside, spread, source), pieces_ref, F_FIRST, F_SOURCE)
    put_faces(smoothed_ref, pieces_ref, F_FIRST, F_FIELD, member)
    put_faces(kappa_ref, pieces_ref, F_FIRST, F_KAPPA, member)
    put_faces(numbers_ref, pieces_ref, F_FIRST, F_MAP, member)


def put_all(values, pieces_ref, rows, row):
    for piece in range(SIDE):
        pieces_ref[piece * rows + row : piece * rows + row + 1, :] = values[0:1, :]


def put_planes(field_ref, faces, pieces, outside):
    owner, member = position()
    left, right = get_faces(*faces, member, outside)
    pieces_ref, rows, plane_row, halo_row = pieces
    for there, plane in (
        (jnp.maximum(owner - 1, 0), 0),
        (jnp.minimum(owner + 1, SIDE - 1), 7),
    ):
        start = there * rows
        pieces_ref[pl.ds(start + plane_row, 8), :] = field_ref[8 * plane : 8 * plane + 8, :]
        for side, halo in enumerate((left, right)):
            pieces_ref[pl.ds(start + halo_row + side, 1), :] = halo[plane : plane + 1, :]


def gathered(rows, step):
    here = iota((SIDE, LANES), 0) % 8
    rows = jnp.where(iota((SIDE, LANES), 1) // SIDE == (here + step) % 8, rows, 0.0)
    parts = [jnp.sum(rows[at : at + 8], axis=0, keepdims=True) for at in (0, 8)]
    if step:
        parts = [
            pltpu.roll(jnp.broadcast_to(part, (8, LANES)), LANES - SIDE * step, 1)
            for part in parts
        ]
    return parts


def first_parts(faces_ref, pieces_ref):
    return (
        ((faces_ref, F_FIRST, F_FIELD), (pieces_ref, C_FIRST, C_FIELD, C_HALOS), 0.0),
        ((faces_ref, F_FIRST, F_KAPPA), (pieces_ref, C_FIRST, C_KAPPA, C_HALOS + 2), 0.0),
        ((faces_ref, F_FIRST, F_MAP), (pieces_ref, C_FIRST, C_MAP, C_HALOS + 4), -1.0),
    )


def second_parts(faces_ref, pieces_ref):
    return (faces_ref, F_SECOND, 0), (pieces_ref, C_SECOND, 0, C_HALO_2), 0.0


def relay_first(faces_ref, smoothed_ref, kappa_ref, numbers_ref, pieces_ref):
    rows = faces_ref[pl.ds(F_SOURCE, SIDE, stride=F_FIRST), :]
    for half in range(2):
        put_all(gathered(rows, 0)[half], pieces_ref, C_FIRST, C_SOURCE + half)
        put_all(gathered(rows, 1)[half], pieces_ref, C_FIRST, C_DIAGONAL + half)
    parts = first_parts(faces_ref, pieces_ref)
    for field_ref, part in zip((smoothed_ref, kappa_ref, numbers_ref), parts):
        put_planes(field_ref, *part)


def halves(pieces_ref, rows, row):
    return jnp.concatenate(
        [pieces_ref[pl.ds(row + half, SIDE, stride=rows), :] for half in range(2)], axis=1
    )


def first_image(
    faces_ref, ends_ref, own_ref, own_kappa_ref, numbers_ref, map_ref, order_ref,
    matrices_hbm,
    pieces_ref, field_ref, image_ref, smoothed_ref, kappa_ref, lanes_ref, diagonal_ref,
    picked_ref, product_ref, slabs_ref, rows_ref, matrices_ref, arrived,
):
    owner, member = position()
    copy = pltpu.make_async_copy(matrices_hbm, matrices_ref, arrived)
    copy.start()
    diagonal = halves(ends_ref, C_FIRST, C_DIAGONAL)
    diagonal_ref[...] = diagonal
    nearby(coarse_solve(halves(ends_ref, C_FIRST, C_SOURCE), diagonal), member, rows_ref)
    parts = first_parts(faces_ref, ends_ref)
    fill_slabs(slabs_ref, numbers_ref, *parts[2])
    row = iota((10, SLAB, LANES), 1)
    shift = jnp.where(row < 8, SIDE, jnp.where(row == RIGHT, 2 * SIDE, 0))
    number = slabs_ref[...]
    lanes_ref[...] = jnp.where(number >= 0.0, number.astype(jnp.int32) + shift, -1)
    fill_slabs(kappa_ref, own_kappa_ref, *parts[1])
    fill_slabs(slabs_ref, own_ref, *parts[0])
    add_prolonged(slabs_ref, lanes_ref, rows_ref)
    field = slabs_ref[...]
    field_ref[...] = field[1:9, :8].reshape(ROWS, LANES)
    image_ref[...] = operate(field, kappa_ref[...]).reshape(ROWS, LANES)
    pick(image_ref, order_ref, picked_ref)
    copy.wait()
    multiply_blocks(matrices_ref, picked_ref, product_ref)
    put_back(product_ref, order_ref, smoothed_ref)
    source = restrict(image_ref[...], offsets(map_ref[...]), member)
    put_all(source, pieces_ref, F_SECOND, F_SOURCE_2)
    put_faces(smoothed_ref, pieces_ref, F_SECOND, 0, member)


def relay_second(faces_ref, smoothed_ref, pieces_ref):
    rows = faces_ref[pl.ds(F_SOURCE_2, SIDE, stride=F_SECOND), :]
    for half, values in enumerate(gathered(rows, 0)):
        put_all(values, pieces_ref, C_SECOND, C_SOURCE_2 + half)
    put_planes(smoothed_ref, *second_parts(faces_ref, pieces_ref))


def second_image(
    faces_ref, ends_ref, own_ref, kappa_ref, lanes_ref, map_ref, order_ref,
    diagonal_ref, side_ref, first_ref, image_ref, matrices_hbm,
    pieces_ref, field_ref, second_ref, smoothed_ref,
    picked_ref, product_ref, slabs_ref, rows_ref, matrices_ref, arrived,
):
    owner, member = position()
    copy = pltpu.make_async_copy(matrices_hbm, matrices_ref, arrived)
    copy.start()
    nearby(coarse_solve(halves(ends_ref, C_SECOND, C_SOURCE_2), diagonal_ref[...]), member, rows_ref)
    fill_slabs(slabs_ref, own_ref, *second_parts(faces_ref, ends_ref))
    add_prolonged(slabs_ref, lanes_ref, rows_ref)
    slabs = slabs_ref[...]
    field = slabs[1:9, :8].reshape(ROWS, LANES)
    field_ref[...] = field
    second = operate(slabs, kappa_ref[...]).reshape(ROWS, LANES)
    second_ref[...] = second
    pick(second_ref, order_ref, picked_ref)
    copy.wait()
    multiply_blocks(matrices_ref, picked_ref, product_ref)
    put_back(product_ref, order_ref, smoothed_ref)
    first = first_ref[...]
    image = image_ref[...]
    pairs = (
        side_ref[...] * first,
        first * image,
        image * field,
        second * first,
        second * field,
        second * smoothed_ref[...],
    )
    lane = iota((8, LANES), 1)
    message = restrict(second, offsets(map_ref[...]), member)
    beside = lax.rem(member + 1, 8) * SIDE
    for number, pair in enumerate(pairs):
        total = jnp.sum(jnp.sum(pair, axis=0, keepdims=True), axis=1, keepdims=True)
        message = jnp.where(lane == beside + number, total, message)
    for start in range(0, WIDE, 8):
        pieces_ref[start : start + 8, :] = message


def finish(
    pieces_ref, diagonal_ref, map_ref, side_ref, first_ref, image_ref, field_ref, second_ref,
    smoothed_ref,
    solution_ref, residual_ref, search_ref,
):
    owner, member = position()
    pieces = pieces_ref[...].reshape(SIDE, SIDE, LANES)
    place = iota((SIDE, LANES), 0) % 8
    group = iota((SIDE, LANES), 1) // SIDE
    pieces_sum = jnp.sum(pieces, axis=0)
    sums = jnp.where(group == (place + 1) % 8, pieces_sum, 0.0)
    kept = jnp.where((group == place)[None], pieces, 0.0)
    source = jnp.concatenate(
        [jnp.sum(kept[:, :8], axis=1), jnp.sum(kept[:, 8:], axis=1)], axis=1
    )
    coarse = coarse_solve(source, diagonal_ref[...])
    lane = iota((1, LANES), 1)
    sums = jnp.sum(sums, axis=0, keepdims=True)

    def total(number):
        picked = jnp.where(lane % SIDE == number, sums, 0.0)
        return jnp.sum(picked, axis=1, keepdims=True)

    def whole(array):
        return jnp.sum(jnp.sum(array, axis=0, keepdims=True), axis=1, keepdims=True)

    r_z, z_az, w_y, v_z, v_y, v_bv = (total(number) for number in range(6))
    v_u = v_bv + 4.0 * whole(source * coarse)
    alpha = r_z / z_az
    following = r_z - 2.0 * alpha * z_az + alpha * alpha * w_y
    grown = 1.0 + following / r_z
    product = grown * grown * z_az - grown * alpha * (v_z + w_y) + alpha * alpha * v_y
    again = following / product
    one = alpha + again * grown
    two = again * alpha
    last = (
        r_z - 2.0 * one * z_az + 2.0 * two * v_z + one * one * w_y
        - 2.0 * one * two * v_y + two * two * v_u
    )
    ratio = last / following
    lanes = iota((SIDE, WIDE), 1)
    rows = iota((SIDE, WIDE), 0)
    near = pltpu.roll(coarse, lax.rem((SIDE - member) * SIDE, WIDE), 1)[:, :LANES]
    row = jnp.sum(
        jnp.where(iota((SIDE, LANES), 0) == owner, near, 0.0), axis=0, keepdims=True
    )
    row = jnp.broadcast_to(row, (8, LANES))
    for g in range(8):
        at = slice(8 * g, 8 * g + 8)
        first, image, field, second = (
            ref[at, :] for ref in (first_ref, image_ref, field_ref, second_ref)
        )
        smoothed = smoothed_ref[at, :] + take_lanes(row, map_ref[at, :])
        solution_ref[at, :] = one * first - two * field
        residual_ref[at, :] = side_ref[at, :] - one * image + two * second
        search_ref[at, :] = (
            first - one * field + two * smoothed + ratio * (grown * first - alpha * field)
        )


def shards(
    right_side, coefficient_index, material_coefficients, block_cells, block_inverses,
    aggregate_map, coarse_diagonal,
):
    dims = right_side.shape
    side = right_side.reshape(ROWS, LANES)
    index = coefficient_index.reshape(ROWS, LANES)
    order = block_cells.reshape(ROWS, LANES)
    matrices = block_inverses.reshape(ROWS, LANES, LANES)
    aggregate = aggregate_map.reshape(ROWS, LANES)
    diagonal = coarse_diagonal.reshape(1, SIDE)
    local = shape(ROWS, LANES)
    cells = pltpu.VMEM((ROWS, LANES), F32)
    int_cells = pltpu.VMEM((ROWS, LANES), jnp.int32)
    held = pltpu.VMEM(matrices.shape, F32)
    scratch = [
        cells, cells, pltpu.VMEM((10, SLAB, LANES), F32), pltpu.VMEM((SIDE, LANES), F32),
        held, pltpu.SemaphoreType.DMA,
    ]

    def call(kernel, outs, ins, scratch=(), specs=None):
        return pl.pallas_call(
            kernel,
            out_shape=outs,
            in_specs=specs or [vmem()] * ins,
            out_specs=[vmem()] * len(outs),
            scratch_shapes=list(scratch),
            compiler_params=params(),
        )

    def exchange(pieces, axis):
        rows = pieces.shape
        pieces = lax.all_to_all(pieces.reshape(rows[0], 1, LANES), axis, 0, 0, tiled=True)
        return pieces.reshape(rows)

    fixed = [
        pltpu.with_memory_space_constraint(array, pltpu.HBM)
        for array in (material_coefficients, side, index, order, matrices, aggregate, diagonal)
    ]
    pieces, kappa, smoothed, numbers = call(
        begin,
        [
            shape(SIDE * F_FIRST, LANES), local, local, local,
        ],
        7,
        [
            pltpu.SMEM(material_coefficients.shape, F32), cells, int_cells, int_cells,
            int_cells, pltpu.VMEM((1, SIDE), F32), cells, cells,
            held, pltpu.SemaphoreType.DMA((7,)),
        ],
        [hbm()] * 7,
    )(*fixed)
    faces = exchange(pieces, FINE)
    (pieces,) = call(relay_first, [shape(SIDE * C_FIRST, LANES)], 4)(
        faces, smoothed, kappa, numbers
    )
    ends = exchange(pieces, COARSE)
    pieces, first, image, smoothed, kappa, lanes, diagonals = call(
        first_image,
        [
            shape(SIDE * F_SECOND, LANES), local, local, local, shape(10, SLAB, LANES),
            shape(10, SLAB, LANES, dtype=jnp.int32), shape(SIDE, WIDE),
        ],
        11,
        scratch,
        [vmem()] * 7 + [hbm()],
    )(
        faces, ends, smoothed, kappa, numbers, aggregate, order, fixed[4],
    )
    faces = exchange(pieces, FINE)
    (pieces,) = call(relay_second, [shape(SIDE * C_SECOND, LANES)], 2)(faces, smoothed)
    ends = exchange(pieces, COARSE)
    pieces, field, second, smoothed = call(
        second_image,
        [shape(WIDE, LANES), local, local, local],
        13,
        scratch,
        [vmem()] * 11 + [hbm()],
    )(
        faces, ends, smoothed, kappa, lanes, aggregate, order, diagonals, side, first,
        image, fixed[4],
    )
    pieces = exchange(pieces, (COARSE, FINE))
    results = call(finish, [local, local, local], 9)(
        pieces, diagonals, aggregate, side, first, image, field, second, smoothed
    )
    return tuple(result.reshape(dims) for result in results)


def solution(mesh):
    cells = P(COARSE, FINE, None)
    in_specs = (
        cells,
        cells,
        P(),
        P(COARSE, FINE, None, None),
        P(COARSE, FINE, None, None, None),
        cells,
        cells,
    )
    return jax.shard_map(
        shards, mesh=mesh, in_specs=in_specs, out_specs=(cells,) * 3, check_vma=False
    )
```

time: 104 us -> 94 us (0.904)
  blocking collectives: 61.4 us -> 78.2 us
  starting transfers between devices: 15.8 us -> 0 us
  Pallas kernels: 22.7 us -> 14.7 us
  waiting for transfers between devices: 3.26 us -> 0 us
    all_to_all x4 -> x5, blocking collectives: 61.4 us -> 78.2 us  [exchange(): lax.all_to_all(pieces.reshape(rows[0], 1, LANES), axis, 0, 0, tiled=True)]
    all_to_all x1 -> x0, starting transfers between devices: 10 us -> none  [exchange(): return lax.all_to_all(pieces, axis, 0, 0, tiled=True)]
    pallas_call x4, Pallas kernels: 15.3 us -> 8.92 us  [the longest x1 4.57 us: shards(): call(first_image, [shape(SIDE * F_SECOND, LANES), local, local, local, sh...]
    ppermute x2 -> x0, starting transfers between devices: 5.76 us -> none  [ring(): lax.ppermute(planes, COARSE, [(i, (i + step) % SIDE) for i in range(SIDE)])]
    all_to_all x1 -> x0, waiting for transfers between devices: 1.75 us -> none  [exchange(): return lax.all_to_all(pieces, axis, 0, 0, tiled=True)]
    pallas_call x1, Pallas kernels: 6.23 us -> 4.64 us  [shards(): call(second_image, [shape(WIDE, LANES), local, local, local], 13, scratch...]
    ppermute x2 -> x0, waiting for transfers between devices: 1.51 us -> none  [ring(): lax.ppermute(planes, COARSE, [(i, (i + step) % SIDE) for i in range(SIDE)])]
  transfers between devices with their start and end apart: 3 -> 0, of which waited for: 2 -> 0; matrix products, arithmetic and copies ran while one was open for 0% -> 0% of each run, Pallas kernels for 0% -> 0%
where the time goes in v3:
time: 94 us; the launch traced here: 93.6 us
  blocking collectives  78.2 us (83%)
  Pallas kernels  14.7 us (16%)
    all_to_all x5, blocking collectives, exchange(): lax.all_to_all(pieces.reshape(rows[0], 1, LANES), axis, 0, 0, tiled=True)  78.2 us
    pallas_call x1, Pallas kernels, shards(): call(second_image, [shape(WIDE, LANES), local, local, local], 13, scratch...  4.64 us
    pallas_call x1, Pallas kernels, shards(): call(first_image, [shape(SIDE * F_SECOND, LANES), local, local, local, sh...  4.57 us
    pallas_call x1, Pallas kernels, shards(): call(begin, [shape(SIDE * F_FIRST, LANES), local, local, local], 7, [pltp...  4.24 us

profile of v3, /device:TPU:1, one launch (start us, length us, event | category | flops | bytes accessed | tf_op | source)
XLA Modules:
  0.0 93.6 jit_solution(18217459308098090981)
XLA Ops:
  0.6 0.0 copy-start
  0.6 0.0 copy-start.1
  0.7 4.2 %shard_map.94 = (f32[400,128]{1,0:T(8,128)S(1)}, f32[64,128]{1,0:T(8,128)S(1)}, f32[64,128]{1,0:T(8,128)S(1)}, f32[64,128]{1,0:T(8,128)S(1)}) custom-call(f32[16]{0:T(128)} %table_hbm.1, f32[64,128]{1,0:T(8,128)} %bitcast.45, s32[64,128]{1,0:T(8,128)} %bitcast.54, s32[64,128]{1,0:T(8,128)} %bitcast.42, f32[64,128,128]{2,1,0:T(8,128)} %bitcast.51, ...), custom_call_target="tpu_custom_call" | custom-call | tf_op jit(solution)/shard_map/pallas_call | solution.py:562
  4.9 0.0 copy-start.2
  4.9 13.7 %all_to_all.25 = f32[400,1,128]{2,1,0:T(1,128)S(1)} all-to-all(f32[400,1,128]{2,1,0:T(1,128)S(1)} %bitcast.48), channel_id=1, replica_groups=mesh['coarse'=16,'fine'=16] {'fine'}, dimensions={0} | all-to-all | bytes 409600 | tf_op jit(solution)/shard_map/all_to_all | solution.py:555
  18.6 0.1 shard_map.95
  18.7 20.2 %all_to_all.26 = f32[544,1,128]{2,1,0:T(1,128)S(1)} all-to-all(f32[544,1,128]{2,1,0:T(1,128)S(1)} %bitcast.32), channel_id=1, replica_groups=mesh['coarse'=16,'fine'=16] {'coarse'}, dimensions={0} | all-to-all | bytes 557056 | tf_op jit(solution)/shard_map/all_to_all | solution.py:555
  38.9 0.0 copy-done
  38.9 0.0 copy-done.1
  38.9 4.6 %shard_map.96 = (f32[144,128]{1,0:T(8,128)S(1)}, f32[64,128]{1,0:T(8,128)S(1)}, f32[64,128]{1,0:T(8,128)S(1)}, f32[64,128]{1,0:T(8,128)S(1)}, f32[10,16,128]{2,1...) custom-call(f32[400,128]{1,0:T(8,128)S(1)} %bitcast.30, f32[544,128]{1,0:T(8,128)S(1)} %bitcast.31, ...), custom_call_target="tpu_custom_call" | custom-call | tf_op jit(solution)/shard_map/pallas_call | solution.py:580
  43.5 11.8 %all_to_all.27 = f32[144,1,128]{2,1,0:T(1,128)S(1)} all-to-all(f32[144,1,128]{2,1,0:T(1,128)S(1)} %bitcast.50), channel_id=1, replica_groups=mesh['coarse'=16,'fine'=16] {'fine'}, dimensions={0} | all-to-all | bytes 147456 | tf_op jit(solution)/shard_map/all_to_all | solution.py:555
  55.3 12.9 %all_to_all.28 = f32[192,1,128]{2,1,0:T(1,128)S(1)} all-to-all(f32[192,1,128]{2,1,0:T(1,128)S(1)} %bitcast.40), channel_id=1, replica_groups=mesh['coarse'=16,'fine'=16] {'coarse'}, dimensions={0} | all-to-all | bytes 196608 | tf_op jit(solution)/shard_map/all_to_all | solution.py:555
  68.3 0.0 copy-done.2
  68.3 4.6 %shard_map.98 = (f32[256,128]{1,0:T(8,128)S(1)}, f32[64,128]{1,0:T(8,128)S(1)}, f32[64,128]{1,0:T(8,128)S(1)}, f32[64,128]{1,0:T(8,128)S(1)}) custom-call(f32[144,128]{1,0:T(8,128)S(1)} %bitcast.34, f32[192,128]{1,0:T(8,128)S(1)} %bitcast.41, f32[64,128]{1,0:T(8,128)S(1)} %get-tuple-element.26.smoothed_ref.own_ref, ...), custom_call_target="tpu_custom_call" | custom-call | tf_op jit(solution)/shard_map/pallas_call | solution.py:595
  72.9 19.6 %all_to_all.29 = f32[256,1,128]{2,1,0:T(1,128)S(1)} all-to-all(f32[256,1,128]{2,1,0:T(1,128)S(1)} %bitcast.49), channel_id=1, replica_groups=mesh['coarse'=16,'fine'=16] {'coarse','fine'}, dimensions={0} | all-to-all | bytes 262144 | tf_op jit(solution)/shard_map/all_to_all | solution.py:555
  92.5 1.1 %shard_map.99 = (f32[64,128]{1,0:T(8,128)}, f32[64,128]{1,0:T(8,128)}, f32[64,128]{1,0:T(8,128)}) custom-call(f32[256,128]{1,0:T(8,128)S(1)} %bitcast.39, f32[16,256]{1,0:T(8,128)S(1)} %get-tuple-element.29.diagonal_ref, s32[64,128]{1,0:T(8,128)S(1)} %bitcast.38, f32[64,128]{1,0:T(8,128)S(1)} %bitcast.47, f32[64,128]{1,0:T(8,128)S(1)} %get-tuple-element.30.first_ref, ...), custom_call_target="tpu_custom_call" | custom-call | tf_op jit(solution)/shard_map/pallas_call | solution.py:606
  (1 shorter events, 0.0 us)
Async XLA Ops:
  0.6 38.3 %copy-start = (s32[8,8,128]{2,1,0:T(8,128)S(1)}, s32[8,8,128]{2,1,0:T(8,128)}, u32[]{:S(2)}) copy-start(s32[8,8,128]{2,1,0:T(8,128)} %param.12) | copy-start | bytes 98308
  0.6 38.2 %copy-start.1 = (s32[1,1,64,128]{3,2,1,0:T(8,128)S(1)}, s32[1,1,64,128]{3,2,1,0:T(8,128)}, u32[]{:S(2)}) copy-start(s32[1,1,64,128]{3,2,1,0:T(8,128)} %param.10) | copy-start | bytes 98308
  4.9 63.4 %copy-start.2 = (f32[8,8,128]{2,1,0:T(8,128)S(1)}, f32[8,8,128]{2,1,0:T(8,128)}, u32[]{:S(2)}) copy-start(f32[8,8,128]{2,1,0:T(8,128)} %param.7) | copy-start | bytes 98308

commit v4 on v3

--- a/solution.py
+++ b/solution.py
@@ -215,26 +215,23 @@
     return left, right
 
 
-def fill_slabs(slabs_ref, field_ref, faces, pieces, outside):
-    owner, member = position()
-    faces_ref, face_rows, face_row = faces
-    pieces_ref, rows, plane_row, halo_row = pieces
-    left, right = get_faces(faces_ref, face_rows, face_row, member, outside)
+def fill_slabs(slabs_ref, field_ref, faces, pieces, outside, planes):
+    owner, member = position()
+    pieces_ref, rows, halo_row = pieces
+    left, right = get_faces(*faces, member, outside)
     gap = jnp.full((8, LANES), outside, F32)
     for plane in range(8):
         slabs_ref[plane + 1, :8, :] = field_ref[8 * plane : 8 * plane + 8, :]
         slabs_ref[plane + 1, 8:, :] = gap
         slabs_ref[plane + 1, RIGHT : RIGHT + 1, :] = right[plane : plane + 1, :]
         slabs_ref[plane + 1, LEFT : LEFT + 1, :] = left[plane : plane + 1, :]
-    for plane, there, inside in (
-        (0, jnp.maximum(owner - 1, 0), owner > 0),
-        (9, jnp.minimum(owner + 1, SIDE - 1), owner < SIDE - 1),
+    for plane, there, inside, own in (
+        (0, jnp.maximum(owner - 1, 0), owner > 0, planes[0]),
+        (9, jnp.minimum(owner + 1, SIDE - 1), owner < SIDE - 1, planes[1]),
     ):
         start = there * rows
         slabs_ref[plane, 8:, :] = gap
-        slabs_ref[plane, :8, :] = jnp.where(
-            inside, pieces_ref[pl.ds(start + plane_row, 8), :], outside
-        )
+        slabs_ref[plane, :8, :] = jnp.where(inside, own, outside)
         for side, target in enumerate((LEFT, RIGHT)):
             slabs_ref[plane, target : target + 1, :] = jnp.where(
                 inside, pieces_ref[pl.ds(start + halo_row + side, 1), :], outside
@@ -269,48 +266,60 @@
 
 
 F_FIELD, F_KAPPA, F_MAP, F_SOURCE, F_FIRST = 0, 8, 16, 24, 25
-C_FIELD, C_KAPPA, C_MAP, C_HALOS, C_SOURCE, C_DIAGONAL, C_FIRST = 0, 8, 16, 24, 30, 32, 34
+C_FIELD, C_HALOS, C_SOURCE, C_DIAGONAL, C_FIRST = 0, 8, 14, 16, 18
 F_SOURCE_2, F_SECOND = 8, 9
 C_HALO_2, C_SOURCE_2, C_SECOND = 8, 10, 12
 
 
-def begin(
-    table_hbm, side_hbm, index_hbm, order_hbm, matrices_hbm, map_hbm, diagonal_hbm,
-    pieces_ref, kappa_ref, smoothed_ref, numbers_ref,
-    table_ref, side_ref, index_ref, order_ref, map_ref, diagonal_ref, picked_ref, product_ref,
-    matrices_ref, arrived,
-):
-    owner, member = position()
+def fetch(pairs, arrived):
     copies = [
         pltpu.make_async_copy(source, target, arrived.at[number])
-        for number, (source, target) in enumerate(
-            (
-                (order_hbm, order_ref),
-                (side_hbm, side_ref),
-                (table_hbm, table_ref),
-                (index_hbm, index_ref),
-                (map_hbm, map_ref),
-                (diagonal_hbm, diagonal_ref),
-                (matrices_hbm, matrices_ref),
-            )
-        )
+        for number, (source, target) in enumerate(pairs)
     ]
     for copy in copies:
         copy.start()
-    copies[0].wait()
-    for copy in copies[1:-1]:
+    return copies
+
+
+def prepare(
+    table_hbm, index_hbm, map_hbm,
+    kappa_ref, numbers_ref, before_ref, after_ref,
+    table_ref, index_ref, map_ref, arrived,
+):
+    pairs = (table_hbm, table_ref), (index_hbm, index_ref), (map_hbm, map_ref)
+    for copy in fetch(pairs, arrived):
         copy.wait()
     index = index_ref[...]
     kappa = jnp.zeros((ROWS, LANES), F32)
     for entry in range(table_ref.shape[0]):
         kappa = jnp.where(index == entry, table_ref[entry], kappa)
     kappa_ref[...] = kappa
+    numbers = map_ref[...].astype(F32)
+    numbers_ref[...] = numbers
+    before_ref[:8, :], before_ref[8:, :] = kappa[:8], numbers[:8]
+    after_ref[:8, :], after_ref[8:, :] = kappa[56:], numbers[56:]
+
+
+def begin(
+    side_hbm, order_hbm, matrices_hbm, diagonal_hbm, kappa_ref, numbers_ref,
+    pieces_ref, smoothed_ref,
+    side_ref, order_ref, matrices_ref, diagonal_ref, picked_ref, product_ref, arrived,
+):
+    owner, member = position()
+    pairs = (
+        (side_hbm, side_ref),
+        (order_hbm, order_ref),
+        (diagonal_hbm, diagonal_ref),
+        (matrices_hbm, matrices_ref),
+    )
+    copies = fetch(pairs, arrived)
+    for copy in copies[:-1]:
+        copy.wait()
     pick(side_ref, order_ref, picked_ref)
     copies[-1].wait()
     multiply_blocks(matrices_ref, picked_ref, product_ref)
     put_back(product_ref, order_ref, smoothed_ref)
-    aggregate = map_ref[...]
-    numbers_ref[...] = aggregate.astype(F32)
+    aggregate = numbers_ref[...].astype(jnp.int32)
     source = restrict(side_ref[...], offsets(aggregate), member)
     spread = jnp.broadcast_to(jnp.concatenate([diagonal_ref[...]] * 8, axis=1), (8, LANES))
     beside = iota((8, LANES), 1) // SIDE == (member + 1) % 8
@@ -325,18 +334,29 @@
         pieces_ref[piece * rows + row : piece * rows + row + 1, :] = values[0:1, :]
 
 
-def put_planes(field_ref, faces, pieces, outside):
+def put_halos(faces, pieces, outside):
     owner, member = position()
     left, right = get_faces(*faces, member, outside)
-    pieces_ref, rows, plane_row, halo_row = pieces
+    pieces_ref, rows, row = pieces
     for there, plane in (
         (jnp.maximum(owner - 1, 0), 0),
         (jnp.minimum(owner + 1, SIDE - 1), 7),
     ):
-        start = there * rows
-        pieces_ref[pl.ds(start + plane_row, 8), :] = field_ref[8 * plane : 8 * plane + 8, :]
         for side, halo in enumerate((left, right)):
-            pieces_ref[pl.ds(start + halo_row + side, 1), :] = halo[plane : plane + 1, :]
+            pieces_ref[pl.ds(there * rows + row + side, 1), :] = halo[plane : plane + 1, :]
+
+
+def put_planes(field_ref, pieces_ref, rows):
+    owner, member = position()
+    before, after = jnp.maximum(owner - 1, 0), jnp.minimum(owner + 1, SIDE - 1)
+    pieces_ref[pl.ds(before * rows, 8), :] = field_ref[:8, :]
+    pieces_ref[pl.ds(after * rows, 8), :] = field_ref[56:, :]
+
+
+def get_planes(pieces_ref, rows):
+    owner, member = position()
+    before, after = jnp.maximum(owner - 1, 0), jnp.minimum(owner + 1, SIDE - 1)
+    return pieces_ref[pl.ds(before * rows, 8), :], pieces_ref[pl.ds(after * rows, 8), :]
 
 
 def gathered(rows, step):
@@ -353,24 +373,24 @@
 
 def first_parts(faces_ref, pieces_ref):
     return (
-        ((faces_ref, F_FIRST, F_FIELD), (pieces_ref, C_FIRST, C_FIELD, C_HALOS), 0.0),
-        ((faces_ref, F_FIRST, F_KAPPA), (pieces_ref, C_FIRST, C_KAPPA, C_HALOS + 2), 0.0),
-        ((faces_ref, F_FIRST, F_MAP), (pieces_ref, C_FIRST, C_MAP, C_HALOS + 4), -1.0),
+        ((faces_ref, F_FIRST, F_FIELD), (pieces_ref, C_FIRST, C_HALOS), 0.0),
+        ((faces_ref, F_FIRST, F_KAPPA), (pieces_ref, C_FIRST, C_HALOS + 2), 0.0),
+        ((faces_ref, F_FIRST, F_MAP), (pieces_ref, C_FIRST, C_HALOS + 4), -1.0),
     )
 
 
 def second_parts(faces_ref, pieces_ref):
-    return (faces_ref, F_SECOND, 0), (pieces_ref, C_SECOND, 0, C_HALO_2), 0.0
-
-
-def relay_first(faces_ref, smoothed_ref, kappa_ref, numbers_ref, pieces_ref):
+    return (faces_ref, F_SECOND, 0), (pieces_ref, C_SECOND, C_HALO_2), 0.0
+
+
+def relay_first(faces_ref, smoothed_ref, pieces_ref):
     rows = faces_ref[pl.ds(F_SOURCE, SIDE, stride=F_FIRST), :]
     for half in range(2):
         put_all(gathered(rows, 0)[half], pieces_ref, C_FIRST, C_SOURCE + half)
         put_all(gathered(rows, 1)[half], pieces_ref, C_FIRST, C_DIAGONAL + half)
-    parts = first_parts(faces_ref, pieces_ref)
-    for field_ref, part in zip((smoothed_ref, kappa_ref, numbers_ref), parts):
-        put_planes(field_ref, *part)
+    put_planes(smoothed_ref, pieces_ref, C_FIRST)
+    for part in first_parts(faces_ref, pieces_ref):
+        put_halos(*part)
 
 
 def halves(pieces_ref, rows, row):
@@ -380,7 +400,7 @@
 
 
 def first_image(
-    faces_ref, ends_ref, own_ref, own_kappa_ref, numbers_ref, map_ref, order_ref,
+    faces_ref, ends_ref, before_ref, after_ref, own_ref, own_kappa_ref, numbers_ref, map_ref, order_ref,
     matrices_hbm,
     pieces_ref, field_ref, image_ref, smoothed_ref, kappa_ref, lanes_ref, diagonal_ref,
     picked_ref, product_ref, slabs_ref, rows_ref, matrices_ref, arrived,
@@ -392,13 +412,13 @@
     diagonal_ref[...] = diagonal
     nearby(coarse_solve(halves(ends_ref, C_FIRST, C_SOURCE), diagonal), member, rows_ref)
     parts = first_parts(faces_ref, ends_ref)
-    fill_slabs(slabs_ref, numbers_ref, *parts[2])
+    fill_slabs(slabs_ref, numbers_ref, *parts[2], (before_ref[8:, :], after_ref[8:, :]))
     row = iota((10, SLAB, LANES), 1)
     shift = jnp.where(row < 8, SIDE, jnp.where(row == RIGHT, 2 * SIDE, 0))
     number = slabs_ref[...]
     lanes_ref[...] = jnp.where(number >= 0.0, number.astype(jnp.int32) + shift, -1)
-    fill_slabs(kappa_ref, own_kappa_ref, *parts[1])
-    fill_slabs(slabs_ref, own_ref, *parts[0])
+    fill_slabs(kappa_ref, own_kappa_ref, *parts[1], (before_ref[:8, :], after_ref[:8, :]))
+    fill_slabs(slabs_ref, own_ref, *parts[0], get_planes(ends_ref, C_FIRST))
     add_prolonged(slabs_ref, lanes_ref, rows_ref)
     field = slabs_ref[...]
     field_ref[...] = field[1:9, :8].reshape(ROWS, LANES)
@@ -416,7 +436,8 @@
     rows = faces_ref[pl.ds(F_SOURCE_2, SIDE, stride=F_SECOND), :]
     for half, values in enumerate(gathered(rows, 0)):
         put_all(values, pieces_ref, C_SECOND, C_SOURCE_2 + half)
-    put_planes(smoothed_ref, *second_parts(faces_ref, pieces_ref))
+    put_planes(smoothed_ref, pieces_ref, C_SECOND)
+    put_halos(*second_parts(faces_ref, pieces_ref))
 
 
 def second_image(
@@ -429,7 +450,8 @@
     copy = pltpu.make_async_copy(matrices_hbm, matrices_ref, arrived)
     copy.start()
     nearby(coarse_solve(halves(ends_ref, C_SECOND, C_SOURCE_2), diagonal_ref[...]), member, rows_ref)
-    fill_slabs(slabs_ref, own_ref, *second_parts(faces_ref, ends_ref))
+    planes = get_planes(ends_ref, C_SECOND)
+    fill_slabs(slabs_ref, own_ref, *second_parts(faces_ref, ends_ref), planes)
     add_prolonged(slabs_ref, lanes_ref, rows_ref)
     slabs = slabs_ref[...]
     field = slabs[1:9, :8].reshape(ROWS, LANES)
@@ -548,6 +570,9 @@
             out_specs=[vmem()] * len(outs),
             scratch_shapes=list(scratch),
             compiler_params=params(),
+            cost_estimate=pl.CostEstimate(
+                flops=2 * 10**9, bytes_accessed=8 * 10**6, transcendentals=0
+            ),
         )
 
     def exchange(pieces, axis):
@@ -555,27 +580,32 @@
         pieces = lax.all_to_all(pieces.reshape(rows[0], 1, LANES), axis, 0, 0, tiled=True)
         return pieces.reshape(rows)
 
-    fixed = [
-        pltpu.with_memory_space_constraint(array, pltpu.HBM)
-        for array in (material_coefficients, side, index, order, matrices, aggregate, diagonal)
-    ]
-    pieces, kappa, smoothed, numbers = call(
+    def ring(planes, step):
+        return lax.ppermute(planes, COARSE, [(i, (i + step) % SIDE) for i in range(SIDE)])
+
+    def pinned(array):
+        return pltpu.with_memory_space_constraint(array, pltpu.HBM)
+
+    matrices = pinned(matrices)
+    copied = pltpu.SemaphoreType.DMA((4,))
+    kappa, numbers, before, after = call(
+        prepare,
+        [local, local, shape(16, LANES), shape(16, LANES)],
+        3,
+        [pltpu.SMEM(material_coefficients.shape, F32), int_cells, int_cells, copied],
+        [hbm()] * 3,
+    )(pinned(material_coefficients), pinned(index), pinned(aggregate))
+    after, before = ring(before, -1), ring(after, 1)
+    pieces, smoothed = call(
         begin,
-        [
-            shape(SIDE * F_FIRST, LANES), local, local, local,
-        ],
-        7,
-        [
-            pltpu.SMEM(material_coefficients.shape, F32), cells, int_cells, int_cells,
-            int_cells, pltpu.VMEM((1, SIDE), F32), cells, cells,
-            held, pltpu.SemaphoreType.DMA((7,)),
-        ],
-        [hbm()] * 7,
-    )(*fixed)
+        [shape(SIDE * F_FIRST, LANES), local],
+        6,
+        [cells, int_cells, held, pltpu.VMEM((1, SIDE), F32), cells, cells, copied],
+        [hbm()] * 4 + [vmem()] * 2,
+    )(pinned(side), pinned(order), matrices, pinned(diagonal), kappa, numbers)
+    pieces, before, after = lax.optimization_barrier((pieces, before, after))
     faces = exchange(pieces, FINE)
-    (pieces,) = call(relay_first, [shape(SIDE * C_FIRST, LANES)], 4)(
-        faces, smoothed, kappa, numbers
-    )
+    (pieces,) = call(relay_first, [shape(SIDE * C_FIRST, LANES)], 2)(faces, smoothed)
     ends = exchange(pieces, COARSE)
     pieces, first, image, smoothed, kappa, lanes, diagonals = call(
         first_image,
@@ -585,9 +615,9 @@
         ],
         11,
         scratch,
-        [vmem()] * 7 + [hbm()],
+        [vmem()] * 9 + [hbm()],
     )(
-        faces, ends, smoothed, kappa, numbers, aggregate, order, fixed[4],
+        faces, ends, before, after, smoothed, kappa, numbers, aggregate, order, matrices,
     )
     faces = exchange(pieces, FINE)
     (pieces,) = call(relay_second, [shape(SIDE * C_SECOND, LANES)], 2)(faces, smoothed)
@@ -600,7 +630,7 @@
         [vmem()] * 11 + [hbm()],
     )(
         faces, ends, smoothed, kappa, lanes, aggregate, order, diagonals, side, first,
-        image, fixed[4],
+        image, matrices,
     )
     pieces = exchange(pieces, (COARSE, FINE))
     results = call(finish, [local, local, local], 9)(

time: 94 us -> 95.9 us (1.020)
  starting transfers between devices: 0 us -> 9.47 us
  blocking collectives: 78.2 us -> 69.7 us
    ppermute x0 -> x2, starting transfers between devices: none -> 9.47 us  [ring(): lax.ppermute(planes, COARSE, [(i, (i + step) % SIDE) for i in range(SIDE)])]
    all_to_all x5, blocking collectives: 78.2 us -> 69.7 us  [exchange(): lax.all_to_all(pieces.reshape(rows[0], 1, LANES), axis, 0, 0, tiled=True)]
    pallas_call x2 -> x3, Pallas kernels: 4.33 us -> 5.11 us  [the longest x1 4.17 us: shards(): call(begin, [shape(SIDE * F_FIRST, LANES), local], 6, [cells, int_cells,...]
  transfers between devices with their start and end apart: 0 -> 2, of which waited for: 0 -> 0; matrix products, arithmetic and copies ran while one was open for 0% -> 0% of each run, Pallas kernels for 0% -> 4%
where the time goes in v4:
time: 95.9 us; the launch traced here: 95.3 us
  blocking collectives  69.7 us (73%)
  Pallas kernels  15.4 us (16%)
  starting transfers between devices  9.47 us (10%)
    all_to_all x5, blocking collectives, exchange(): lax.all_to_all(pieces.reshape(rows[0], 1, LANES), axis, 0, 0, tiled=True)  69.7 us
    ppermute x2, starting transfers between devices, ring(): lax.ppermute(planes, COARSE, [(i, (i + step) % SIDE) for i in range(SIDE)])  9.47 us
    pallas_call x1, Pallas kernels, shards(): call(second_image, [shape(WIDE, LANES), local, local, local], 13, scratch...  4.64 us
    pallas_call x1, Pallas kernels, shards(): call(first_image, [shape(SIDE * F_SECOND, LANES), local, local, local, sh...  4.54 us
    pallas_call x1, Pallas kernels, shards(): call(begin, [shape(SIDE * F_FIRST, LANES), local], 6, [cells, int_cells,...  4.17 us
  transfers between devices with their start and end apart: 2, of which 0 were waited for; matrix products, arithmetic and copies ran while one was open for 0% of the time, Pallas kernels for 4%

profile of v4, /device:TPU:1, one launch (start us, length us, event | category | flops | bytes accessed | tf_op | source)
XLA Modules:
  0.0 95.3 jit_solution(3036398870461793173)
XLA Ops:
  0.6 0.9 shard_map.94
  1.5 2.2 %collective-permute-start = (f32[16,128]{1,0:T(8,128)S(1)}, f32[16,128]{1,0:T(8,128)S(1)}, u32[]{:S(2)}, u32[]{:S(2)}) collective-permute-start(f32[16,128]{1,0:T(8,128)S(1)} %get-tuple-element.29), channel_id=1, source_target_pairs={{0,16},{16,32},{32,48},{48,64},{64,80},{80,96},{96,112},{112,128},... | collective-permute-start | bytes 24584 | tf_op jit(solution)/shard_map/ppermute | solution.py:584
  3.7 7.3 %collective-permute-start.1 = (f32[16,128]{1,0:T(8,128)S(1)}, f32[16,128]{1,0:T(8,128)S(1)}, u32[]{:S(2)}, u32[]{:S(2)}) collective-permute-start(f32[16,128]{1,0:T(8,128)S(1)} %get-tuple-element.30), channel_id=1, source_target_pairs={{0,240},{16,0},{32,16},{48,32},{64,48},{80,64},{96,80},{112,96},{1... | collective-permute-start | bytes 24584 | tf_op jit(solution)/shard_map/ppermute | solution.py:584
  11.0 4.2 %shard_map.95 = (f32[400,128]{1,0:T(8,128)S(1)}, f32[64,128]{1,0:T(8,128)S(1)}) custom-call(f32[64,128]{1,0:T(8,128)} %bitcast.44, s32[64,128]{1,0:T(8,128)} %bitcast.41, f32[64,128,128]{2,1,0:T(8,128)} %bitcast.51, f32[1,16]{1,0:T(1,128)} %bitcast.55, f32[64,128]{1,0:T(8,128)S(1)} %get-tuple-element.26.kappa_ref.own_kappa_ref, ...), custom_call_target="tpu_custom_call" | custom-call | flops 2000000000 | bytes 8000000 | tf_op jit(solution)/shard_map/pallas_call | solution.py:599
  15.1 0.0 copy-start
  15.1 0.0 copy-start.2
  15.2 0.0 collective-permute-done.before_ref
  15.2 0.0 collective-permute-done.1.after_ref
  15.2 12.2 %all_to_all.25 = f32[400,1,128]{2,1,0:T(1,128)S(1)} all-to-all(f32[400,1,128]{2,1,0:T(1,128)S(1)} %bitcast.31), channel_id=1, replica_groups=mesh['coarse'=16,'fine'=16] {'fine'}, dimensions={0} | all-to-all | bytes 409600 | tf_op jit(solution)/shard_map/all_to_all | solution.py:580
  27.4 0.1 shard_map.96
  27.5 14.9 %all_to_all.26 = f32[288,1,128]{2,1,0:T(1,128)S(1)} all-to-all(f32[288,1,128]{2,1,0:T(1,128)S(1)} %bitcast.33), channel_id=1, replica_groups=mesh['coarse'=16,'fine'=16] {'coarse'}, dimensions={0} | all-to-all | bytes 294912 | tf_op jit(solution)/shard_map/all_to_all | solution.py:580
  42.4 0.0 copy-done
  42.4 0.0 copy-done.2
  42.4 4.5 %shard_map.97 = (f32[144,128]{1,0:T(8,128)S(1)}, f32[64,128]{1,0:T(8,128)S(1)}, f32[64,128]{1,0:T(8,128)S(1)}, f32[64,128]{1,0:T(8,128)S(1)}, f32[10,16,128]{2,1...) custom-call(f32[400,128]{1,0:T(8,128)S(1)} %bitcast.30, f32[288,128]{1,0:T(8,128)S(1)} %bitcast.32, ...), custom_call_target="tpu_custom_call" | custom-call | flops 2000000000 | bytes 8000000 | tf_op jit(solution)/shard_map/pallas_call | solution.py:610
  47.0 0.0 copy-start.1
  47.0 10.8 %all_to_all.27 = f32[144,1,128]{2,1,0:T(1,128)S(1)} all-to-all(f32[144,1,128]{2,1,0:T(1,128)S(1)} %bitcast.38), channel_id=1, replica_groups=mesh['coarse'=16,'fine'=16] {'fine'}, dimensions={0} | all-to-all | bytes 147456 | tf_op jit(solution)/shard_map/all_to_all | solution.py:580
  57.8 12.2 %all_to_all.28 = f32[192,1,128]{2,1,0:T(1,128)S(1)} all-to-all(f32[192,1,128]{2,1,0:T(1,128)S(1)} %bitcast.37), channel_id=1, replica_groups=mesh['coarse'=16,'fine'=16] {'coarse'}, dimensions={0} | all-to-all | bytes 196608 | tf_op jit(solution)/shard_map/all_to_all | solution.py:580
  70.0 0.0 copy-done.1
  70.0 4.6 %shard_map.99 = (f32[256,128]{1,0:T(8,128)S(1)}, f32[64,128]{1,0:T(8,128)S(1)}, f32[64,128]{1,0:T(8,128)S(1)}, f32[64,128]{1,0:T(8,128)S(1)}) custom-call(f32[144,128]{1,0:T(8,128)S(1)} %bitcast.40, f32[192,128]{1,0:T(8,128)S(1)} %bitcast.36, f32[64,128]{1,0:T(8,128)S(1)} %get-tuple-element.36.smoothed_ref.own_ref, ...), custom_call_target="tpu_custom_call" | custom-call | flops 2000000000 | bytes 8000000 | tf_op jit(solution)/shard_map/pallas_call | solution.py:625
  74.6 19.6 %all_to_all.29 = f32[256,1,128]{2,1,0:T(1,128)S(1)} all-to-all(f32[256,1,128]{2,1,0:T(1,128)S(1)} %bitcast.35), channel_id=1, replica_groups=mesh['coarse'=16,'fine'=16] {'coarse','fine'}, dimensions={0} | all-to-all | bytes 262144 | tf_op jit(solution)/shard_map/all_to_all | solution.py:580
  94.2 1.1 %shard_map.100 = (f32[64,128]{1,0:T(8,128)}, f32[64,128]{1,0:T(8,128)}, f32[64,128]{1,0:T(8,128)}) custom-call(f32[256,128]{1,0:T(8,128)S(1)} %bitcast.34, f32[16,256]{1,0:T(8,128)S(1)} %get-tuple-element.39.diagonal_ref, s32[64,128]{1,0:T(8,128)S(1)} %bitcast.50, f32[64,128]{1,0:T(8,128)S(1)} %bitcast.46, f32[64,128]{1,0:T(8,128)S(1)} %get-tuple-element.40.first_ref, ...), custom_call_target="tpu_custom_call" | custom-call | flops 2000000000 | bytes 8000000 | tf_op jit(solution)/shard_map/pallas_call | solution.py:636
  (1 shorter events, 0.0 us)
Async XLA Ops:
  1.5 13.7 %collective-permute-start = (f32[16,128]{1,0:T(8,128)S(1)}, f32[16,128]{1,0:T(8,128)S(1)}, u32[]{:S(2)}, u32[]{:S(2)}) collective-permute-start(f32[16,128]{1,0:T(8,128)S(1)} %get-tuple-element.29), channel_id=1, source_target_pairs={{0,16},{16,32},{32,48},{48,64},{64,80},{80,96},{96,112},{112,128},... | collective-permute-start | bytes 24584 | tf_op jit(solution)/shard_map/ppermute | solution.py:584
  3.7 11.5 %collective-permute-start.1 = (f32[16,128]{1,0:T(8,128)S(1)}, f32[16,128]{1,0:T(8,128)S(1)}, u32[]{:S(2)}, u32[]{:S(2)}) collective-permute-start(f32[16,128]{1,0:T(8,128)S(1)} %get-tuple-element.30), channel_id=1, source_target_pairs={{0,240},{16,0},{32,16},{48,32},{64,48},{80,64},{96,80},{112,96},{1... | collective-permute-start | bytes 24584 | tf_op jit(solution)/shard_map/ppermute | solution.py:584
  15.1 27.3 %copy-start = (s32[1,1,64,128]{3,2,1,0:T(8,128)S(1)}, s32[1,1,64,128]{3,2,1,0:T(8,128)}, u32[]{:S(2)}) copy-start(s32[1,1,64,128]{3,2,1,0:T(8,128)} %param.10) | copy-start | bytes 98308
  15.1 27.3 %copy-start.2 = (s32[8,8,128]{2,1,0:T(8,128)S(1)}, s32[8,8,128]{2,1,0:T(8,128)}, u32[]{:S(2)}) copy-start(s32[8,8,128]{2,1,0:T(8,128)} %param.12) | copy-start | bytes 98308
  47.0 23.0 %copy-start.1 = (f32[8,8,128]{2,1,0:T(8,128)S(1)}, f32[8,8,128]{2,1,0:T(8,128)}, u32[]{:S(2)}) copy-start(f32[8,8,128]{2,1,0:T(8,128)} %param.7) | copy-start | bytes 98308

commit v5 on v3

--- a/solution.py
+++ b/solution.py
@@ -106,10 +106,12 @@
         picked_ref[start : start + GROUP, :] = jnp.concatenate(rows, axis=0)
 
 
-def multiply_blocks(matrices_ref, picked_ref, product_ref):
+def multiply_blocks(matrices_ref, picked_ref, product_ref, copies=()):
     wide = (2 * GROUP, GROUP * LANES)
     spread = jnp.where(iota(wide, 0) % GROUP == iota(wide, 1) // LANES, 1.0, 0.0).astype(BF16)
     for start in range(0, ROWS, GROUP):
+        if copies:
+            copies[start // GROUP].wait()
         high, low = split(picked_ref[start : start + GROUP, :])
         both = jnp.concatenate([high.astype(F32), low.astype(F32)], axis=0)
         columns = matmul(jnp.transpose(both).astype(BF16), spread, 1, 0)
@@ -291,14 +293,21 @@
                 (index_hbm, index_ref),
                 (map_hbm, map_ref),
                 (diagonal_hbm, diagonal_ref),
-                (matrices_hbm, matrices_ref),
             )
         )
+    ]
+    copies += [
+        pltpu.make_async_copy(
+            matrices_hbm.at[pl.ds(start, GROUP)],
+            matrices_ref.at[pl.ds(start, GROUP)],
+            arrived.at[6 + start // GROUP],
+        )
+        for start in range(0, ROWS, GROUP)
     ]
     for copy in copies:
         copy.start()
     copies[0].wait()
-    for copy in copies[1:-1]:
+    for copy in copies[1:6]:
         copy.wait()
     index = index_ref[...]
     kappa = jnp.zeros((ROWS, LANES), F32)
@@ -306,8 +315,7 @@
         kappa = jnp.where(index == entry, table_ref[entry], kappa)
     kappa_ref[...] = kappa
     pick(side_ref, order_ref, picked_ref)
-    copies[-1].wait()
-    multiply_blocks(matrices_ref, picked_ref, product_ref)
+    multiply_blocks(matrices_ref, picked_ref, product_ref, copies[6:])
     put_back(product_ref, order_ref, smoothed_ref)
     aggregate = map_ref[...]
     numbers_ref[...] = aggregate.astype(F32)
@@ -422,8 +430,8 @@
 def second_image(
     faces_ref, ends_ref, own_ref, kappa_ref, lanes_ref, map_ref, order_ref,
     diagonal_ref, side_ref, first_ref, image_ref, matrices_hbm,
-    pieces_ref, field_ref, second_ref, smoothed_ref,
-    picked_ref, product_ref, slabs_ref, rows_ref, matrices_ref, arrived,
+    pieces_ref, field_ref, second_ref, product_ref,
+    picked_ref, slabs_ref, rows_ref, matrices_ref, arrived,
 ):
     owner, member = position()
     copy = pltpu.make_async_copy(matrices_hbm, matrices_ref, arrived)
@@ -439,7 +447,6 @@
     pick(second_ref, order_ref, picked_ref)
     copy.wait()
     multiply_blocks(matrices_ref, picked_ref, product_ref)
-    put_back(product_ref, order_ref, smoothed_ref)
     first = first_ref[...]
     image = image_ref[...]
     pairs = (
@@ -448,7 +455,7 @@
         image * field,
         second * first,
         second * field,
-        second * smoothed_ref[...],
+        picked_ref[...] * product_ref[...],
     )
     lane = iota((8, LANES), 1)
     message = restrict(second, offsets(map_ref[...]), member)
@@ -548,6 +555,9 @@
             out_specs=[vmem()] * len(outs),
             scratch_shapes=list(scratch),
             compiler_params=params(),
+            cost_estimate=pl.CostEstimate(
+                flops=10**9, bytes_accessed=4 * 10**6, transcendentals=0
+            ),
         )
 
     def exchange(pieces, axis):
@@ -568,7 +578,7 @@
         [
             pltpu.SMEM(material_coefficients.shape, F32), cells, int_cells, int_cells,
             int_cells, pltpu.VMEM((1, SIDE), F32), cells, cells,
-            held, pltpu.SemaphoreType.DMA((7,)),
+            held, pltpu.SemaphoreType.DMA((6 + ROWS // GROUP,)),
         ],
         [hbm()] * 7,
     )(*fixed)
@@ -592,17 +602,18 @@
     faces = exchange(pieces, FINE)
     (pieces,) = call(relay_second, [shape(SIDE * C_SECOND, LANES)], 2)(faces, smoothed)
     ends = exchange(pieces, COARSE)
-    pieces, field, second, smoothed = call(
+    pieces, field, second, product = call(
         second_image,
         [shape(WIDE, LANES), local, local, local],
         13,
-        scratch,
+        scratch[:1] + scratch[2:],
         [vmem()] * 11 + [hbm()],
     )(
         faces, ends, smoothed, kappa, lanes, aggregate, order, diagonals, side, first,
         image, fixed[4],
     )
     pieces = exchange(pieces, (COARSE, FINE))
+    (smoothed,) = call(put_back, [local], 2)(product, order)
     results = call(finish, [local, local, local], 9)(
         pieces, diagonals, aggregate, side, first, image, field, second, smoothed
     )

time: 94 us -> 95.1 us (1.012)
  blocking collectives: 78.2 us -> 58.6 us
  waiting for transfers between devices: 0 us -> 11.9 us
  starting transfers between devices: 0 us -> 6.95 us
  Pallas kernels: 14.7 us -> 16.6 us
    all_to_all x5 -> x4, blocking collectives: 78.2 us -> 58.6 us  [exchange(): lax.all_to_all(pieces.reshape(rows[0], 1, LANES), axis, 0, 0, tiled=True)]
    all_to_all x0 -> x1, waiting for transfers between devices: none -> 11.9 us  [exchange(): lax.all_to_all(pieces.reshape(rows[0], 1, LANES), axis, 0, 0, tiled=True)]
    all_to_all x0 -> x1, starting transfers between devices: none -> 6.95 us  [exchange(): lax.all_to_all(pieces.reshape(rows[0], 1, LANES), axis, 0, 0, tiled=True)]
    pallas_call x1, Pallas kernels: 4.24 us -> 5.55 us  [shards(): call(begin, [shape(SIDE * F_FIRST, LANES), local, local, local], 7, [pltp...]
    pallas_call x0 -> x1, Pallas kernels: none -> 1.05 us  [shards(): smoothed, = call(put_back, [local], 2)(product, order)]
  transfers between devices with their start and end apart: 0 -> 1, of which waited for: 0 -> 1; matrix products, arithmetic and copies ran while one was open for 0% -> 0% of each run, Pallas kernels for 0% -> 1%
where the time goes in v5:
time: 95.1 us; the launch traced here: 94.8 us
  blocking collectives  58.6 us (62%)
  Pallas kernels  16.6 us (17%)
  waiting for transfers between devices  11.9 us (13%)
  starting transfers between devices  6.95 us (7%)
    all_to_all x4, blocking collectives, exchange(): lax.all_to_all(pieces.reshape(rows[0], 1, LANES), axis, 0, 0, tiled=True)  58.6 us
    all_to_all x1, waiting for transfers between devices, exchange(): lax.all_to_all(pieces.reshape(rows[0], 1, LANES), axis, 0, 0, tiled=True)  11.9 us
    all_to_all x1, starting transfers between devices, exchange(): lax.all_to_all(pieces.reshape(rows[0], 1, LANES), axis, 0, 0, tiled=True)  6.95 us
    pallas_call x1, Pallas kernels, shards(): call(begin, [shape(SIDE * F_FIRST, LANES), local, local, local], 7, [pltp...  5.55 us
    pallas_call x1, Pallas kernels, shards(): call(first_image, [shape(SIDE * F_SECOND, LANES), local, local, local, sh...  4.57 us
    pallas_call x1, Pallas kernels, shards(): call(second_image, [shape(WIDE, LANES), local, local, local], 13, scratch...  4.18 us
  transfers between devices with their start and end apart: 1, of which 1 were waited for; matrix products, arithmetic and copies ran while one was open for 0% of the time, Pallas kernels for 1%

profile of v5, /device:TPU:1, one launch (start us, length us, event | category | flops | bytes accessed | tf_op | source)
XLA Modules:
  0.0 94.8 jit_solution(5661752803258375097)
XLA Ops:
  0.6 0.0 copy-start
  0.6 0.0 copy-start.1
  0.7 5.6 %shard_map.94 = (f32[400,128]{1,0:T(8,128)S(1)}, f32[64,128]{1,0:T(8,128)S(1)}, f32[64,128]{1,0:T(8,128)S(1)}, f32[64,128]{1,0:T(8,128)S(1)}) custom-call(f32[16]{0:T(128)} %table_hbm.1, f32[64,128]{1,0:T(8,128)} %bitcast.45, s32[64,128]{1,0:T(8,128)} %bitcast.54, s32[64,128]{1,0:T(8,128)} %bitcast.33, f32[64,128,128]{2,1,0:T(8,128)} %bitcast.51, ...), custom_call_target="tpu_custom_call" | custom-call | flops 1000000000 | bytes 4000000 | tf_op jit(solution)/shard_map/pallas_call | solution.py:572
  6.2 13.7 %all_to_all.25 = f32[400,1,128]{2,1,0:T(1,128)S(1)} all-to-all(f32[400,1,128]{2,1,0:T(1,128)S(1)} %bitcast.44), channel_id=1, replica_groups=mesh['coarse'=16,'fine'=16] {'fine'}, dimensions={0} | all-to-all | bytes 409600 | tf_op jit(solution)/shard_map/all_to_all | solution.py:565
  19.9 0.1 shard_map.95
  20.0 20.2 %all_to_all.26 = f32[544,1,128]{2,1,0:T(1,128)S(1)} all-to-all(f32[544,1,128]{2,1,0:T(1,128)S(1)} %bitcast.43), channel_id=1, replica_groups=mesh['coarse'=16,'fine'=16] {'coarse'}, dimensions={0} | all-to-all | bytes 557056 | tf_op jit(solution)/shard_map/all_to_all | solution.py:565
  40.2 0.0 copy-done
  40.2 0.0 copy-done.1
  40.2 0.0 copy-start.2
  40.2 4.6 %shard_map.96 = (f32[144,128]{1,0:T(8,128)S(1)}, f32[64,128]{1,0:T(8,128)S(1)}, f32[64,128]{1,0:T(8,128)S(1)}, f32[64,128]{1,0:T(8,128)S(1)}, f32[10,16,128]{2,1...) custom-call(f32[400,128]{1,0:T(8,128)S(1)} %bitcast.31, f32[544,128]{1,0:T(8,128)S(1)} %bitcast.29, ...), custom_call_target="tpu_custom_call" | custom-call | flops 1000000000 | bytes 4000000 | tf_op jit(solution)/shard_map/pallas_call | solution.py:590
  44.8 11.8 %all_to_all.27 = f32[144,1,128]{2,1,0:T(1,128)S(1)} all-to-all(f32[144,1,128]{2,1,0:T(1,128)S(1)} %bitcast.50), channel_id=1, replica_groups=mesh['coarse'=16,'fine'=16] {'fine'}, dimensions={0} | all-to-all | bytes 147456 | tf_op jit(solution)/shard_map/all_to_all | solution.py:565
  56.6 12.9 %all_to_all.28 = f32[192,1,128]{2,1,0:T(1,128)S(1)} all-to-all(f32[192,1,128]{2,1,0:T(1,128)S(1)} %bitcast.49), channel_id=1, replica_groups=mesh['coarse'=16,'fine'=16] {'coarse'}, dimensions={0} | all-to-all | bytes 196608 | tf_op jit(solution)/shard_map/all_to_all | solution.py:565
  69.6 0.0 copy-done.2
  69.6 4.2 %shard_map.98 = (f32[256,128]{1,0:T(8,128)}, f32[64,128]{1,0:T(8,128)S(1)}, f32[64,128]{1,0:T(8,128)S(1)}, f32[64,128]{1,0:T(8,128)S(1)}) custom-call(f32[144,128]{1,0:T(8,128)S(1)} %bitcast.42, f32[192,128]{1,0:T(8,128)S(1)} %bitcast.32, f32[64,128]{1,0:T(8,128)S(1)} %get-tuple-element.26.smoothed_ref.own_ref, ...), custom_call_target="tpu_custom_call" | custom-call | flops 1000000000 | bytes 4000000 | tf_op jit(solution)/shard_map/pallas_call | solution.py:605
  73.8 6.9 %all-to-all-start.4 = ((f32[256,1,128]{2,1,0:T(1,128)}), f32[256,1,128]{2,1,0:T(1,128)S(1)}, u32[]{:S(2)}, u32[]{:S(2)}) async-start(f32[256,1,128]{2,1,0:T(1,128)} %bitcast.19), calls=%async_computation.4 | async-start | bytes 262144 | tf_op jit(solution)/shard_map/all_to_all | solution.py:565
  80.7 1.1 %shard_map.99.smoothed_ref = f32[64,128]{1,0:T(8,128)S(1)} custom-call(f32[64,128]{1,0:T(8,128)S(1)} %get-tuple-element.35.product_ref, s32[64,128]{1,0:T(8,128)S(1)} %bitcast.36), custom_call_target="tpu_custom_call" | custom-call | flops 1000000000 | bytes 4000000 | tf_op jit(solution)/shard_map/pallas_call | solution.py:616
  81.8 11.9 %all-to-all-done.4 = f32[256,1,128]{2,1,0:T(1,128)S(1)} async-done(((f32[256,1,128]{2,1,0:T(1,128)}), f32[256,1,128]{2,1,0:T(1,128)S(1)}, u32[]{:S(2)}, u32[]{:S(2)}) %all-to-all-start.4) | async-done | bytes 131104 | tf_op jit(solution)/shard_map/all_to_all | solution.py:565
  93.7 1.1 %shard_map.100 = (f32[64,128]{1,0:T(8,128)}, f32[64,128]{1,0:T(8,128)}, f32[64,128]{1,0:T(8,128)}) custom-call(f32[256,128]{1,0:T(8,128)S(1)} %bitcast.48, f32[16,256]{1,0:T(8,128)S(1)} %get-tuple-element.29.diagonal_ref, s32[64,128]{1,0:T(8,128)S(1)} %bitcast.40, f32[64,128]{1,0:T(8,128)S(1)} %bitcast.47, f32[64,128]{1,0:T(8,128)S(1)} %get-tuple-element.30.first_ref, ...), custom_call_target="tpu_custom_call" | custom-call | flops 1000000000 | bytes 4000000 | tf_op jit(solution)/shard_map/pallas_call | solution.py:617
  (1 shorter events, 0.0 us)
Async XLA Ops:
  0.6 39.6 %copy-start = (s32[1,1,64,128]{3,2,1,0:T(8,128)S(1)}, s32[1,1,64,128]{3,2,1,0:T(8,128)}, u32[]{:S(2)}) copy-start(s32[1,1,64,128]{3,2,1,0:T(8,128)} %param.10) | copy-start | bytes 98308
  0.6 39.6 %copy-start.1 = (s32[8,8,128]{2,1,0:T(8,128)S(1)}, s32[8,8,128]{2,1,0:T(8,128)}, u32[]{:S(2)}) copy-start(s32[8,8,128]{2,1,0:T(8,128)} %param.12) | copy-start | bytes 98308
  40.2 29.4 %copy-start.2 = (f32[8,8,128]{2,1,0:T(8,128)S(1)}, f32[8,8,128]{2,1,0:T(8,128)}, u32[]{:S(2)}) copy-start(f32[8,8,128]{2,1,0:T(8,128)} %param.7) | copy-start | bytes 98308
  73.8 19.9 %all-to-all-start.4 = ((f32[256,1,128]{2,1,0:T(1,128)}), f32[256,1,128]{2,1,0:T(1,128)S(1)}, u32[]{:S(2)}, u32[]{:S(2)}) async-start(f32[256,1,128]{2,1,0:T(1,128)} %bitcast.19), calls=%async_computation.4 | async-start | bytes 262144 | tf_op jit(solution)/shard_map/all_to_all | solution.py:565

commit v6 on v3

--- a/solution.py
+++ b/solution.py
@@ -403,8 +403,8 @@
     field = slabs_ref[...]
     field_ref[...] = field[1:9, :8].reshape(ROWS, LANES)
     image_ref[...] = operate(field, kappa_ref[...]).reshape(ROWS, LANES)
+    copy.wait()
     pick(image_ref, order_ref, picked_ref)
-    copy.wait()
     multiply_blocks(matrices_ref, picked_ref, product_ref)
     put_back(product_ref, order_ref, smoothed_ref)
     source = restrict(image_ref[...], offsets(map_ref[...]), member)
@@ -422,8 +422,8 @@
 def second_image(
     faces_ref, ends_ref, own_ref, kappa_ref, lanes_ref, map_ref, order_ref,
     diagonal_ref, side_ref, first_ref, image_ref, matrices_hbm,
-    pieces_ref, field_ref, second_ref, smoothed_ref,
-    picked_ref, product_ref, slabs_ref, rows_ref, matrices_ref, arrived,
+    pieces_ref, field_ref, second_ref, product_ref,
+    picked_ref, slabs_ref, rows_ref, matrices_ref, arrived,
 ):
     owner, member = position()
     copy = pltpu.make_async_copy(matrices_hbm, matrices_ref, arrived)
@@ -436,10 +436,9 @@
     field_ref[...] = field
     second = operate(slabs, kappa_ref[...]).reshape(ROWS, LANES)
     second_ref[...] = second
+    copy.wait()
     pick(second_ref, order_ref, picked_ref)
-    copy.wait()
     multiply_blocks(matrices_ref, picked_ref, product_ref)
-    put_back(product_ref, order_ref, smoothed_ref)
     first = first_ref[...]
     image = image_ref[...]
     pairs = (
@@ -448,7 +447,7 @@
         image * field,
         second * first,
         second * field,
-        second * smoothed_ref[...],
+        picked_ref[...] * product_ref[...],
     )
     lane = iota((8, LANES), 1)
     message = restrict(second, offsets(map_ref[...]), member)
@@ -548,6 +547,9 @@
             out_specs=[vmem()] * len(outs),
             scratch_shapes=list(scratch),
             compiler_params=params(),
+            cost_estimate=pl.CostEstimate(
+                flops=10**9, bytes_accessed=4 * 10**6, transcendentals=0
+            ),
         )
 
     def exchange(pieces, axis):
@@ -592,17 +594,18 @@
     faces = exchange(pieces, FINE)
     (pieces,) = call(relay_second, [shape(SIDE * C_SECOND, LANES)], 2)(faces, smoothed)
     ends = exchange(pieces, COARSE)
-    pieces, field, second, smoothed = call(
+    pieces, field, second, product = call(
         second_image,
         [shape(WIDE, LANES), local, local, local],
         13,
-        scratch,
+        scratch[:1] + scratch[2:],
         [vmem()] * 11 + [hbm()],
     )(
         faces, ends, smoothed, kappa, lanes, aggregate, order, diagonals, side, first,
         image, fixed[4],
     )
     pieces = exchange(pieces, (COARSE, FINE))
+    (smoothed,) = call(put_back, [local], 2)(product, order)
     results = call(finish, [local, local, local], 9)(
         pieces, diagonals, aggregate, side, first, image, field, second, smoothed
     )

time: 94 us -> 95.5 us (1.016)
  blocking collectives: 78.2 us -> 58.6 us
  waiting for transfers between devices: 0 us -> 11.9 us
  starting transfers between devices: 0 us -> 6.95 us
  Pallas kernels: 14.7 us -> 17 us
    all_to_all x5 -> x4, blocking collectives: 78.2 us -> 58.6 us  [exchange(): lax.all_to_all(pieces.reshape(rows[0], 1, LANES), axis, 0, 0, tiled=True)]
    all_to_all x0 -> x1, waiting for transfers between devices: none -> 11.9 us  [exchange(): lax.all_to_all(pieces.reshape(rows[0], 1, LANES), axis, 0, 0, tiled=True)]
    all_to_all x0 -> x1, starting transfers between devices: none -> 6.95 us  [exchange(): lax.all_to_all(pieces.reshape(rows[0], 1, LANES), axis, 0, 0, tiled=True)]
    pallas_call x0 -> x1, Pallas kernels: none -> 1.05 us  [shards(): smoothed, = call(put_back, [local], 2)(product, order)]
  transfers between devices with their start and end apart: 0 -> 1, of which waited for: 0 -> 1; matrix products, arithmetic and copies ran while one was open for 0% -> 0% of each run, Pallas kernels for 0% -> 1%
where the time goes in v6:
time: 95.5 us; the launch traced here: 95.2 us
  blocking collectives  58.6 us (61%)
  Pallas kernels  17 us (18%)
  waiting for transfers between devices  11.9 us (12%)
  starting transfers between devices  6.95 us (7%)
    all_to_all x4, blocking collectives, exchange(): lax.all_to_all(pieces.reshape(rows[0], 1, LANES), axis, 0, 0, tiled=True)  58.6 us
    all_to_all x1, waiting for transfers between devices, exchange(): lax.all_to_all(pieces.reshape(rows[0], 1, LANES), axis, 0, 0, tiled=True)  11.9 us
    all_to_all x1, starting transfers between devices, exchange(): lax.all_to_all(pieces.reshape(rows[0], 1, LANES), axis, 0, 0, tiled=True)  6.95 us
    pallas_call x1, Pallas kernels, shards(): call(second_image, [shape(WIDE, LANES), local, local, local], 13, scratch...  5.24 us
    pallas_call x1, Pallas kernels, shards(): call(first_image, [shape(SIDE * F_SECOND, LANES), local, local, local, sh...  5.22 us
    pallas_call x1, Pallas kernels, shards(): call(begin, [shape(SIDE * F_FIRST, LANES), local, local, local], 7, [pltp...  4.24 us
  transfers between devices with their start and end apart: 1, of which 1 were waited for; matrix products, arithmetic and copies ran while one was open for 0% of the time, Pallas kernels for 1%

profile of v6, /device:TPU:1, one launch (start us, length us, event | category | flops | bytes accessed | tf_op | source)
XLA Modules:
  0.0 95.2 jit_solution(16448847212669869402)
XLA Ops:
  0.6 0.0 copy-start
  0.6 0.0 copy-start.1
  0.7 4.2 %shard_map.94 = (f32[400,128]{1,0:T(8,128)S(1)}, f32[64,128]{1,0:T(8,128)S(1)}, f32[64,128]{1,0:T(8,128)S(1)}, f32[64,128]{1,0:T(8,128)S(1)}) custom-call(f32[16]{0:T(128)} %table_hbm.1, f32[64,128]{1,0:T(8,128)} %bitcast.45, s32[64,128]{1,0:T(8,128)} %bitcast.54, s32[64,128]{1,0:T(8,128)} %bitcast.33, f32[64,128,128]{2,1,0:T(8,128)} %bitcast.51, ...), custom_call_target="tpu_custom_call" | custom-call | flops 1000000000 | bytes 4000000 | tf_op jit(solution)/shard_map/pallas_call | solution.py:564
  4.9 13.7 %all_to_all.25 = f32[400,1,128]{2,1,0:T(1,128)S(1)} all-to-all(f32[400,1,128]{2,1,0:T(1,128)S(1)} %bitcast.44), channel_id=1, replica_groups=mesh['coarse'=16,'fine'=16] {'fine'}, dimensions={0} | all-to-all | bytes 409600 | tf_op jit(solution)/shard_map/all_to_all | solution.py:557
  18.6 0.1 shard_map.95
  18.7 20.2 %all_to_all.26 = f32[544,1,128]{2,1,0:T(1,128)S(1)} all-to-all(f32[544,1,128]{2,1,0:T(1,128)S(1)} %bitcast.43), channel_id=1, replica_groups=mesh['coarse'=16,'fine'=16] {'coarse'}, dimensions={0} | all-to-all | bytes 557056 | tf_op jit(solution)/shard_map/all_to_all | solution.py:557
  38.9 0.0 copy-done
  38.9 0.0 copy-done.1
  38.9 0.0 copy-start.2
  38.9 5.2 %shard_map.96 = (f32[144,128]{1,0:T(8,128)S(1)}, f32[64,128]{1,0:T(8,128)S(1)}, f32[64,128]{1,0:T(8,128)S(1)}, f32[64,128]{1,0:T(8,128)S(1)}, f32[10,16,128]{2,1...) custom-call(f32[400,128]{1,0:T(8,128)S(1)} %bitcast.31, f32[544,128]{1,0:T(8,128)S(1)} %bitcast.29, ...), custom_call_target="tpu_custom_call" | custom-call | flops 1000000000 | bytes 4000000 | tf_op jit(solution)/shard_map/pallas_call | solution.py:582
  44.1 11.8 %all_to_all.27 = f32[144,1,128]{2,1,0:T(1,128)S(1)} all-to-all(f32[144,1,128]{2,1,0:T(1,128)S(1)} %bitcast.50), channel_id=1, replica_groups=mesh['coarse'=16,'fine'=16] {'fine'}, dimensions={0} | all-to-all | bytes 147456 | tf_op jit(solution)/shard_map/all_to_all | solution.py:557
  56.0 12.9 %all_to_all.28 = f32[192,1,128]{2,1,0:T(1,128)S(1)} all-to-all(f32[192,1,128]{2,1,0:T(1,128)S(1)} %bitcast.49), channel_id=1, replica_groups=mesh['coarse'=16,'fine'=16] {'coarse'}, dimensions={0} | all-to-all | bytes 196608 | tf_op jit(solution)/shard_map/all_to_all | solution.py:557
  68.9 0.0 copy-done.2
  68.9 5.2 %shard_map.98 = (f32[256,128]{1,0:T(8,128)}, f32[64,128]{1,0:T(8,128)S(1)}, f32[64,128]{1,0:T(8,128)S(1)}, f32[64,128]{1,0:T(8,128)S(1)}) custom-call(f32[144,128]{1,0:T(8,128)S(1)} %bitcast.42, f32[192,128]{1,0:T(8,128)S(1)} %bitcast.32, f32[64,128]{1,0:T(8,128)S(1)} %get-tuple-element.26.smoothed_ref.own_ref, ...), custom_call_target="tpu_custom_call" | custom-call | flops 1000000000 | bytes 4000000 | tf_op jit(solution)/shard_map/pallas_call | solution.py:597
  74.2 7.0 %all-to-all-start.4 = ((f32[256,1,128]{2,1,0:T(1,128)}), f32[256,1,128]{2,1,0:T(1,128)S(1)}, u32[]{:S(2)}, u32[]{:S(2)}) async-start(f32[256,1,128]{2,1,0:T(1,128)} %bitcast.19), calls=%async_computation.4 | async-start | bytes 262144 | tf_op jit(solution)/shard_map/all_to_all | solution.py:557
  81.1 1.0 %shard_map.99.smoothed_ref = f32[64,128]{1,0:T(8,128)S(1)} custom-call(f32[64,128]{1,0:T(8,128)S(1)} %get-tuple-element.35.product_ref, s32[64,128]{1,0:T(8,128)S(1)} %bitcast.36), custom_call_target="tpu_custom_call" | custom-call | flops 1000000000 | bytes 4000000 | tf_op jit(solution)/shard_map/pallas_call | solution.py:608
  82.2 11.9 %all-to-all-done.4 = f32[256,1,128]{2,1,0:T(1,128)S(1)} async-done(((f32[256,1,128]{2,1,0:T(1,128)}), f32[256,1,128]{2,1,0:T(1,128)S(1)}, u32[]{:S(2)}, u32[]{:S(2)}) %all-to-all-start.4) | async-done | bytes 131104 | tf_op jit(solution)/shard_map/all_to_all | solution.py:557
  94.1 1.1 %shard_map.100 = (f32[64,128]{1,0:T(8,128)}, f32[64,128]{1,0:T(8,128)}, f32[64,128]{1,0:T(8,128)}) custom-call(f32[256,128]{1,0:T(8,128)S(1)} %bitcast.48, f32[16,256]{1,0:T(8,128)S(1)} %get-tuple-element.29.diagonal_ref, s32[64,128]{1,0:T(8,128)S(1)} %bitcast.40, f32[64,128]{1,0:T(8,128)S(1)} %bitcast.47, f32[64,128]{1,0:T(8,128)S(1)} %get-tuple-element.30.first_ref, ...), custom_call_target="tpu_custom_call" | custom-call | flops 1000000000 | bytes 4000000 | tf_op jit(solution)/shard_map/pallas_call | solution.py:609
  (1 shorter events, 0.0 us)
Async XLA Ops:
  0.6 38.2 %copy-start = (s32[1,1,64,128]{3,2,1,0:T(8,128)S(1)}, s32[1,1,64,128]{3,2,1,0:T(8,128)}, u32[]{:S(2)}) copy-start(s32[1,1,64,128]{3,2,1,0:T(8,128)} %param.10) | copy-start | bytes 98308
  0.6 38.2 %copy-start.1 = (s32[8,8,128]{2,1,0:T(8,128)S(1)}, s32[8,8,128]{2,1,0:T(8,128)}, u32[]{:S(2)}) copy-start(s32[8,8,128]{2,1,0:T(8,128)} %param.12) | copy-start | bytes 98308
  38.9 30.0 %copy-start.2 = (f32[8,8,128]{2,1,0:T(8,128)S(1)}, f32[8,8,128]{2,1,0:T(8,128)}, u32[]{:S(2)}) copy-start(f32[8,8,128]{2,1,0:T(8,128)} %param.7) | copy-start | bytes 98308
  74.2 19.9 %all-to-all-start.4 = ((f32[256,1,128]{2,1,0:T(1,128)}), f32[256,1,128]{2,1,0:T(1,128)S(1)}, u32[]{:S(2)}, u32[]{:S(2)}) async-start(f32[256,1,128]{2,1,0:T(1,128)} %bitcast.19), calls=%async_computation.4 | async-start | bytes 262144 | tf_op jit(solution)/shard_map/all_to_all | solution.py:557

commit v7 on v6

--- a/solution.py
+++ b/solution.py
@@ -276,9 +276,9 @@
 
 def begin(
     table_hbm, side_hbm, index_hbm, order_hbm, matrices_hbm, map_hbm, diagonal_hbm,
-    pieces_ref, kappa_ref, smoothed_ref, numbers_ref,
+    pieces_ref, kappa_ref, smoothed_ref, numbers_ref, matrices_ref,
     table_ref, side_ref, index_ref, order_ref, map_ref, diagonal_ref, picked_ref, product_ref,
-    matrices_ref, arrived,
+    arrived,
 ):
     owner, member = position()
     copies = [
@@ -381,13 +381,11 @@
 
 def first_image(
     faces_ref, ends_ref, own_ref, own_kappa_ref, numbers_ref, map_ref, order_ref,
-    matrices_hbm,
+    matrices_ref,
     pieces_ref, field_ref, image_ref, smoothed_ref, kappa_ref, lanes_ref, diagonal_ref,
-    picked_ref, product_ref, slabs_ref, rows_ref, matrices_ref, arrived,
+    picked_ref, product_ref, slabs_ref, rows_ref,
 ):
     owner, member = position()
-    copy = pltpu.make_async_copy(matrices_hbm, matrices_ref, arrived)
-    copy.start()
     diagonal = halves(ends_ref, C_FIRST, C_DIAGONAL)
     diagonal_ref[...] = diagonal
     nearby(coarse_solve(halves(ends_ref, C_FIRST, C_SOURCE), diagonal), member, rows_ref)
@@ -403,7 +401,6 @@
     field = slabs_ref[...]
     field_ref[...] = field[1:9, :8].reshape(ROWS, LANES)
     image_ref[...] = operate(field, kappa_ref[...]).reshape(ROWS, LANES)
-    copy.wait()
     pick(image_ref, order_ref, picked_ref)
     multiply_blocks(matrices_ref, picked_ref, product_ref)
     put_back(product_ref, order_ref, smoothed_ref)
@@ -421,13 +418,11 @@
 
 def second_image(
     faces_ref, ends_ref, own_ref, kappa_ref, lanes_ref, map_ref, order_ref,
-    diagonal_ref, side_ref, first_ref, image_ref, matrices_hbm,
+    diagonal_ref, side_ref, first_ref, image_ref, matrices_ref,
     pieces_ref, field_ref, second_ref, product_ref,
-    picked_ref, slabs_ref, rows_ref, matrices_ref, arrived,
+    picked_ref, slabs_ref, rows_ref,
 ):
     owner, member = position()
-    copy = pltpu.make_async_copy(matrices_hbm, matrices_ref, arrived)
-    copy.start()
     nearby(coarse_solve(halves(ends_ref, C_SECOND, C_SOURCE_2), diagonal_ref[...]), member, rows_ref)
     fill_slabs(slabs_ref, own_ref, *second_parts(faces_ref, ends_ref))
     add_prolonged(slabs_ref, lanes_ref, rows_ref)
@@ -436,7 +431,6 @@
     field_ref[...] = field
     second = operate(slabs, kappa_ref[...]).reshape(ROWS, LANES)
     second_ref[...] = second
-    copy.wait()
     pick(second_ref, order_ref, picked_ref)
     multiply_blocks(matrices_ref, picked_ref, product_ref)
     first = first_ref[...]
@@ -533,10 +527,8 @@
     local = shape(ROWS, LANES)
     cells = pltpu.VMEM((ROWS, LANES), F32)
     int_cells = pltpu.VMEM((ROWS, LANES), jnp.int32)
-    held = pltpu.VMEM(matrices.shape, F32)
     scratch = [
         cells, cells, pltpu.VMEM((10, SLAB, LANES), F32), pltpu.VMEM((SIDE, LANES), F32),
-        held, pltpu.SemaphoreType.DMA,
     ]
 
     def call(kernel, outs, ins, scratch=(), specs=None):
@@ -561,19 +553,20 @@
         pltpu.with_memory_space_constraint(array, pltpu.HBM)
         for array in (material_coefficients, side, index, order, matrices, aggregate, diagonal)
     ]
-    pieces, kappa, smoothed, numbers = call(
+    pieces, kappa, smoothed, numbers, matrices = call(
         begin,
         [
-            shape(SIDE * F_FIRST, LANES), local, local, local,
+            shape(SIDE * F_FIRST, LANES), local, local, local, pltpu.VMEM(matrices.shape, F32),
         ],
         7,
         [
             pltpu.SMEM(material_coefficients.shape, F32), cells, int_cells, int_cells,
             int_cells, pltpu.VMEM((1, SIDE), F32), cells, cells,
-            held, pltpu.SemaphoreType.DMA((7,)),
+            pltpu.SemaphoreType.DMA((7,)),
         ],
         [hbm()] * 7,
     )(*fixed)
+    matrices = pltpu.with_memory_space_constraint(matrices, pltpu.VMEM)
     faces = exchange(pieces, FINE)
     (pieces,) = call(relay_first, [shape(SIDE * C_FIRST, LANES)], 4)(
         faces, smoothed, kappa, numbers
@@ -585,11 +578,10 @@
             shape(SIDE * F_SECOND, LANES), local, local, local, shape(10, SLAB, LANES),
             shape(10, SLAB, LANES, dtype=jnp.int32), shape(SIDE, WIDE),
         ],
-        11,
+        8,
         scratch,
-        [vmem()] * 7 + [hbm()],
     )(
-        faces, ends, smoothed, kappa, numbers, aggregate, order, fixed[4],
+        faces, ends, smoothed, kappa, numbers, aggregate, order, matrices,
     )
     faces = exchange(pieces, FINE)
     (pieces,) = call(relay_second, [shape(SIDE * C_SECOND, LANES)], 2)(faces, smoothed)
@@ -597,12 +589,11 @@
     pieces, field, second, product = call(
         second_image,
         [shape(WIDE, LANES), local, local, local],
-        13,
+        12,
         scratch[:1] + scratch[2:],
-        [vmem()] * 11 + [hbm()],
     )(
         faces, ends, smoothed, kappa, lanes, aggregate, order, diagonals, side, first,
-        image, fixed[4],
+        image, matrices,
     )
     pieces = exchange(pieces, (COARSE, FINE))
     (smoothed,) = call(put_back, [local], 2)(product, order)

time: 95.5 us -> 91.4 us (0.957)
  Pallas kernels: 17 us -> 13 us
    pallas_call x1, Pallas kernels: 5.22 us -> 3.22 us  [shards(): call(first_image, [shape(SIDE * F_SECOND, LANES), local, local, local, sh...]
    pallas_call x2, Pallas kernels: 9.48 us -> 7.48 us  [the longest x1 4.24 us: shards(): call(begin, [shape(SIDE * F_FIRST, LANES), local, local, local, pltpu.VME...]
where the time goes in v7:
time: 91.4 us; the launch traced here: 91.1 us
  blocking collectives  58.6 us (64%)
  Pallas kernels  13 us (14%)
  waiting for transfers between devices  11.9 us (13%)
  starting transfers between devices  6.94 us (8%)
    all_to_all x4, blocking collectives, exchange(): lax.all_to_all(pieces.reshape(rows[0], 1, LANES), axis, 0, 0, tiled=True)  58.6 us
    all_to_all x1, waiting for transfers between devices, exchange(): lax.all_to_all(pieces.reshape(rows[0], 1, LANES), axis, 0, 0, tiled=True)  11.9 us
    all_to_all x1, starting transfers between devices, exchange(): lax.all_to_all(pieces.reshape(rows[0], 1, LANES), axis, 0, 0, tiled=True)  6.94 us
    pallas_call x1, Pallas kernels, shards(): call(begin, [shape(SIDE * F_FIRST, LANES), local, local, local, pltpu.VME...  4.24 us
    pallas_call x1, Pallas kernels, shards(): call(second_image, [shape(WIDE, LANES), local, local, local], 12, scratch...  3.25 us
    pallas_call x1, Pallas kernels, shards(): call(first_image, [shape(SIDE * F_SECOND, LANES), local, local, local, sh...  3.22 us
  transfers between devices with their start and end apart: 1, of which 1 were waited for; matrix products, arithmetic and copies ran while one was open for 0% of the time, Pallas kernels for 1%

profile of v7, /device:TPU:1, one launch (start us, length us, event | category | flops | bytes accessed | tf_op | source)
XLA Modules:
  0.0 91.1 jit_solution(8420301397923257889)
XLA Ops:
  0.6 0.0 copy-start
  0.6 0.0 copy-start.1
  0.7 4.2 %shard_map.94 = (f32[400,128]{1,0:T(8,128)S(1)}, f32[64,128]{1,0:T(8,128)S(1)}, f32[64,128]{1,0:T(8,128)S(1)}, f32[64,128]{1,0:T(8,128)S(1)}, f32[64,128,128]{2,1,0:T(8,128)S(1)}) custom-call(f32[16]{0:T(128)} %table_hbm.1, f32[64,128]{1,0:T(8,128)} %bitcast.45, s32[64,128]{1,0:T(8,128)} %bitcast.52, s32[64,128]{1,0:T(8,128)} %bitcast.33, ...), custom_call_target="tpu_custom_call" | custom-call | flops 1000000000 | bytes 4000000 | tf_op jit(solution)/shard_map/pallas_call | solution.py:556
  4.9 13.7 %all_to_all.25 = f32[400,1,128]{2,1,0:T(1,128)S(1)} all-to-all(f32[400,1,128]{2,1,0:T(1,128)S(1)} %bitcast.44), channel_id=1, replica_groups=mesh['coarse'=16,'fine'=16] {'fine'}, dimensions={0} | all-to-all | bytes 409600 | tf_op jit(solution)/shard_map/all_to_all | solution.py:549
  18.6 0.1 shard_map.95
  18.7 20.2 %all_to_all.26 = f32[544,1,128]{2,1,0:T(1,128)S(1)} all-to-all(f32[544,1,128]{2,1,0:T(1,128)S(1)} %bitcast.43), channel_id=1, replica_groups=mesh['coarse'=16,'fine'=16] {'coarse'}, dimensions={0} | all-to-all | bytes 557056 | tf_op jit(solution)/shard_map/all_to_all | solution.py:549
  38.9 0.0 copy-done
  38.9 0.0 copy-done.1
  38.9 0.0 copy-start.2
  38.9 3.2 %shard_map.96 = (f32[144,128]{1,0:T(8,128)S(1)}, f32[64,128]{1,0:T(8,128)S(1)}, f32[64,128]{1,0:T(8,128)S(1)}, f32[64,128]{1,0:T(8,128)S(1)}, f32[10,16,128]{2,1...) custom-call(f32[400,128]{1,0:T(8,128)S(1)} %bitcast.31, f32[544,128]{1,0:T(8,128)S(1)} %bitcast.29, ...), custom_call_target="tpu_custom_call" | custom-call | flops 1000000000 | bytes 4000000 | tf_op jit(solution)/shard_map/pallas_call | solution.py:575
  42.1 11.8 %all_to_all.27 = f32[144,1,128]{2,1,0:T(1,128)S(1)} all-to-all(f32[144,1,128]{2,1,0:T(1,128)S(1)} %bitcast.50), channel_id=1, replica_groups=mesh['coarse'=16,'fine'=16] {'fine'}, dimensions={0} | all-to-all | bytes 147456 | tf_op jit(solution)/shard_map/all_to_all | solution.py:549
  54.0 12.9 %all_to_all.28 = f32[192,1,128]{2,1,0:T(1,128)S(1)} all-to-all(f32[192,1,128]{2,1,0:T(1,128)S(1)} %bitcast.49), channel_id=1, replica_groups=mesh['coarse'=16,'fine'=16] {'coarse'}, dimensions={0} | all-to-all | bytes 196608 | tf_op jit(solution)/shard_map/all_to_all | solution.py:549
  66.9 0.0 copy-done.2
  66.9 3.2 %shard_map.98 = (f32[256,128]{1,0:T(8,128)}, f32[64,128]{1,0:T(8,128)S(1)}, f32[64,128]{1,0:T(8,128)S(1)}, f32[64,128]{1,0:T(8,128)S(1)}) custom-call(f32[144,128]{1,0:T(8,128)S(1)} %bitcast.42, f32[192,128]{1,0:T(8,128)S(1)} %bitcast.32, f32[64,128]{1,0:T(8,128)S(1)} %get-tuple-element.28.smoothed_ref.own_ref, ...), custom_call_target="tpu_custom_call" | custom-call | flops 1000000000 | bytes 4000000 | tf_op jit(solution)/shard_map/pallas_call | solution.py:589
  70.1 6.9 %all-to-all-start.4 = ((f32[256,1,128]{2,1,0:T(1,128)}), f32[256,1,128]{2,1,0:T(1,128)S(1)}, u32[]{:S(2)}, u32[]{:S(2)}) async-start(f32[256,1,128]{2,1,0:T(1,128)} %bitcast.19), calls=%async_computation.4 | async-start | bytes 262144 | tf_op jit(solution)/shard_map/all_to_all | solution.py:549
  77.1 1.1 %shard_map.99.smoothed_ref = f32[64,128]{1,0:T(8,128)S(1)} custom-call(f32[64,128]{1,0:T(8,128)S(1)} %get-tuple-element.37.product_ref, s32[64,128]{1,0:T(8,128)S(1)} %bitcast.36), custom_call_target="tpu_custom_call" | custom-call | flops 1000000000 | bytes 4000000 | tf_op jit(solution)/shard_map/pallas_call | solution.py:599
  78.2 11.9 %all-to-all-done.4 = f32[256,1,128]{2,1,0:T(1,128)S(1)} async-done(((f32[256,1,128]{2,1,0:T(1,128)}), f32[256,1,128]{2,1,0:T(1,128)S(1)}, u32[]{:S(2)}, u32[]{:S(2)}) %all-to-all-start.4) | async-done | bytes 131104 | tf_op jit(solution)/shard_map/all_to_all | solution.py:549
  90.0 1.1 %shard_map.100 = (f32[64,128]{1,0:T(8,128)}, f32[64,128]{1,0:T(8,128)}, f32[64,128]{1,0:T(8,128)}) custom-call(f32[256,128]{1,0:T(8,128)S(1)} %bitcast.48, f32[16,256]{1,0:T(8,128)S(1)} %get-tuple-element.31.diagonal_ref, s32[64,128]{1,0:T(8,128)S(1)} %bitcast.40, f32[64,128]{1,0:T(8,128)S(1)} %bitcast.47, f32[64,128]{1,0:T(8,128)S(1)} %get-tuple-element.32.first_ref, ...), custom_call_target="tpu_custom_call" | custom-call | flops 1000000000 | bytes 4000000 | tf_op jit(solution)/shard_map/pallas_call | solution.py:600
  (1 shorter events, 0.0 us)
Async XLA Ops:
  0.6 38.2 %copy-start = (s32[1,1,64,128]{3,2,1,0:T(8,128)S(1)}, s32[1,1,64,128]{3,2,1,0:T(8,128)}, u32[]{:S(2)}) copy-start(s32[1,1,64,128]{3,2,1,0:T(8,128)} %param.10) | copy-start | bytes 98308
  0.6 38.2 %copy-start.1 = (s32[8,8,128]{2,1,0:T(8,128)S(1)}, s32[8,8,128]{2,1,0:T(8,128)}, u32[]{:S(2)}) copy-start(s32[8,8,128]{2,1,0:T(8,128)} %param.12) | copy-start | bytes 98308
  38.9 28.0 %copy-start.2 = (f32[8,8,128]{2,1,0:T(8,128)S(1)}, f32[8,8,128]{2,1,0:T(8,128)}, u32[]{:S(2)}) copy-start(f32[8,8,128]{2,1,0:T(8,128)} %param.7) | copy-start | bytes 98308
  70.1 19.9 %all-to-all-start.4 = ((f32[256,1,128]{2,1,0:T(1,128)}), f32[256,1,128]{2,1,0:T(1,128)S(1)}, u32[]{:S(2)}, u32[]{:S(2)}) async-start(f32[256,1,128]{2,1,0:T(1,128)} %bitcast.19), calls=%async_computation.4 | async-start | bytes 262144 | tf_op jit(solution)/shard_map/all_to_all | solution.py:549

commit v8 on v7

--- a/solution.py
+++ b/solution.py
@@ -206,39 +206,36 @@
     pieces_ref[pl.ds(after * rows + row, 8), :] = field_ref[pl.ds(7, 8, stride=8), :]
 
 
+def within(left, right, member, outside):
+    left = jnp.where(member > 0, left, outside)
+    right = jnp.where(member < SIDE - 1, right, outside)
+    return left, right
+
+
 def get_faces(pieces_ref, rows, row, member, outside):
     before, after = jnp.maximum(member - 1, 0), jnp.minimum(member + 1, SIDE - 1)
     left = pieces_ref[pl.ds(before * rows + row, 8), :]
     right = pieces_ref[pl.ds(after * rows + row, 8), :]
-    left = jnp.where(member > 0, left, outside)
-    right = jnp.where(member < SIDE - 1, right, outside)
-    return left, right
-
-
-def fill_slabs(slabs_ref, field_ref, faces, pieces, outside):
-    owner, member = position()
-    faces_ref, face_rows, face_row = faces
-    pieces_ref, rows, plane_row, halo_row = pieces
-    left, right = get_faces(faces_ref, face_rows, face_row, member, outside)
+    return within(left, right, member, outside)
+
+
+def fill_slabs(slabs_ref, field_ref, faces, ends, outside):
+    owner, member = position()
+    left, right = faces
     gap = jnp.full((8, LANES), outside, F32)
     for plane in range(8):
         slabs_ref[plane + 1, :8, :] = field_ref[8 * plane : 8 * plane + 8, :]
         slabs_ref[plane + 1, 8:, :] = gap
         slabs_ref[plane + 1, RIGHT : RIGHT + 1, :] = right[plane : plane + 1, :]
         slabs_ref[plane + 1, LEFT : LEFT + 1, :] = left[plane : plane + 1, :]
-    for plane, there, inside in (
-        (0, jnp.maximum(owner - 1, 0), owner > 0),
-        (9, jnp.minimum(owner + 1, SIDE - 1), owner < SIDE - 1),
+    for plane, inside, (own, *halos) in (
+        (0, owner > 0, ends[0]),
+        (9, owner < SIDE - 1, ends[1]),
     ):
-        start = there * rows
         slabs_ref[plane, 8:, :] = gap
-        slabs_ref[plane, :8, :] = jnp.where(
-            inside, pieces_ref[pl.ds(start + plane_row, 8), :], outside
-        )
-        for side, target in enumerate((LEFT, RIGHT)):
-            slabs_ref[plane, target : target + 1, :] = jnp.where(
-                inside, pieces_ref[pl.ds(start + halo_row + side, 1), :], outside
-            )
+        slabs_ref[plane, :8, :] = jnp.where(inside, own, outside)
+        for target, halo in zip((LEFT, RIGHT), halos):
+            slabs_ref[plane, target : target + 1, :] = jnp.where(inside, halo, outside)
 
 
 def add_prolonged(slabs_ref, numbers_ref, rows_ref):
@@ -268,17 +265,17 @@
     return aggregate - iota((ROWS, LANES), 1) // AGG
 
 
-F_FIELD, F_KAPPA, F_MAP, F_SOURCE, F_FIRST = 0, 8, 16, 24, 25
-C_FIELD, C_KAPPA, C_MAP, C_HALOS, C_SOURCE, C_DIAGONAL, C_FIRST = 0, 8, 16, 24, 30, 32, 34
+FIELD, KAPPA, MAP, FACE_ROWS, PLANE_ROWS = 0, 8, 16, 24, 32
+OUTSIDE = (0.0, 0.0, -1.0)
 F_SOURCE_2, F_SECOND = 8, 9
 C_HALO_2, C_SOURCE_2, C_SECOND = 8, 10, 12
 
 
 def begin(
     table_hbm, side_hbm, index_hbm, order_hbm, matrices_hbm, map_hbm, diagonal_hbm,
-    pieces_ref, kappa_ref, smoothed_ref, numbers_ref, matrices_ref,
+    pieces_ref, left_ref, right_ref, kappa_ref, smoothed_ref, numbers_ref,
     table_ref, side_ref, index_ref, order_ref, map_ref, diagonal_ref, picked_ref, product_ref,
-    arrived,
+    matrices_ref, arrived,
 ):
     owner, member = position()
     copies = [
@@ -314,10 +311,12 @@
     source = restrict(side_ref[...], offsets(aggregate), member)
     spread = jnp.broadcast_to(jnp.concatenate([diagonal_ref[...]] * 8, axis=1), (8, LANES))
     beside = iota((8, LANES), 1) // SIDE == (member + 1) % 8
-    put_all(jnp.where(beside, spread, source), pieces_ref, F_FIRST, F_SOURCE)
-    put_faces(smoothed_ref, pieces_ref, F_FIRST, F_FIELD, member)
-    put_faces(kappa_ref, pieces_ref, F_FIRST, F_KAPPA, member)
-    put_faces(numbers_ref, pieces_ref, F_FIRST, F_MAP, member)
+    message = jnp.where(beside, spread, source)
+    for start in range(0, WIDE, 8):
+        pieces_ref[start : start + 8, :] = message
+    for row, field_ref in ((FIELD, smoothed_ref), (KAPPA, kappa_ref), (MAP, numbers_ref)):
+        left_ref[row : row + 8, :] = field_ref[pl.ds(0, 8, stride=8), :]
+        right_ref[row : row + 8, :] = field_ref[pl.ds(7, 8, stride=8), :]
 
 
 def put_all(values, pieces_ref, rows, row):
@@ -339,38 +338,68 @@
             pieces_ref[pl.ds(start + halo_row + side, 1), :] = halo[plane : plane + 1, :]
 
 
-def gathered(rows, step):
-    here = iota((SIDE, LANES), 0) % 8
-    rows = jnp.where(iota((SIDE, LANES), 1) // SIDE == (here + step) % 8, rows, 0.0)
-    parts = [jnp.sum(rows[at : at + 8], axis=0, keepdims=True) for at in (0, 8)]
+def gathered(rows):
+    place = iota((SIDE, LANES), 0) % 8
+    rows = jnp.where(iota((SIDE, LANES), 1) // SIDE == place, rows, 0.0)
+    return [jnp.sum(rows[at : at + 8], axis=0, keepdims=True) for at in (0, 8)]
+
+
+def coarse_rows(pieces_ref, step):
+    pieces = pieces_ref[...].reshape(SIDE, SIDE, LANES)
+    place = (iota((SIDE, LANES), 0) + step) % 8
+    kept = jnp.where((iota((SIDE, LANES), 1) // SIDE == place)[None], pieces, 0.0)
+    halves_of = [jnp.sum(kept[:, :8], axis=1), jnp.sum(kept[:, 8:], axis=1)]
     if step:
-        parts = [
-            pltpu.roll(jnp.broadcast_to(part, (8, LANES)), LANES - SIDE * step, 1)
-            for part in parts
-        ]
-    return parts
-
-
-def first_parts(faces_ref, pieces_ref):
-    return (
-        ((faces_ref, F_FIRST, F_FIELD), (pieces_ref, C_FIRST, C_FIELD, C_HALOS), 0.0),
-        ((faces_ref, F_FIRST, F_KAPPA), (pieces_ref, C_FIRST, C_KAPPA, C_HALOS + 2), 0.0),
-        ((faces_ref, F_FIRST, F_MAP), (pieces_ref, C_FIRST, C_MAP, C_HALOS + 4), -1.0),
-    )
-
-
-def second_parts(faces_ref, pieces_ref):
-    return (faces_ref, F_SECOND, 0), (pieces_ref, C_SECOND, 0, C_HALO_2), 0.0
-
-
-def relay_first(faces_ref, smoothed_ref, kappa_ref, numbers_ref, pieces_ref):
-    rows = faces_ref[pl.ds(F_SOURCE, SIDE, stride=F_FIRST), :]
-    for half in range(2):
-        put_all(gathered(rows, 0)[half], pieces_ref, C_FIRST, C_SOURCE + half)
-        put_all(gathered(rows, 1)[half], pieces_ref, C_FIRST, C_DIAGONAL + half)
-    parts = first_parts(faces_ref, pieces_ref)
-    for field_ref, part in zip((smoothed_ref, kappa_ref, numbers_ref), parts):
-        put_planes(field_ref, *part)
+        halves_of = [pltpu.roll(half, LANES - SIDE * step, 1) for half in halves_of]
+    return jnp.concatenate(halves_of, axis=1)
+
+
+def first_faces(left_ref, right_ref, row, member, outside):
+    return within(left_ref[row : row + 8, :], right_ref[row : row + 8, :], member, outside)
+
+
+def relay_first(
+    left_ref, right_ref, smoothed_ref, kappa_ref, numbers_ref, before_ref, after_ref
+):
+    owner, member = position()
+    fields = (smoothed_ref, kappa_ref, numbers_ref)
+    for target_ref, plane in ((before_ref, 0), (after_ref, 7)):
+        target_ref[FACE_ROWS:, :] = jnp.zeros((8, LANES), F32)
+        for number, field_ref in enumerate(fields):
+            row = 8 * number
+            faces = first_faces(left_ref, right_ref, row, member, OUTSIDE[number])
+            target_ref[row : row + 8, :] = field_ref[8 * plane : 8 * plane + 8, :]
+            for side, face in enumerate(faces):
+                halo = FACE_ROWS + 2 * number + side
+                target_ref[halo : halo + 1, :] = face[plane : plane + 1, :]
+
+
+def fill_first(slabs_ref, field_ref, left_ref, right_ref, before_ref, after_ref, number):
+    owner, member = position()
+    row, outside = 8 * number, OUTSIDE[number]
+    halo = FACE_ROWS + 2 * number
+    ends = [
+        (end[row : row + 8, :], end[halo : halo + 1, :], end[halo + 1 : halo + 2, :])
+        for end in (before_ref, after_ref)
+    ]
+    faces = first_faces(left_ref, right_ref, row, member, outside)
+    fill_slabs(slabs_ref, field_ref, faces, ends, outside)
+
+
+def fill_second(slabs_ref, field_ref, faces_ref, pieces_ref):
+    owner, member = position()
+    ends = []
+    for there in (jnp.maximum(owner - 1, 0), jnp.minimum(owner + 1, SIDE - 1)):
+        start = there * C_SECOND
+        ends.append(
+            (
+                pieces_ref[pl.ds(start, 8), :],
+                pieces_ref[pl.ds(start + C_HALO_2, 1), :],
+                pieces_ref[pl.ds(start + C_HALO_2 + 1, 1), :],
+            )
+        )
+    faces = get_faces(faces_ref, F_SECOND, 0, member, 0.0)
+    fill_slabs(slabs_ref, field_ref, faces, ends, 0.0)
 
 
 def halves(pieces_ref, rows, row):
@@ -380,28 +409,32 @@
 
 
 def first_image(
-    faces_ref, ends_ref, own_ref, own_kappa_ref, numbers_ref, map_ref, order_ref,
+    rows_of_all_ref, left_ref, right_ref, before_ref, after_ref,
+    own_ref, own_kappa_ref, numbers_ref, map_ref, order_ref, matrices_hbm,
+    pieces_ref, field_ref, image_ref, smoothed_ref, kappa_ref, lanes_ref, diagonal_ref,
     matrices_ref,
-    pieces_ref, field_ref, image_ref, smoothed_ref, kappa_ref, lanes_ref, diagonal_ref,
-    picked_ref, product_ref, slabs_ref, rows_ref,
+    picked_ref, product_ref, slabs_ref, rows_ref, arrived,
 ):
     owner, member = position()
-    diagonal = halves(ends_ref, C_FIRST, C_DIAGONAL)
+    copy = pltpu.make_async_copy(matrices_hbm, matrices_ref, arrived)
+    copy.start()
+    diagonal = coarse_rows(rows_of_all_ref, 1)
     diagonal_ref[...] = diagonal
-    nearby(coarse_solve(halves(ends_ref, C_FIRST, C_SOURCE), diagonal), member, rows_ref)
-    parts = first_parts(faces_ref, ends_ref)
-    fill_slabs(slabs_ref, numbers_ref, *parts[2])
+    nearby(coarse_solve(coarse_rows(rows_of_all_ref, 0), diagonal), member, rows_ref)
+    around = left_ref, right_ref, before_ref, after_ref
+    fill_first(slabs_ref, numbers_ref, *around, 2)
     row = iota((10, SLAB, LANES), 1)
     shift = jnp.where(row < 8, SIDE, jnp.where(row == RIGHT, 2 * SIDE, 0))
     number = slabs_ref[...]
     lanes_ref[...] = jnp.where(number >= 0.0, number.astype(jnp.int32) + shift, -1)
-    fill_slabs(kappa_ref, own_kappa_ref, *parts[1])
-    fill_slabs(slabs_ref, own_ref, *parts[0])
+    fill_first(kappa_ref, own_kappa_ref, *around, 1)
+    fill_first(slabs_ref, own_ref, *around, 0)
     add_prolonged(slabs_ref, lanes_ref, rows_ref)
     field = slabs_ref[...]
     field_ref[...] = field[1:9, :8].reshape(ROWS, LANES)
     image_ref[...] = operate(field, kappa_ref[...]).reshape(ROWS, LANES)
     pick(image_ref, order_ref, picked_ref)
+    copy.wait()
     multiply_blocks(matrices_ref, picked_ref, product_ref)
     put_back(product_ref, order_ref, smoothed_ref)
     source = restrict(image_ref[...], offsets(map_ref[...]), member)
@@ -411,9 +444,10 @@
 
 def relay_second(faces_ref, smoothed_ref, pieces_ref):
     rows = faces_ref[pl.ds(F_SOURCE_2, SIDE, stride=F_SECOND), :]
-    for half, values in enumerate(gathered(rows, 0)):
+    for half, values in enumerate(gathered(rows)):
         put_all(values, pieces_ref, C_SECOND, C_SOURCE_2 + half)
-    put_planes(smoothed_ref, *second_parts(faces_ref, pieces_ref))
+    faces, pieces = (faces_ref, F_SECOND, 0), (pieces_ref, C_SECOND, 0, C_HALO_2)
+    put_planes(smoothed_ref, faces, pieces, 0.0)
 
 
 def second_image(
@@ -423,8 +457,9 @@
     picked_ref, slabs_ref, rows_ref,
 ):
     owner, member = position()
-    nearby(coarse_solve(halves(ends_ref, C_SECOND, C_SOURCE_2), diagonal_ref[...]), member, rows_ref)
-    fill_slabs(slabs_ref, own_ref, *second_parts(faces_ref, ends_ref))
+    source = halves(ends_ref, C_SECOND, C_SOURCE_2)
+    nearby(coarse_solve(source, diagonal_ref[...]), member, rows_ref)
+    fill_second(slabs_ref, own_ref, faces_ref, ends_ref)
     add_prolonged(slabs_ref, lanes_ref, rows_ref)
     slabs = slabs_ref[...]
     field = slabs[1:9, :8].reshape(ROWS, LANES)
@@ -464,10 +499,7 @@
     group = iota((SIDE, LANES), 1) // SIDE
     pieces_sum = jnp.sum(pieces, axis=0)
     sums = jnp.where(group == (place + 1) % 8, pieces_sum, 0.0)
-    kept = jnp.where((group == place)[None], pieces, 0.0)
-    source = jnp.concatenate(
-        [jnp.sum(kept[:, :8], axis=1), jnp.sum(kept[:, 8:], axis=1)], axis=1
-    )
+    source = coarse_rows(pieces_ref, 0)
     coarse = coarse_solve(source, diagonal_ref[...])
     lane = iota((1, LANES), 1)
     sums = jnp.sum(sums, axis=0, keepdims=True)
@@ -549,40 +581,47 @@
         pieces = lax.all_to_all(pieces.reshape(rows[0], 1, LANES), axis, 0, 0, tiled=True)
         return pieces.reshape(rows)
 
+    def ring(rows, axis, step):
+        return lax.ppermute(rows, axis, [(i, (i + step) % SIDE) for i in range(SIDE)])
+
     fixed = [
         pltpu.with_memory_space_constraint(array, pltpu.HBM)
         for array in (material_coefficients, side, index, order, matrices, aggregate, diagonal)
     ]
-    pieces, kappa, smoothed, numbers, matrices = call(
+    pieces, left, right, kappa, smoothed, numbers = call(
         begin,
         [
-            shape(SIDE * F_FIRST, LANES), local, local, local, pltpu.VMEM(matrices.shape, F32),
+            shape(WIDE, LANES), shape(FACE_ROWS, LANES), shape(FACE_ROWS, LANES), local, local,
+            local,
         ],
         7,
         [
             pltpu.SMEM(material_coefficients.shape, F32), cells, int_cells, int_cells,
             int_cells, pltpu.VMEM((1, SIDE), F32), cells, cells,
-            pltpu.SemaphoreType.DMA((7,)),
+            pltpu.VMEM(matrices.shape, F32), pltpu.SemaphoreType.DMA((7,)),
         ],
         [hbm()] * 7,
     )(*fixed)
-    matrices = pltpu.with_memory_space_constraint(matrices, pltpu.VMEM)
-    faces = exchange(pieces, FINE)
-    (pieces,) = call(relay_first, [shape(SIDE * C_FIRST, LANES)], 4)(
-        faces, smoothed, kappa, numbers
-    )
-    ends = exchange(pieces, COARSE)
-    pieces, first, image, smoothed, kappa, lanes, diagonals = call(
+    right, left = ring(left, FINE, -1), ring(right, FINE, 1)
+    rows = exchange(pieces, (COARSE, FINE))
+    before, after = call(
+        relay_first, [shape(PLANE_ROWS, LANES), shape(PLANE_ROWS, LANES)], 5
+    )(left, right, smoothed, kappa, numbers)
+    after, before = ring(before, COARSE, -1), ring(after, COARSE, 1)
+    pieces, first, image, smoothed, kappa, lanes, diagonals, matrices = call(
         first_image,
         [
             shape(SIDE * F_SECOND, LANES), local, local, local, shape(10, SLAB, LANES),
             shape(10, SLAB, LANES, dtype=jnp.int32), shape(SIDE, WIDE),
+            pltpu.VMEM(matrices.shape, F32),
         ],
-        8,
-        scratch,
+        11,
+        scratch + [pltpu.SemaphoreType.DMA],
+        [vmem()] * 10 + [hbm()],
     )(
-        faces, ends, smoothed, kappa, numbers, aggregate, order, matrices,
-    )
+        rows, left, right, before, after, smoothed, kappa, numbers, aggregate, order, fixed[4]
+    )
+    matrices = pltpu.with_memory_space_constraint(matrices, pltpu.VMEM)
     faces = exchange(pieces, FINE)
     (pieces,) = call(relay_second, [shape(SIDE * C_SECOND, LANES)], 2)(faces, smoothed)
     ends = exchange(pieces, COARSE)

time: 91.4 us -> 92.2 us (level)
  blocking collectives: 58.6 us -> 28.8 us
  starting transfers between devices: 6.94 us -> 32.2 us
  waiting for transfers between devices: 11.9 us -> 15.7 us
  Pallas kernels: 13 us -> 14.5 us
    all_to_all x4 -> x2, blocking collectives: 58.6 us -> 28.8 us  [exchange(): lax.all_to_all(pieces.reshape(rows[0], 1, LANES), axis, 0, 0, tiled=True)]
    all_to_all x1 -> x2, starting transfers between devices: 6.94 us -> 22.6 us  [exchange(): lax.all_to_all(pieces.reshape(rows[0], 1, LANES), axis, 0, 0, tiled=True)]
    ppermute x0 -> x4, starting transfers between devices: none -> 9.55 us  [ring(): lax.ppermute(rows, axis, [(i, (i + step) % SIDE) for i in range(SIDE)])]
    ppermute x0 -> x4, waiting for transfers between devices: none -> 3.87 us  [ring(): lax.ppermute(rows, axis, [(i, (i + step) % SIDE) for i in range(SIDE)])]
    pallas_call x1, Pallas kernels: 3.22 us -> 4.39 us  [shards(): call(first_image, [shape(SIDE * F_SECOND, LANES), local, local, local, sh...]
    all_to_all x1 -> x2, waiting for transfers between devices: 11.9 us -> 11.9 us  [exchange(): lax.all_to_all(pieces.reshape(rows[0], 1, LANES), axis, 0, 0, tiled=True)]
  transfers between devices with their start and end apart: 1 -> 6, of which waited for: 1 -> 4; matrix products, arithmetic and copies ran while one was open for 0% -> 0% of each run, Pallas kernels for 1% -> 1%
where the time goes in v8:
time: 92.2 us; the launch traced here: 91.9 us
  starting transfers between devices  32.2 us (35%)
  blocking collectives  28.8 us (31%)
  waiting for transfers between devices  15.7 us (17%)
  Pallas kernels  14.5 us (16%)
    all_to_all x2, blocking collectives, exchange(): lax.all_to_all(pieces.reshape(rows[0], 1, LANES), axis, 0, 0, tiled=True)  28.8 us
    all_to_all x2, starting transfers between devices, exchange(): lax.all_to_all(pieces.reshape(rows[0], 1, LANES), axis, 0, 0, tiled=True)  22.6 us
    all_to_all x2, waiting for transfers between devices, exchange(): lax.all_to_all(pieces.reshape(rows[0], 1, LANES), axis, 0, 0, tiled=True)  11.9 us
    ppermute x4, starting transfers between devices, ring(): lax.ppermute(rows, axis, [(i, (i + step) % SIDE) for i in range(SIDE)])  9.55 us
    pallas_call x1, Pallas kernels, shards(): call(begin, [shape(WIDE, LANES), shape(FACE_ROWS, LANES), shape(FACE_ROWS...  4.65 us
    pallas_call x1, Pallas kernels, shards(): call(first_image, [shape(SIDE * F_SECOND, LANES), local, local, local, sh...  4.39 us
    ppermute x4, waiting for transfers between devices, ring(): lax.ppermute(rows, axis, [(i, (i + step) % SIDE) for i in range(SIDE)])  3.87 us
    pallas_call x1, Pallas kernels, shards(): call(second_image, [shape(WIDE, LANES), local, local, local], 12, scratch...  3.26 us
  transfers between devices with their start and end apart: 6, of which 4 were waited for; matrix products, arithmetic and copies ran while one was open for 0% of the time, Pallas kernels for 1%

profile of v8, /device:TPU:1, one launch (start us, length us, event | category | flops | bytes accessed | tf_op | source)
XLA Modules:
  0.0 91.9 jit_solution(8238085948473343014)
XLA Ops:
  0.6 0.0 copy-start.1
  0.6 0.0 copy-start
  0.7 4.7 %shard_map.94 = (f32[256,128]{1,0:T(8,128)}, f32[24,128]{1,0:T(8,128)S(1)}, f32[24,128]{1,0:T(8,128)S(1)}, f32[64,128]{1,0:T(8,128)S(1)}, f32[64,128]{1,0:T(8,128)S(1)}, /*index=5*/f32[64,128]{1,0:T(8,128)S(1)}) custom-call(f32[16]{0:T(128)} %table_hbm.1, f32[64,128]{1,0:T(8,128)} %bitcast.37, s32[64,128]{1,0:T(8,128)} %bitcast.45, s32[64,128]{1,0:T(8,128)} %bitcast.27, ...), custom_call_target="tpu_custom_call" | custom-call | flops 1000000000 | bytes 4000000 | tf_op jit(solution)/shard_map/pallas_call | solution.py:591
  5.3 15.7 %all-to-all-start = ((f32[256,1,128]{2,1,0:T(1,128)}), f32[256,1,128]{2,1,0:T(1,128)S(1)}, u32[]{:S(2)}, u32[]{:S(2)}) async-start(f32[256,1,128]{2,1,0:T(1,128)} %bitcast.7), calls=%async_computation | async-start | bytes 262144 | tf_op jit(solution)/shard_map/all_to_all | solution.py:581
  21.0 1.7 %collective-permute-start = (f32[24,128]{1,0:T(8,128)S(1)}, f32[24,128]{1,0:T(8,128)S(1)}, u32[]{:S(2)}, u32[]{:S(2)}) collective-permute-start(f32[24,128]{1,0:T(8,128)S(1)} %get-tuple-element.27), channel_id=1, source_target_pairs={{0,1},{1,2},{2,3},{3,4},{4,5},{5,6},{6,7},{7,8},{8,9},{9,10},{10,1... | collective-permute-start | bytes 36872 | tf_op jit(solution)/shard_map/ppermute | solution.py:585
  22.7 0.6 collective-permute-start.1
  23.3 0.6 collective-permute-done.left_ref
  23.9 2.2 %collective-permute-done.1.right_ref = f32[24,128]{1,0:T(8,128)S(1)} collective-permute-done((f32[24,128]{1,0:T(8,128)S(1)}, f32[24,128]{1,0:T(8,128)S(1)}, u32[]{:S(2)}, u32[]{:S(2)}) %collective-permute-start.1) | collective-permute-done | bytes 12320 | tf_op jit(solution)/shard_map/ppermute | solution.py:585
  26.1 1.3 %collective-permute-start.2 = (f32[32,128]{1,0:T(8,128)S(1)}, f32[32,128]{1,0:T(8,128)S(1)}, u32[]{:S(2)}, u32[]{:S(2)}) collective-permute-start(f32[32,128]{1,0:T(8,128)S(1)} %get-tuple-element.32), channel_id=1, source_target_pairs={{0,16},{16,32},{32,48},{48,64},{64,80},{80,96},{96,112},{112,128},... | collective-permute-start | bytes 49160 | tf_op jit(solution)/shard_map/ppermute | solution.py:585
  27.4 6.0 %collective-permute-start.3 = (f32[32,128]{1,0:T(8,128)S(1)}, f32[32,128]{1,0:T(8,128)S(1)}, u32[]{:S(2)}, u32[]{:S(2)}) collective-permute-start(f32[32,128]{1,0:T(8,128)S(1)} %get-tuple-element.33), channel_id=1, source_target_pairs={{0,240},{16,0},{32,16},{48,32},{64,48},{80,64},{96,80},{112,96},{1... | collective-permute-start | bytes 49160 | tf_op jit(solution)/shard_map/ppermute | solution.py:585
  33.4 1.0 %collective-permute-done.2.before_ref = f32[32,128]{1,0:T(8,128)S(1)} collective-permute-done((f32[32,128]{1,0:T(8,128)S(1)}, f32[32,128]{1,0:T(8,128)S(1)}, u32[]{:S(2)}, u32[]{:S(2)}) %collective-permute-start.2) | collective-permute-done | bytes 16416 | tf_op jit(solution)/shard_map/ppermute | solution.py:585
  34.4 0.0 collective-permute-done.3.after_ref
  34.4 0.0 all-to-all-done
  34.4 0.0 copy-done.1
  34.4 0.0 copy-done
  34.4 0.0 copy-start.2
  34.5 4.4 %shard_map.96 = (f32[144,128]{1,0:T(8,128)S(1)}, f32[64,128]{1,0:T(8,128)S(1)}, f32[64,128]{1,0:T(8,128)S(1)}, f32[64,128]{1,0:T(8,128)S(1)}, f32[10,16,128]{2,1...) custom-call(f32[256,128]{1,0:T(8,128)S(1)} %bitcast.25, ...), custom_call_target="tpu_custom_call" | custom-call | flops 1000000000 | bytes 4000000 | tf_op jit(solution)/shard_map/pallas_call | solution.py:611
  38.9 12.0 %all_to_all.20 = f32[144,1,128]{2,1,0:T(1,128)S(1)} all-to-all(f32[144,1,128]{2,1,0:T(1,128)S(1)} %bitcast.42), channel_id=1, replica_groups=mesh['coarse'=16,'fine'=16] {'fine'}, dimensions={0} | all-to-all | bytes 147456 | tf_op jit(solution)/shard_map/all_to_all | solution.py:581
  50.9 16.8 %all_to_all.21 = f32[192,1,128]{2,1,0:T(1,128)S(1)} all-to-all(f32[192,1,128]{2,1,0:T(1,128)S(1)} %bitcast.41), channel_id=1, replica_groups=mesh['coarse'=16,'fine'=16] {'coarse'}, dimensions={0} | all-to-all | bytes 196608 | tf_op jit(solution)/shard_map/all_to_all | solution.py:581
  67.6 0.0 copy-done.2
  67.6 3.3 %shard_map.98 = (f32[256,128]{1,0:T(8,128)}, f32[64,128]{1,0:T(8,128)S(1)}, f32[64,128]{1,0:T(8,128)S(1)}, f32[64,128]{1,0:T(8,128)S(1)}) custom-call(f32[144,128]{1,0:T(8,128)S(1)} %bitcast.36, f32[192,128]{1,0:T(8,128)S(1)} %bitcast.26, f32[64,128]{1,0:T(8,128)S(1)} %get-tuple-element.35.smoothed_ref.own_ref, ...), custom_call_target="tpu_custom_call" | custom-call | flops 1000000000 | bytes 4000000 | tf_op jit(solution)/shard_map/pallas_call | solution.py:628
  70.9 6.9 %all-to-all-start.3 = ((f32[256,1,128]{2,1,0:T(1,128)}), f32[256,1,128]{2,1,0:T(1,128)S(1)}, u32[]{:S(2)}, u32[]{:S(2)}) async-start(f32[256,1,128]{2,1,0:T(1,128)} %bitcast.16), calls=%async_computation.3 | async-start | bytes 262144 | tf_op jit(solution)/shard_map/all_to_all | solution.py:581
  77.9 1.1 %shard_map.99.smoothed_ref = f32[64,128]{1,0:T(8,128)S(1)} custom-call(f32[64,128]{1,0:T(8,128)S(1)} %get-tuple-element.45.product_ref, s32[64,128]{1,0:T(8,128)S(1)} %bitcast.30), custom_call_target="tpu_custom_call" | custom-call | flops 1000000000 | bytes 4000000 | tf_op jit(solution)/shard_map/pallas_call | solution.py:638
  78.9 11.9 %all-to-all-done.3 = f32[256,1,128]{2,1,0:T(1,128)S(1)} async-done(((f32[256,1,128]{2,1,0:T(1,128)}), f32[256,1,128]{2,1,0:T(1,128)S(1)}, u32[]{:S(2)}, u32[]{:S(2)}) %all-to-all-start.3) | async-done | bytes 131104 | tf_op jit(solution)/shard_map/all_to_all | solution.py:581
  90.8 1.1 %shard_map.100 = (f32[64,128]{1,0:T(8,128)}, f32[64,128]{1,0:T(8,128)}, f32[64,128]{1,0:T(8,128)}) custom-call(f32[256,128]{1,0:T(8,128)S(1)} %bitcast.40, f32[16,256]{1,0:T(8,128)S(1)} %get-tuple-element.38.diagonal_ref, s32[64,128]{1,0:T(8,128)S(1)} %bitcast.34, f32[64,128]{1,0:T(8,128)S(1)} %bitcast.39, f32[64,128]{1,0:T(8,128)S(1)} %get-tuple-element.39.first_ref, ...), custom_call_target="tpu_custom_call" | custom-call | flops 1000000000 | bytes 4000000 | tf_op jit(solution)/shard_map/pallas_call | solution.py:639
  (2 shorter events, 0.0 us)
Async XLA Ops:
  0.6 33.8 %copy-start.1 = (s32[8,8,128]{2,1,0:T(8,128)S(1)}, s32[8,8,128]{2,1,0:T(8,128)}, u32[]{:S(2)}) copy-start(s32[8,8,128]{2,1,0:T(8,128)} %param.12) | copy-start | bytes 98308
  0.6 33.8 %copy-start = (s32[1,1,64,128]{3,2,1,0:T(8,128)S(1)}, s32[1,1,64,128]{3,2,1,0:T(8,128)}, u32[]{:S(2)}) copy-start(s32[1,1,64,128]{3,2,1,0:T(8,128)} %param.10) | copy-start | bytes 98308
  5.3 29.1 %all-to-all-start = ((f32[256,1,128]{2,1,0:T(1,128)}), f32[256,1,128]{2,1,0:T(1,128)S(1)}, u32[]{:S(2)}, u32[]{:S(2)}) async-start(f32[256,1,128]{2,1,0:T(1,128)} %bitcast.7), calls=%async_computation | async-start | bytes 262144 | tf_op jit(solution)/shard_map/all_to_all | solution.py:581
  21.0 2.9 %collective-permute-start = (f32[24,128]{1,0:T(8,128)S(1)}, f32[24,128]{1,0:T(8,128)S(1)}, u32[]{:S(2)}, u32[]{:S(2)}) collective-permute-start(f32[24,128]{1,0:T(8,128)S(1)} %get-tuple-element.27), channel_id=1, source_target_pairs={{0,1},{1,2},{2,3},{3,4},{4,5},{5,6},{6,7},{7,8},{8,9},{9,10},{10,1... | collective-permute-start | bytes 36872 | tf_op jit(solution)/shard_map/ppermute | solution.py:585
  22.7 3.4 %collective-permute-start.1 = (f32[24,128]{1,0:T(8,128)S(1)}, f32[24,128]{1,0:T(8,128)S(1)}, u32[]{:S(2)}, u32[]{:S(2)}) collective-permute-start(f32[24,128]{1,0:T(8,128)S(1)} %get-tuple-element.28), channel_id=1, source_target_pairs={{0,15},{1,0},{2,1},{3,2},{4,3},{5,4},{6,5},{7,6},{8,7},{9,8},{10,9... | collective-permute-start | bytes 36872 | tf_op jit(solution)/shard_map/ppermute | solution.py:585
  26.1 8.3 %collective-permute-start.2 = (f32[32,128]{1,0:T(8,128)S(1)}, f32[32,128]{1,0:T(8,128)S(1)}, u32[]{:S(2)}, u32[]{:S(2)}) collective-permute-start(f32[32,128]{1,0:T(8,128)S(1)} %get-tuple-element.32), channel_id=1, source_target_pairs={{0,16},{16,32},{32,48},{48,64},{64,80},{80,96},{96,112},{112,128},... | collective-permute-start | bytes 49160 | tf_op jit(solution)/shard_map/ppermute | solution.py:585
  27.4 7.0 %collective-permute-start.3 = (f32[32,128]{1,0:T(8,128)S(1)}, f32[32,128]{1,0:T(8,128)S(1)}, u32[]{:S(2)}, u32[]{:S(2)}) collective-permute-start(f32[32,128]{1,0:T(8,128)S(1)} %get-tuple-element.33), channel_id=1, source_target_pairs={{0,240},{16,0},{32,16},{48,32},{64,48},{80,64},{96,80},{112,96},{1... | collective-permute-start | bytes 49160 | tf_op jit(solution)/shard_map/ppermute | solution.py:585
  34.4 33.2 %copy-start.2 = (f32[8,8,128]{2,1,0:T(8,128)S(1)}, f32[8,8,128]{2,1,0:T(8,128)}, u32[]{:S(2)}) copy-start(f32[8,8,128]{2,1,0:T(8,128)} %param.7) | copy-start | bytes 98308
  70.9 19.9 %all-to-all-start.3 = ((f32[256,1,128]{2,1,0:T(1,128)}), f32[256,1,128]{2,1,0:T(1,128)S(1)}, u32[]{:S(2)}, u32[]{:S(2)}) async-start(f32[256,1,128]{2,1,0:T(1,128)} %bitcast.16), calls=%async_computation.3 | async-start | bytes 262144 | tf_op jit(solution)/shard_map/all_to_all | solution.py:581

commit v9 on v8

--- a/solution.py
+++ b/solution.py
@@ -273,7 +273,7 @@
 
 def begin(
     table_hbm, side_hbm, index_hbm, order_hbm, matrices_hbm, map_hbm, diagonal_hbm,
-    pieces_ref, left_ref, right_ref, kappa_ref, smoothed_ref, numbers_ref,
+    pieces_ref, pair_ref, cross_ref, kappa_ref, smoothed_ref, numbers_ref,
     table_ref, side_ref, index_ref, order_ref, map_ref, diagonal_ref, picked_ref, product_ref,
     matrices_ref, arrived,
 ):
@@ -315,8 +315,11 @@
     for start in range(0, WIDE, 8):
         pieces_ref[start : start + 8, :] = message
     for row, field_ref in ((FIELD, smoothed_ref), (KAPPA, kappa_ref), (MAP, numbers_ref)):
-        left_ref[row : row + 8, :] = field_ref[pl.ds(0, 8, stride=8), :]
-        right_ref[row : row + 8, :] = field_ref[pl.ds(7, 8, stride=8), :]
+        left = field_ref[pl.ds(0, 8, stride=8), :]
+        right = field_ref[pl.ds(7, 8, stride=8), :]
+        even = member % 2 == 0
+        pair_ref[row : row + 8, :] = jnp.where(even, right, left)
+        cross_ref[row : row + 8, :] = jnp.where(even, left, right)
 
 
 def put_all(values, pieces_ref, rows, row):
@@ -354,12 +357,15 @@
     return jnp.concatenate(halves_of, axis=1)
 
 
-def first_faces(left_ref, right_ref, row, member, outside):
-    return within(left_ref[row : row + 8, :], right_ref[row : row + 8, :], member, outside)
+def first_faces(pair_ref, cross_ref, row, member, outside):
+    pair, cross = pair_ref[row : row + 8, :], cross_ref[row : row + 8, :]
+    even = member % 2 == 0
+    left, right = jnp.where(even, cross, pair), jnp.where(even, pair, cross)
+    return within(left, right, member, outside)
 
 
 def relay_first(
-    left_ref, right_ref, smoothed_ref, kappa_ref, numbers_ref, before_ref, after_ref
+    pair_ref, cross_ref, smoothed_ref, kappa_ref, numbers_ref, before_ref, after_ref
 ):
     owner, member = position()
     fields = (smoothed_ref, kappa_ref, numbers_ref)
@@ -367,14 +373,14 @@
         target_ref[FACE_ROWS:, :] = jnp.zeros((8, LANES), F32)
         for number, field_ref in enumerate(fields):
             row = 8 * number
-            faces = first_faces(left_ref, right_ref, row, member, OUTSIDE[number])
+            faces = first_faces(pair_ref, cross_ref, row, member, OUTSIDE[number])
             target_ref[row : row + 8, :] = field_ref[8 * plane : 8 * plane + 8, :]
             for side, face in enumerate(faces):
                 halo = FACE_ROWS + 2 * number + side
                 target_ref[halo : halo + 1, :] = face[plane : plane + 1, :]
 
 
-def fill_first(slabs_ref, field_ref, left_ref, right_ref, before_ref, after_ref, number):
+def fill_first(slabs_ref, field_ref, pair_ref, cross_ref, before_ref, after_ref, number):
     owner, member = position()
     row, outside = 8 * number, OUTSIDE[number]
     halo = FACE_ROWS + 2 * number
@@ -382,7 +388,7 @@
         (end[row : row + 8, :], end[halo : halo + 1, :], end[halo + 1 : halo + 2, :])
         for end in (before_ref, after_ref)
     ]
-    faces = first_faces(left_ref, right_ref, row, member, outside)
+    faces = first_faces(pair_ref, cross_ref, row, member, outside)
     fill_slabs(slabs_ref, field_ref, faces, ends, outside)
 
 
@@ -409,7 +415,7 @@
 
 
 def first_image(
-    rows_of_all_ref, left_ref, right_ref, before_ref, after_ref,
+    rows_of_all_ref, pair_ref, cross_ref, before_ref, after_ref,
     own_ref, own_kappa_ref, numbers_ref, map_ref, order_ref, matrices_hbm,
     pieces_ref, field_ref, image_ref, smoothed_ref, kappa_ref, lanes_ref, diagonal_ref,
     matrices_ref,
@@ -421,7 +427,7 @@
     diagonal = coarse_rows(rows_of_all_ref, 1)
     diagonal_ref[...] = diagonal
     nearby(coarse_solve(coarse_rows(rows_of_all_ref, 0), diagonal), member, rows_ref)
-    around = left_ref, right_ref, before_ref, after_ref
+    around = pair_ref, cross_ref, before_ref, after_ref
     fill_first(slabs_ref, numbers_ref, *around, 2)
     row = iota((10, SLAB, LANES), 1)
     shift = jnp.where(row < 8, SIDE, jnp.where(row == RIGHT, 2 * SIDE, 0))
@@ -588,7 +594,7 @@
         pltpu.with_memory_space_constraint(array, pltpu.HBM)
         for array in (material_coefficients, side, index, order, matrices, aggregate, diagonal)
     ]
-    pieces, left, right, kappa, smoothed, numbers = call(
+    pieces, pair, cross, kappa, smoothed, numbers = call(
         begin,
         [
             shape(WIDE, LANES), shape(FACE_ROWS, LANES), shape(FACE_ROWS, LANES), local, local,
@@ -602,11 +608,14 @@
         ],
         [hbm()] * 7,
     )(*fixed)
-    right, left = ring(left, FINE, -1), ring(right, FINE, 1)
+    pair = lax.ppermute(pair, FINE, [(i, i ^ 1) for i in range(SIDE)])
+    cross = lax.ppermute(
+        cross, FINE, [(i, (i + (1 if i % 2 else -1)) % SIDE) for i in range(SIDE)]
+    )
     rows = exchange(pieces, (COARSE, FINE))
     before, after = call(
         relay_first, [shape(PLANE_ROWS, LANES), shape(PLANE_ROWS, LANES)], 5
-    )(left, right, smoothed, kappa, numbers)
+    )(pair, cross, smoothed, kappa, numbers)
     after, before = ring(before, COARSE, -1), ring(after, COARSE, 1)
     pieces, first, image, smoothed, kappa, lanes, diagonals, matrices = call(
         first_image,
@@ -619,7 +628,7 @@
         scratch + [pltpu.SemaphoreType.DMA],
         [vmem()] * 10 + [hbm()],
     )(
-        rows, left, right, before, after, smoothed, kappa, numbers, aggregate, order, fixed[4]
+        rows, pair, cross, before, after, smoothed, kappa, numbers, aggregate, order, fixed[4]
     )
     matrices = pltpu.with_memory_space_constraint(matrices, pltpu.VMEM)
     faces = exchange(pieces, FINE)

time: 92.2 us -> 91.9 us (level)
  starting transfers between devices: 32.2 us -> 30.6 us
  waiting for transfers between devices: 15.7 us -> 16.8 us
    ppermute x4 -> x2, starting transfers between devices: 9.55 us -> 5.75 us  [ring(): lax.ppermute(rows, axis, [(i, (i + step) % SIDE) for i in range(SIDE)])]
    ppermute x0 -> x2, waiting for transfers between devices: none -> 3.48 us  [the longest x1 2.65 us: shards(): lax.ppermute(cross, FINE, [(i, (i + (1 if i % 2 else -1)) % SIDE) for i i...]
    ppermute x4 -> x2, waiting for transfers between devices: 3.87 us -> 1.42 us  [ring(): lax.ppermute(rows, axis, [(i, (i + step) % SIDE) for i in range(SIDE)])]
    ppermute x0 -> x2, starting transfers between devices: none -> 2.23 us  [the longest x1 2.23 us: shards(): pair = lax.ppermute(pair, FINE, [(i, i ^ 1) for i in range(SIDE)])]
where the time goes in v9:
time: 91.9 us; the launch traced here: 91.6 us
  starting transfers between devices  30.6 us (33%)
  blocking collectives  28.9 us (31%)
  waiting for transfers between devices  16.8 us (18%)
  Pallas kernels  14.7 us (16%)
    all_to_all x2, blocking collectives, exchange(): lax.all_to_all(pieces.reshape(rows[0], 1, LANES), axis, 0, 0, tiled=True)  28.9 us
    all_to_all x2, starting transfers between devices, exchange(): lax.all_to_all(pieces.reshape(rows[0], 1, LANES), axis, 0, 0, tiled=True)  22.6 us
    all_to_all x2, waiting for transfers between devices, exchange(): lax.all_to_all(pieces.reshape(rows[0], 1, LANES), axis, 0, 0, tiled=True)  11.9 us
    ppermute x2, starting transfers between devices, ring(): lax.ppermute(rows, axis, [(i, (i + step) % SIDE) for i in range(SIDE)])  5.75 us
    pallas_call x1, Pallas kernels, shards(): call(begin, [shape(WIDE, LANES), shape(FACE_ROWS, LANES), shape(FACE_ROWS...  4.65 us
    pallas_call x1, Pallas kernels, shards(): call(first_image, [shape(SIDE * F_SECOND, LANES), local, local, local, sh...  4.55 us
    pallas_call x1, Pallas kernels, shards(): call(second_image, [shape(WIDE, LANES), local, local, local], 12, scratch...  3.27 us
    ppermute x1, waiting for transfers between devices, shards(): lax.ppermute(cross, FINE, [(i, (i + (1 if i % 2 else -1)) % SIDE) for i i...  2.65 us
  transfers between devices with their start and end apart: 6, of which 4 were waited for; matrix products, arithmetic and copies ran while one was open for 0% of the time, Pallas kernels for 1%

profile of v9, /device:TPU:1, one launch (start us, length us, event | category | flops | bytes accessed | tf_op | source)
XLA Modules:
  0.0 91.6 jit_solution(13499958174215083616)
XLA Ops:
  0.6 0.0 copy-start.1
  0.6 0.0 copy-start
  0.7 4.6 %shard_map.94 = (f32[256,128]{1,0:T(8,128)}, f32[24,128]{1,0:T(8,128)S(1)}, f32[24,128]{1,0:T(8,128)S(1)}, f32[64,128]{1,0:T(8,128)S(1)}, f32[64,128]{1,0:T(8,128)S(1)}, /*index=5*/f32[64,128]{1,0:T(8,128)S(1)}) custom-call(f32[16]{0:T(128)} %table_hbm.1, f32[64,128]{1,0:T(8,128)} %bitcast.37, s32[64,128]{1,0:T(8,128)} %bitcast.45, s32[64,128]{1,0:T(8,128)} %bitcast.27, ...), custom_call_target="tpu_custom_call" | custom-call | flops 1000000000 | bytes 4000000 | tf_op jit(solution)/shard_map/pallas_call | solution.py:597
  5.3 15.7 %all-to-all-start = ((f32[256,1,128]{2,1,0:T(1,128)}), f32[256,1,128]{2,1,0:T(1,128)S(1)}, u32[]{:S(2)}, u32[]{:S(2)}) async-start(f32[256,1,128]{2,1,0:T(1,128)} %bitcast.7), calls=%async_computation | async-start | bytes 262144 | tf_op jit(solution)/shard_map/all_to_all | solution.py:587
  21.0 2.2 %collective-permute-start = (f32[24,128]{1,0:T(8,128)S(1)}, f32[24,128]{1,0:T(8,128)S(1)}, u32[]{:S(2)}, u32[]{:S(2)}) collective-permute-start(f32[24,128]{1,0:T(8,128)S(1)} %get-tuple-element.27), channel_id=1, source_target_pairs={{0,1},{1,0},{2,3},{3,2},{4,5},{5,4},{6,7},{7,6},{8,9},{9,8},{10,11... | collective-permute-start | bytes 36872 | tf_op jit(solution)/shard_map/ppermute | solution.py:611
  23.2 0.0 collective-permute-start.1
  23.2 0.8 collective-permute-done.pair_ref
  24.1 2.6 %collective-permute-done.1.cross_ref = f32[24,128]{1,0:T(8,128)S(1)} collective-permute-done((f32[24,128]{1,0:T(8,128)S(1)}, f32[24,128]{1,0:T(8,128)S(1)}, u32[]{:S(2)}, u32[]{:S(2)}) %collective-permute-start.1) | collective-permute-done | bytes 12320 | tf_op jit(solution)/shard_map/ppermute | solution.py:612
  26.7 0.1 collective-permute-start.2
  26.8 5.7 %collective-permute-start.3 = (f32[32,128]{1,0:T(8,128)S(1)}, f32[32,128]{1,0:T(8,128)S(1)}, u32[]{:S(2)}, u32[]{:S(2)}) collective-permute-start(f32[32,128]{1,0:T(8,128)S(1)} %get-tuple-element.33), channel_id=1, source_target_pairs={{0,240},{16,0},{32,16},{48,32},{64,48},{80,64},{96,80},{112,96},{1... | collective-permute-start | bytes 49160 | tf_op jit(solution)/shard_map/ppermute | solution.py:591
  32.5 1.4 %collective-permute-done.2.before_ref = f32[32,128]{1,0:T(8,128)S(1)} collective-permute-done((f32[32,128]{1,0:T(8,128)S(1)}, f32[32,128]{1,0:T(8,128)S(1)}, u32[]{:S(2)}, u32[]{:S(2)}) %collective-permute-start.2) | collective-permute-done | bytes 16416 | tf_op jit(solution)/shard_map/ppermute | solution.py:591
  33.9 0.0 collective-permute-done.3.after_ref
  33.9 0.0 all-to-all-done
  33.9 0.0 copy-done.1
  33.9 0.0 copy-done
  33.9 0.0 copy-start.2
  33.9 4.6 %shard_map.96 = (f32[144,128]{1,0:T(8,128)S(1)}, f32[64,128]{1,0:T(8,128)S(1)}, f32[64,128]{1,0:T(8,128)S(1)}, f32[64,128]{1,0:T(8,128)S(1)}, f32[10,16,128]{2,1...) custom-call(f32[256,128]{1,0:T(8,128)S(1)} %bitcast.25, ...), custom_call_target="tpu_custom_call" | custom-call | flops 1000000000 | bytes 4000000 | tf_op jit(solution)/shard_map/pallas_call | solution.py:620
  38.5 11.3 %all_to_all.20 = f32[144,1,128]{2,1,0:T(1,128)S(1)} all-to-all(f32[144,1,128]{2,1,0:T(1,128)S(1)} %bitcast.42), channel_id=1, replica_groups=mesh['coarse'=16,'fine'=16] {'fine'}, dimensions={0} | all-to-all | bytes 147456 | tf_op jit(solution)/shard_map/all_to_all | solution.py:587
  49.8 17.6 %all_to_all.21 = f32[192,1,128]{2,1,0:T(1,128)S(1)} all-to-all(f32[192,1,128]{2,1,0:T(1,128)S(1)} %bitcast.41), channel_id=1, replica_groups=mesh['coarse'=16,'fine'=16] {'coarse'}, dimensions={0} | all-to-all | bytes 196608 | tf_op jit(solution)/shard_map/all_to_all | solution.py:587
  67.4 0.0 copy-done.2
  67.4 3.3 %shard_map.98 = (f32[256,128]{1,0:T(8,128)}, f32[64,128]{1,0:T(8,128)S(1)}, f32[64,128]{1,0:T(8,128)S(1)}, f32[64,128]{1,0:T(8,128)S(1)}) custom-call(f32[144,128]{1,0:T(8,128)S(1)} %bitcast.36, f32[192,128]{1,0:T(8,128)S(1)} %bitcast.26, f32[64,128]{1,0:T(8,128)S(1)} %get-tuple-element.35.smoothed_ref.own_ref, ...), custom_call_target="tpu_custom_call" | custom-call | flops 1000000000 | bytes 4000000 | tf_op jit(solution)/shard_map/pallas_call | solution.py:637
  70.6 6.9 %all-to-all-start.3 = ((f32[256,1,128]{2,1,0:T(1,128)}), f32[256,1,128]{2,1,0:T(1,128)S(1)}, u32[]{:S(2)}, u32[]{:S(2)}) async-start(f32[256,1,128]{2,1,0:T(1,128)} %bitcast.16), calls=%async_computation.3 | async-start | bytes 262144 | tf_op jit(solution)/shard_map/all_to_all | solution.py:587
  77.6 1.1 %shard_map.99.smoothed_ref = f32[64,128]{1,0:T(8,128)S(1)} custom-call(f32[64,128]{1,0:T(8,128)S(1)} %get-tuple-element.45.product_ref, s32[64,128]{1,0:T(8,128)S(1)} %bitcast.30), custom_call_target="tpu_custom_call" | custom-call | flops 1000000000 | bytes 4000000 | tf_op jit(solution)/shard_map/pallas_call | solution.py:647
  78.6 11.9 %all-to-all-done.3 = f32[256,1,128]{2,1,0:T(1,128)S(1)} async-done(((f32[256,1,128]{2,1,0:T(1,128)}), f32[256,1,128]{2,1,0:T(1,128)S(1)}, u32[]{:S(2)}, u32[]{:S(2)}) %all-to-all-start.3) | async-done | bytes 131104 | tf_op jit(solution)/shard_map/all_to_all | solution.py:587
  90.5 1.1 %shard_map.100 = (f32[64,128]{1,0:T(8,128)}, f32[64,128]{1,0:T(8,128)}, f32[64,128]{1,0:T(8,128)}) custom-call(f32[256,128]{1,0:T(8,128)S(1)} %bitcast.40, f32[16,256]{1,0:T(8,128)S(1)} %get-tuple-element.38.diagonal_ref, s32[64,128]{1,0:T(8,128)S(1)} %bitcast.34, f32[64,128]{1,0:T(8,128)S(1)} %bitcast.39, f32[64,128]{1,0:T(8,128)S(1)} %get-tuple-element.39.first_ref, ...), custom_call_target="tpu_custom_call" | custom-call | flops 1000000000 | bytes 4000000 | tf_op jit(solution)/shard_map/pallas_call | solution.py:648
  (2 shorter events, 0.0 us)
Async XLA Ops:
  0.6 33.3 %copy-start.1 = (s32[8,8,128]{2,1,0:T(8,128)S(1)}, s32[8,8,128]{2,1,0:T(8,128)}, u32[]{:S(2)}) copy-start(s32[8,8,128]{2,1,0:T(8,128)} %param.12) | copy-start | bytes 98308
  0.6 33.3 %copy-start = (s32[1,1,64,128]{3,2,1,0:T(8,128)S(1)}, s32[1,1,64,128]{3,2,1,0:T(8,128)}, u32[]{:S(2)}) copy-start(s32[1,1,64,128]{3,2,1,0:T(8,128)} %param.10) | copy-start | bytes 98308
  5.3 28.6 %all-to-all-start = ((f32[256,1,128]{2,1,0:T(1,128)}), f32[256,1,128]{2,1,0:T(1,128)S(1)}, u32[]{:S(2)}, u32[]{:S(2)}) async-start(f32[256,1,128]{2,1,0:T(1,128)} %bitcast.7), calls=%async_computation | async-start | bytes 262144 | tf_op jit(solution)/shard_map/all_to_all | solution.py:587
  21.0 3.1 %collective-permute-start = (f32[24,128]{1,0:T(8,128)S(1)}, f32[24,128]{1,0:T(8,128)S(1)}, u32[]{:S(2)}, u32[]{:S(2)}) collective-permute-start(f32[24,128]{1,0:T(8,128)S(1)} %get-tuple-element.27), channel_id=1, source_target_pairs={{0,1},{1,0},{2,3},{3,2},{4,5},{5,4},{6,7},{7,6},{8,9},{9,8},{10,11... | collective-permute-start | bytes 36872 | tf_op jit(solution)/shard_map/ppermute | solution.py:611
  23.2 3.5 %collective-permute-start.1 = (f32[24,128]{1,0:T(8,128)S(1)}, f32[24,128]{1,0:T(8,128)S(1)}, u32[]{:S(2)}, u32[]{:S(2)}) collective-permute-start(f32[24,128]{1,0:T(8,128)S(1)} %get-tuple-element.28), channel_id=1, source_target_pairs={{0,15},{1,2},{2,1},{3,4},{4,3},{5,6},{6,5},{7,8},{8,7},{9,10},{10,... | collective-permute-start | bytes 36872 | tf_op jit(solution)/shard_map/ppermute | solution.py:612
  26.7 7.2 %collective-permute-start.2 = (f32[32,128]{1,0:T(8,128)S(1)}, f32[32,128]{1,0:T(8,128)S(1)}, u32[]{:S(2)}, u32[]{:S(2)}) collective-permute-start(f32[32,128]{1,0:T(8,128)S(1)} %get-tuple-element.32), channel_id=1, source_target_pairs={{0,16},{16,32},{32,48},{48,64},{64,80},{80,96},{96,112},{112,128},... | collective-permute-start | bytes 49160 | tf_op jit(solution)/shard_map/ppermute | solution.py:591
  26.8 7.1 %collective-permute-start.3 = (f32[32,128]{1,0:T(8,128)S(1)}, f32[32,128]{1,0:T(8,128)S(1)}, u32[]{:S(2)}, u32[]{:S(2)}) collective-permute-start(f32[32,128]{1,0:T(8,128)S(1)} %get-tuple-element.33), channel_id=1, source_target_pairs={{0,240},{16,0},{32,16},{48,32},{64,48},{80,64},{96,80},{112,96},{1... | collective-permute-start | bytes 49160 | tf_op jit(solution)/shard_map/ppermute | solution.py:591
  33.9 33.5 %copy-start.2 = (f32[8,8,128]{2,1,0:T(8,128)S(1)}, f32[8,8,128]{2,1,0:T(8,128)}, u32[]{:S(2)}) copy-start(f32[8,8,128]{2,1,0:T(8,128)} %param.7) | copy-start | bytes 98308
  70.6 19.9 %all-to-all-start.3 = ((f32[256,1,128]{2,1,0:T(1,128)}), f32[256,1,128]{2,1,0:T(1,128)S(1)}, u32[]{:S(2)}, u32[]{:S(2)}) async-start(f32[256,1,128]{2,1,0:T(1,128)} %bitcast.16), calls=%async_computation.3 | async-start | bytes 262144 | tf_op jit(solution)/shard_map/all_to_all | solution.py:587

commit v10 on v9

--- a/solution.py
+++ b/solution.py
@@ -271,11 +271,26 @@
 C_HALO_2, C_SOURCE_2, C_SECOND = 8, 10, 12
 
 
+def fetch_matrices(matrices_hbm, matrices_ref, arrived):
+    part = ROWS // 4
+    copies = [
+        pltpu.make_async_copy(
+            matrices_hbm.at[pl.ds(part * number, part)],
+            matrices_ref.at[pl.ds(part * number, part)],
+            arrived.at[number],
+        )
+        for number in range(4)
+    ]
+    for copy in copies:
+        copy.start()
+    return copies
+
+
 def begin(
     table_hbm, side_hbm, index_hbm, order_hbm, matrices_hbm, map_hbm, diagonal_hbm,
     pieces_ref, pair_ref, cross_ref, kappa_ref, smoothed_ref, numbers_ref,
     table_ref, side_ref, index_ref, order_ref, map_ref, diagonal_ref, picked_ref, product_ref,
-    matrices_ref, arrived,
+    matrices_ref, arrived, quarter_arrived,
 ):
     owner, member = position()
     copies = [
@@ -288,14 +303,14 @@
                 (index_hbm, index_ref),
                 (map_hbm, map_ref),
                 (diagonal_hbm, diagonal_ref),
-                (matrices_hbm, matrices_ref),
             )
         )
     ]
     for copy in copies:
         copy.start()
+    quarters = fetch_matrices(matrices_hbm, matrices_ref, quarter_arrived)
     copies[0].wait()
-    for copy in copies[1:-1]:
+    for copy in copies[1:]:
         copy.wait()
     index = index_ref[...]
     kappa = jnp.zeros((ROWS, LANES), F32)
@@ -303,7 +318,8 @@
         kappa = jnp.where(index == entry, table_ref[entry], kappa)
     kappa_ref[...] = kappa
     pick(side_ref, order_ref, picked_ref)
-    copies[-1].wait()
+    for copy in quarters:
+        copy.wait()
     multiply_blocks(matrices_ref, picked_ref, product_ref)
     put_back(product_ref, order_ref, smoothed_ref)
     aggregate = map_ref[...]
@@ -422,8 +438,7 @@
     picked_ref, product_ref, slabs_ref, rows_ref, arrived,
 ):
     owner, member = position()
-    copy = pltpu.make_async_copy(matrices_hbm, matrices_ref, arrived)
-    copy.start()
+    copies = fetch_matrices(matrices_hbm, matrices_ref, arrived)
     diagonal = coarse_rows(rows_of_all_ref, 1)
     diagonal_ref[...] = diagonal
     nearby(coarse_solve(coarse_rows(rows_of_all_ref, 0), diagonal), member, rows_ref)
@@ -440,7 +455,8 @@
     field_ref[...] = field[1:9, :8].reshape(ROWS, LANES)
     image_ref[...] = operate(field, kappa_ref[...]).reshape(ROWS, LANES)
     pick(image_ref, order_ref, picked_ref)
-    copy.wait()
+    for copy in copies:
+        copy.wait()
     multiply_blocks(matrices_ref, picked_ref, product_ref)
     put_back(product_ref, order_ref, smoothed_ref)
     source = restrict(image_ref[...], offsets(map_ref[...]), member)
@@ -604,7 +620,7 @@
         [
             pltpu.SMEM(material_coefficients.shape, F32), cells, int_cells, int_cells,
             int_cells, pltpu.VMEM((1, SIDE), F32), cells, cells,
-            pltpu.VMEM(matrices.shape, F32), pltpu.SemaphoreType.DMA((7,)),
+            pltpu.VMEM(matrices.shape, F32), pltpu.SemaphoreType.DMA((6,)), pltpu.SemaphoreType.DMA((4,)),
         ],
         [hbm()] * 7,
     )(*fixed)
@@ -625,7 +641,7 @@
             pltpu.VMEM(matrices.shape, F32),
         ],
         11,
-        scratch + [pltpu.SemaphoreType.DMA],
+        scratch + [pltpu.SemaphoreType.DMA((4,))],
         [vmem()] * 10 + [hbm()],
     )(
         rows, pair, cross, before, after, smoothed, kappa, numbers, aggregate, order, fixed[4]

time: 91.9 us -> 92.8 us (level)
    pallas_call x1, Pallas kernels: 4.65 us -> 5.64 us  [shards(): call(begin, [shape(WIDE, LANES), shape(FACE_ROWS, LANES), shape(FACE_ROWS...]
where the time goes in v10:
time: 92.8 us; the launch traced here: 92.6 us
  starting transfers between devices  30.6 us (33%)
  blocking collectives  28.9 us (31%)
  waiting for transfers between devices  16.8 us (18%)
  Pallas kernels  15.6 us (17%)
    all_to_all x2, blocking collectives, exchange(): lax.all_to_all(pieces.reshape(rows[0], 1, LANES), axis, 0, 0, tiled=True)  28.9 us
    all_to_all x2, starting transfers between devices, exchange(): lax.all_to_all(pieces.reshape(rows[0], 1, LANES), axis, 0, 0, tiled=True)  22.6 us
    all_to_all x2, waiting for transfers between devices, exchange(): lax.all_to_all(pieces.reshape(rows[0], 1, LANES), axis, 0, 0, tiled=True)  11.9 us
    ppermute x2, starting transfers between devices, ring(): lax.ppermute(rows, axis, [(i, (i + step) % SIDE) for i in range(SIDE)])  5.75 us
    pallas_call x1, Pallas kernels, shards(): call(begin, [shape(WIDE, LANES), shape(FACE_ROWS, LANES), shape(FACE_ROWS...  5.64 us
    pallas_call x1, Pallas kernels, shards(): call(first_image, [shape(SIDE * F_SECOND, LANES), local, local, local, sh...  4.55 us
    pallas_call x1, Pallas kernels, shards(): call(second_image, [shape(WIDE, LANES), local, local, local], 12, scratch...  3.24 us
    ppermute x1, waiting for transfers between devices, shards(): lax.ppermute(cross, FINE, [(i, (i + (1 if i % 2 else -1)) % SIDE) for i i...  2.65 us
  transfers between devices with their start and end apart: 6, of which 4 were waited for; matrix products, arithmetic and copies ran while one was open for 0% of the time, Pallas kernels for 1%

profile of v10, /device:TPU:1, one launch (start us, length us, event | category | flops | bytes accessed | tf_op | source)
XLA Modules:
  0.0 92.6 jit_solution(17011117256159958867)
XLA Ops:
  0.6 0.0 copy-start.1
  0.6 0.0 copy-start
  0.7 5.6 %shard_map.94 = (f32[256,128]{1,0:T(8,128)}, f32[24,128]{1,0:T(8,128)S(1)}, f32[24,128]{1,0:T(8,128)S(1)}, f32[64,128]{1,0:T(8,128)S(1)}, f32[64,128]{1,0:T(8,128)S(1)}, /*index=5*/f32[64,128]{1,0:T(8,128)S(1)}) custom-call(f32[16]{0:T(128)} %table_hbm.1, f32[64,128]{1,0:T(8,128)} %bitcast.37, s32[64,128]{1,0:T(8,128)} %bitcast.45, s32[64,128]{1,0:T(8,128)} %bitcast.27, ...), custom_call_target="tpu_custom_call" | custom-call | flops 1000000000 | bytes 4000000 | tf_op jit(solution)/shard_map/pallas_call | solution.py:613
  6.3 15.7 %all-to-all-start = ((f32[256,1,128]{2,1,0:T(1,128)}), f32[256,1,128]{2,1,0:T(1,128)S(1)}, u32[]{:S(2)}, u32[]{:S(2)}) async-start(f32[256,1,128]{2,1,0:T(1,128)} %bitcast.7), calls=%async_computation | async-start | bytes 262144 | tf_op jit(solution)/shard_map/all_to_all | solution.py:603
  22.0 2.2 %collective-permute-start = (f32[24,128]{1,0:T(8,128)S(1)}, f32[24,128]{1,0:T(8,128)S(1)}, u32[]{:S(2)}, u32[]{:S(2)}) collective-permute-start(f32[24,128]{1,0:T(8,128)S(1)} %get-tuple-element.27), channel_id=1, source_target_pairs={{0,1},{1,0},{2,3},{3,2},{4,5},{5,4},{6,7},{7,6},{8,9},{9,8},{10,11... | collective-permute-start | bytes 36872 | tf_op jit(solution)/shard_map/ppermute | solution.py:627
  24.2 0.0 collective-permute-start.1
  24.2 0.8 collective-permute-done.pair_ref
  25.1 2.6 %collective-permute-done.1.cross_ref = f32[24,128]{1,0:T(8,128)S(1)} collective-permute-done((f32[24,128]{1,0:T(8,128)S(1)}, f32[24,128]{1,0:T(8,128)S(1)}, u32[]{:S(2)}, u32[]{:S(2)}) %collective-permute-start.1) | collective-permute-done | bytes 12320 | tf_op jit(solution)/shard_map/ppermute | solution.py:628
  27.7 0.1 collective-permute-start.2
  27.8 5.7 %collective-permute-start.3 = (f32[32,128]{1,0:T(8,128)S(1)}, f32[32,128]{1,0:T(8,128)S(1)}, u32[]{:S(2)}, u32[]{:S(2)}) collective-permute-start(f32[32,128]{1,0:T(8,128)S(1)} %get-tuple-element.33), channel_id=1, source_target_pairs={{0,240},{16,0},{32,16},{48,32},{64,48},{80,64},{96,80},{112,96},{1... | collective-permute-start | bytes 49160 | tf_op jit(solution)/shard_map/ppermute | solution.py:607
  33.5 1.4 %collective-permute-done.2.before_ref = f32[32,128]{1,0:T(8,128)S(1)} collective-permute-done((f32[32,128]{1,0:T(8,128)S(1)}, f32[32,128]{1,0:T(8,128)S(1)}, u32[]{:S(2)}, u32[]{:S(2)}) %collective-permute-start.2) | collective-permute-done | bytes 16416 | tf_op jit(solution)/shard_map/ppermute | solution.py:607
  34.9 0.0 collective-permute-done.3.after_ref
  34.9 0.0 all-to-all-done
  34.9 0.0 copy-done.1
  34.9 0.0 copy-done
  34.9 0.0 copy-start.2
  34.9 4.5 %shard_map.96 = (f32[144,128]{1,0:T(8,128)S(1)}, f32[64,128]{1,0:T(8,128)S(1)}, f32[64,128]{1,0:T(8,128)S(1)}, f32[64,128]{1,0:T(8,128)S(1)}, f32[10,16,128]{2,1...) custom-call(f32[256,128]{1,0:T(8,128)S(1)} %bitcast.25, ...), custom_call_target="tpu_custom_call" | custom-call | flops 1000000000 | bytes 4000000 | tf_op jit(solution)/shard_map/pallas_call | solution.py:636
  39.5 11.3 %all_to_all.20 = f32[144,1,128]{2,1,0:T(1,128)S(1)} all-to-all(f32[144,1,128]{2,1,0:T(1,128)S(1)} %bitcast.42), channel_id=1, replica_groups=mesh['coarse'=16,'fine'=16] {'fine'}, dimensions={0} | all-to-all | bytes 147456 | tf_op jit(solution)/shard_map/all_to_all | solution.py:603
  50.8 17.6 %all_to_all.21 = f32[192,1,128]{2,1,0:T(1,128)S(1)} all-to-all(f32[192,1,128]{2,1,0:T(1,128)S(1)} %bitcast.41), channel_id=1, replica_groups=mesh['coarse'=16,'fine'=16] {'coarse'}, dimensions={0} | all-to-all | bytes 196608 | tf_op jit(solution)/shard_map/all_to_all | solution.py:603
  68.4 0.0 copy-done.2
  68.4 3.2 %shard_map.98 = (f32[256,128]{1,0:T(8,128)}, f32[64,128]{1,0:T(8,128)S(1)}, f32[64,128]{1,0:T(8,128)S(1)}, f32[64,128]{1,0:T(8,128)S(1)}) custom-call(f32[144,128]{1,0:T(8,128)S(1)} %bitcast.36, f32[192,128]{1,0:T(8,128)S(1)} %bitcast.26, f32[64,128]{1,0:T(8,128)S(1)} %get-tuple-element.35.smoothed_ref.own_ref, ...), custom_call_target="tpu_custom_call" | custom-call | flops 1000000000 | bytes 4000000 | tf_op jit(solution)/shard_map/pallas_call | solution.py:653
  71.6 7.0 %all-to-all-start.3 = ((f32[256,1,128]{2,1,0:T(1,128)}), f32[256,1,128]{2,1,0:T(1,128)S(1)}, u32[]{:S(2)}, u32[]{:S(2)}) async-start(f32[256,1,128]{2,1,0:T(1,128)} %bitcast.16), calls=%async_computation.3 | async-start | bytes 262144 | tf_op jit(solution)/shard_map/all_to_all | solution.py:603
  78.6 1.1 %shard_map.99.smoothed_ref = f32[64,128]{1,0:T(8,128)S(1)} custom-call(f32[64,128]{1,0:T(8,128)S(1)} %get-tuple-element.45.product_ref, s32[64,128]{1,0:T(8,128)S(1)} %bitcast.30), custom_call_target="tpu_custom_call" | custom-call | flops 1000000000 | bytes 4000000 | tf_op jit(solution)/shard_map/pallas_call | solution.py:663
  79.6 11.9 %all-to-all-done.3 = f32[256,1,128]{2,1,0:T(1,128)S(1)} async-done(((f32[256,1,128]{2,1,0:T(1,128)}), f32[256,1,128]{2,1,0:T(1,128)S(1)}, u32[]{:S(2)}, u32[]{:S(2)}) %all-to-all-start.3) | async-done | bytes 131104 | tf_op jit(solution)/shard_map/all_to_all | solution.py:603
  91.5 1.1 %shard_map.100 = (f32[64,128]{1,0:T(8,128)}, f32[64,128]{1,0:T(8,128)}, f32[64,128]{1,0:T(8,128)}) custom-call(f32[256,128]{1,0:T(8,128)S(1)} %bitcast.40, f32[16,256]{1,0:T(8,128)S(1)} %get-tuple-element.38.diagonal_ref, s32[64,128]{1,0:T(8,128)S(1)} %bitcast.34, f32[64,128]{1,0:T(8,128)S(1)} %bitcast.39, f32[64,128]{1,0:T(8,128)S(1)} %get-tuple-element.39.first_ref, ...), custom_call_target="tpu_custom_call" | custom-call | flops 1000000000 | bytes 4000000 | tf_op jit(solution)/shard_map/pallas_call | solution.py:664
  (2 shorter events, 0.0 us)
Async XLA Ops:
  0.6 34.3 %copy-start.1 = (s32[8,8,128]{2,1,0:T(8,128)S(1)}, s32[8,8,128]{2,1,0:T(8,128)}, u32[]{:S(2)}) copy-start(s32[8,8,128]{2,1,0:T(8,128)} %param.12) | copy-start | bytes 98308
  0.6 34.3 %copy-start = (s32[1,1,64,128]{3,2,1,0:T(8,128)S(1)}, s32[1,1,64,128]{3,2,1,0:T(8,128)}, u32[]{:S(2)}) copy-start(s32[1,1,64,128]{3,2,1,0:T(8,128)} %param.10) | copy-start | bytes 98308
  6.3 28.6 %all-to-all-start = ((f32[256,1,128]{2,1,0:T(1,128)}), f32[256,1,128]{2,1,0:T(1,128)S(1)}, u32[]{:S(2)}, u32[]{:S(2)}) async-start(f32[256,1,128]{2,1,0:T(1,128)} %bitcast.7), calls=%async_computation | async-start | bytes 262144 | tf_op jit(solution)/shard_map/all_to_all | solution.py:603
  22.0 3.1 %collective-permute-start = (f32[24,128]{1,0:T(8,128)S(1)}, f32[24,128]{1,0:T(8,128)S(1)}, u32[]{:S(2)}, u32[]{:S(2)}) collective-permute-start(f32[24,128]{1,0:T(8,128)S(1)} %get-tuple-element.27), channel_id=1, source_target_pairs={{0,1},{1,0},{2,3},{3,2},{4,5},{5,4},{6,7},{7,6},{8,9},{9,8},{10,11... | collective-permute-start | bytes 36872 | tf_op jit(solution)/shard_map/ppermute | solution.py:627
  24.2 3.5 %collective-permute-start.1 = (f32[24,128]{1,0:T(8,128)S(1)}, f32[24,128]{1,0:T(8,128)S(1)}, u32[]{:S(2)}, u32[]{:S(2)}) collective-permute-start(f32[24,128]{1,0:T(8,128)S(1)} %get-tuple-element.28), channel_id=1, source_target_pairs={{0,15},{1,2},{2,1},{3,4},{4,3},{5,6},{6,5},{7,8},{8,7},{9,10},{10,... | collective-permute-start | bytes 36872 | tf_op jit(solution)/shard_map/ppermute | solution.py:628
  27.7 7.2 %collective-permute-start.2 = (f32[32,128]{1,0:T(8,128)S(1)}, f32[32,128]{1,0:T(8,128)S(1)}, u32[]{:S(2)}, u32[]{:S(2)}) collective-permute-start(f32[32,128]{1,0:T(8,128)S(1)} %get-tuple-element.32), channel_id=1, source_target_pairs={{0,16},{16,32},{32,48},{48,64},{64,80},{80,96},{96,112},{112,128},... | collective-permute-start | bytes 49160 | tf_op jit(solution)/shard_map/ppermute | solution.py:607
  27.8 7.1 %collective-permute-start.3 = (f32[32,128]{1,0:T(8,128)S(1)}, f32[32,128]{1,0:T(8,128)S(1)}, u32[]{:S(2)}, u32[]{:S(2)}) collective-permute-start(f32[32,128]{1,0:T(8,128)S(1)} %get-tuple-element.33), channel_id=1, source_target_pairs={{0,240},{16,0},{32,16},{48,32},{64,48},{80,64},{96,80},{112,96},{1... | collective-permute-start | bytes 49160 | tf_op jit(solution)/shard_map/ppermute | solution.py:607
  34.9 33.5 %copy-start.2 = (f32[8,8,128]{2,1,0:T(8,128)S(1)}, f32[8,8,128]{2,1,0:T(8,128)}, u32[]{:S(2)}) copy-start(f32[8,8,128]{2,1,0:T(8,128)} %param.7) | copy-start | bytes 98308
  71.6 19.9 %all-to-all-start.3 = ((f32[256,1,128]{2,1,0:T(1,128)}), f32[256,1,128]{2,1,0:T(1,128)S(1)}, u32[]{:S(2)}, u32[]{:S(2)}) async-start(f32[256,1,128]{2,1,0:T(1,128)} %bitcast.16), calls=%async_computation.3 | async-start | bytes 262144 | tf_op jit(solution)/shard_map/all_to_all | solution.py:603
